TPU v7x, 128 devices: a whole 4x4x4 slice. The times are simulated.
128 devices in a mesh: cand: 8 (over x_hi, z), prompt: 16 (over x_lo, y, core).
Axes of the slice: x: 4 (x_hi: 2, x_lo: 2; x = x_hi * 2 + x_lo), y: 4, z: 4, core: 2. Of those that a mesh axis runs over, the one named last changes fastest.
Arguments:
- hidden_states: bfloat16 [16, 8, 128, 4096], P('prompt', 'cand'), may hold values from -8 to 8
- proj_weight: bfloat16 [4096, 1024], P(('cand', 'prompt')), may hold values from -0.0625 to 0.0625
- bilinear: bfloat16 [1024, 1024], P(('cand', 'prompt')), may hold values from -0.005859375 to 0.005859375
- lengths: int32 [16, 8], P('prompt'), may hold values from 32 to 128, as said below
- labels: int32 [16, 28], P('prompt'), may hold values 0 or 1
Outputs:
- pair_logits: float32 [16, 8, 8], P('prompt')
- grad_proj: float32 [4096, 1024], P(('cand', 'prompt'))
- grad_bilinear: float32 [1024, 1024], P(('cand', 'prompt'))
Inputs may be any that keep to these rules, and one draw needn't show every extreme that they name: `lengths`: every prompt has a candidate with all 128 rows valid.
All inputs are finite; a program needn't handle non-finite values. No bound on the sum of `labels` on one device may be relied on, other than what follows from the above.
Results may differ from a plain program's by a relative error of at most 0.0045.
Values may be sent and summed in bfloat16 or wider, within the bound.
No kernel may reach another device: no remote copies, remote signals or barrier semaphores. Data moves between devices by JAX's collectives and lax.ppermute only.
A program may use at most 128 MiB of HBM per device.

v0:
```python
import jax
import jax.numpy as jnp
import numpy as np
from jax import lax
from jax.sharding import PartitionSpec as P

HEADS = 16
HEAD_DIM = 64


EPSILON = 1e-06
HIGH = lax.Precision.HIGHEST


def shifted_2(value, axis, steps):
    count = lax.axis_size(axis)
    pairs = [(source, (source + steps) % count) for source in range(count)]
    return lax.ppermute(value, axis, pairs)


def attend_block(queries, keys, key_valid, factor):
    prompts, rows, width = queries.shape
    query_heads = queries.reshape(prompts, rows, HEADS, HEAD_DIM)
    key_heads = keys.reshape(prompts, rows, HEADS, HEAD_DIM)
    scores = (
        jnp.einsum("pthd,pshd->phts", query_heads, key_heads, preferred_element_type=jnp.float32)
        * factor
    )
    scores = jnp.where(key_valid[:, None, None, :], scores, -jnp.inf)
    shifted = jnp.exp(scores - jnp.max(scores, axis=3, keepdims=True))
    weights = shifted / jnp.sum(shifted, axis=3, keepdims=True)
    mixed = jnp.einsum(
        "phts,pshd->pthd",
        weights.astype(jnp.bfloat16),
        key_heads,
        preferred_element_type=jnp.float32,
    )
    return (weights, mixed)


def body(hidden_states, proj_weight, bilinear, lengths, labels):
    cands = lax.axis_size("cand")
    here = lax.axis_index("cand")
    prompts = hidden_states.shape[0]
    rows = hidden_states.shape[2]
    width = hidden_states.shape[3]
    inner = proj_weight.shape[1]
    factor = HEAD_DIM ** (-0.5)
    flat = hidden_states.reshape(prompts * rows, width)
    columns = flat
    projected = jnp.dot(
        columns,
        lax.all_gather(proj_weight, ("cand", "prompt"), axis=0, tiled=True),
        preferred_element_type=jnp.float32,
    )
    own_rows = projected.astype(jnp.bfloat16).reshape(prompts, rows, inner)
    own_heads = own_rows.reshape(prompts, rows, HEADS, HEAD_DIM)
    cand_ids = jnp.arange(cands, dtype=jnp.int32)
    positions = jnp.arange(rows, dtype=jnp.int32)

    def length_of(source):
        return jnp.sum(jnp.where(cand_ids[None, :] == source, lengths, 0), axis=1)

    own_length = length_of(here)
    own_valid = positions[None, :] < own_length[:, None]
    own_length_f = own_length.astype(jnp.float32)
    received = {}
    moving = own_rows
    for offset in range(1, cands):
        moving = shifted_2(moving, "cand", 1)
        received[offset] = moving
    sources = {}
    means = {}
    radii = {}
    pooled = jnp.zeros((prompts, cands, inner), jnp.float32)
    for offset in range(1, cands):
        source = (here - offset) % cands
        other_valid = positions[None, :] < length_of(source)[:, None]
        weights, mixed = attend_block(own_rows, received[offset], other_valid, factor)
        total = jnp.sum(jnp.where(own_valid[:, :, None, None], mixed, 0.0), axis=1)
        mean_row = total.reshape(prompts, inner) / own_length_f[:, None]
        radius = jnp.sqrt(jnp.mean(mean_row * mean_row, axis=1, keepdims=True) + EPSILON)
        normed = mean_row / radius
        pooled = pooled + jnp.where((cand_ids == source)[None, :, None], normed[:, None, :], 0.0)
        sources[offset] = source
        means[offset] = mean_row
        radii[offset] = radius
    everything = lax.all_gather(pooled[:, None], "cand", axis=1, tiled=True)
    full_bil = lax.all_gather(bilinear, ("cand", "prompt"), axis=0, tiled=True).astype(jnp.float32)
    toward = jnp.einsum("ab,pjib->pija", full_bil, everything, precision=HIGH)
    pair_logits = jnp.sum(everything * toward, axis=3)
    upper_i, upper_j = np.triu_indices(cands, 1)
    wins = labels.astype(jnp.float32)
    target = (
        jnp.zeros((prompts, cands, cands), jnp.float32)
        .at[:, upper_i, upper_j]
        .set(wins)
        .at[:, upper_j, upper_i]
        .set(1.0 - wins)
    )
    offdiag = 1.0 - jnp.eye(cands, dtype=jnp.float32)
    sign = 2.0 * target - 1.0
    dlogit = -sign * jax.nn.sigmoid(-sign * pair_logits) * offdiag[None]
    backward_dir = jnp.einsum("ba,pjib->pija", full_bil, everything, precision=HIGH)
    dpooled = dlogit[..., None] * toward + jnp.swapaxes(dlogit, 1, 2)[..., None] * backward_dir
    own_mask = cand_ids == here
    dnormed_own = jnp.sum(jnp.where(own_mask[None, :, None, None], dpooled, 0.0), axis=1)
    reverse_pool = jnp.sum(jnp.where(own_mask[None, None, :, None], everything, 0.0), axis=2)
    own_dlogit = jnp.sum(jnp.where(own_mask[None, :, None], dlogit, 0.0), axis=1)
    bil_term = jnp.einsum("pj,pja,pjb->ab", own_dlogit, pooled, reverse_pool, precision=HIGH)
    grad_bilinear = lax.psum_scatter(bil_term, ("cand", "prompt"), scatter_dimension=0, tiled=True)
    row_weight = jnp.where(own_valid, 1.0, 0.0) / own_length_f[:, None]
    query_grads = jnp.zeros((prompts, rows, inner), jnp.float32)
    owners = jnp.zeros((cands, prompts, rows, inner), jnp.float32)
    for offset in range(1, cands):
        backward_source = sources[offset]
        others = received[offset]
        backward_other_valid = positions[None, :] < length_of(backward_source)[:, None]
        backward_weights, unused = attend_block(own_rows, others, backward_other_valid, factor)
        dnorm = jnp.sum(
            jnp.where((cand_ids == backward_source)[None, :, None], dnormed_own, 0.0), axis=1
        )
        norm_row = means[offset] / radii[offset]
        dmean = (dnorm - norm_row * jnp.mean(dnorm * norm_row, axis=1, keepdims=True)) / radii[
            offset
        ]
        dmean_heads = dmean.reshape(prompts, HEADS, HEAD_DIM)
        other_heads = others.reshape(prompts, rows, HEADS, HEAD_DIM)
        along = jnp.einsum(
            "pshd,phd->phs", other_heads.astype(jnp.float32), dmean_heads, precision=HIGH
        )
        expected = jnp.einsum("phts,phs->pht", backward_weights, along, precision=HIGH)
        dscore = (
            row_weight[:, None, :, None]
            * backward_weights
            * (along[:, :, None, :] - expected[:, :, :, None])
            * factor
        )
        dscore = dscore.astype(jnp.bfloat16)
        dquery = jnp.einsum(
            "phts,pshd->pthd", dscore, other_heads, preferred_element_type=jnp.float32
        )
        column = jnp.einsum("phts,pt->phs", backward_weights, row_weight, precision=HIGH)
        dkey = jnp.einsum(
            "phts,pthd->pshd", dscore, own_heads, preferred_element_type=jnp.float32
        ) + jnp.einsum("phs,phd->pshd", column, dmean_heads, precision=HIGH)
        dquery, dkey, source = (
            dquery.reshape(prompts, rows, inner),
            dkey.reshape(prompts, rows, inner),
            backward_source,
        )
        query_grads = query_grads + dquery
        owners = owners + jnp.where((cand_ids == source)[:, None, None, None], dkey[None], 0.0)
    home = lax.psum_scatter(owners, "cand", scatter_dimension=0, tiled=True)[0]
    total_grad = (query_grads + home).astype(jnp.bfloat16).reshape(prompts * rows, inner)
    columns = flat
    grad_proj = lax.psum_scatter(
        lax.dot_general(
            columns, total_grad, (((0,), (0,)), ((), ())), preferred_element_type=jnp.float32
        ),
        ("cand", "prompt"),
        scatter_dimension=0,
        tiled=True,
    )
    return (pair_logits, grad_proj, grad_bilinear)


def solution(mesh):
    in_specs = (
        P("prompt", "cand", None, None),
        P(("cand", "prompt"), None),
        P(("cand", "prompt"), None),
        P("prompt", None),
        P("prompt", None),
    )
    out_specs = (P("prompt", None, None), P(("cand", "prompt"), None), P(("cand", "prompt"), None))
    return jax.shard_map(body, mesh=mesh, in_specs=in_specs, out_specs=out_specs, check_vma=False)
```

profile of v0, /device:TPU:0, one launch (start us, length us, event | category | flops | bytes accessed | tf_op | source)
XLA Modules:
  0.0 1862.1 jit_solution(6400430401243026478)
XLA Ops:
  10.2 1.4 fusion.129
  17.0 1.1 iota_compare_fusion.2
  18.1 197.4 %all-gather.3.cloned.1.call-done = bf16[4096,1024]{1,0:T(8,128)(2,1)} async-done(((bf16[32,1024]{1,0:T(8,128)(2,1)}), bf16[4096,1024]{1,0:T(8,128)(2,1)}) %all-gather.3.cloned.1.call-update) | async-done | bytes 8388624 | tf_op jit(solution)/shard_map/all_gather | solution.py:53
  215.5 4.6 convolution_convert_fusion
  220.2 1.0 collective-permute-start
  221.2 1.1 iota_compare_fusion.4
  222.3 2.0 scatter_fusion
  224.3 2.0 scatter_fusion.1
  226.5 5.1 collective-permute-done
  234.1 1.7 fusion.148
  235.9 8.7 collective-permute-done.1
  244.5 0.8 copy.181
  245.4 1.4 fusion.206
  247.0 1.7 fusion.146
  249.1 9.9 collective-permute-done.2
  259.1 1.8 copy.183
  260.9 1.3 fusion.205
  262.4 0.8 copy-done.1
  263.1 1.3 fusion.22
  266.8 3.0 fusion.144
  269.8 7.3 collective-permute-done.3
  277.1 1.8 copy.185
  278.9 1.4 fusion.204
  280.5 1.7 fusion.142
  282.7 10.1 collective-permute-done.4
  292.8 1.8 copy.187
  294.6 1.3 fusion.203
  296.1 0.8 copy-done.7
  296.9 1.3 fusion.20
  300.5 3.0 fusion.140
  303.4 7.4 collective-permute-done.5
  310.8 1.8 copy.189
  312.6 1.4 fusion.202
  314.2 1.7 fusion.138
  316.4 6.8 collective-permute-done.6
  323.2 1.8 copy.191
  325.0 1.3 fusion.201
  326.5 0.8 copy-done.13
  327.3 1.3 fusion.18
  330.9 36.7 %all_gather.10 = f32[1,8,8,1024]{3,2,0,1:T(8,128)} all-gather(f32[1,1,8,1024]{3,2,0,1:T(8,128)S(1)} %select_add_fusion.1), channel_id=1, replica_groups=mesh['cand'=8,'prompt'=16] {'cand'}, dimensions={1}, use_global_device_ids=true | all-gather | bytes 294912 | tf_op jit(solution)/shard_map/all_gather | solution.py:88
  367.6 3.0 fusion.136
  370.6 48.0 %all-gather.5.cloned.1.call-done = bf16[1024,1024]{1,0:T(8,128)(2,1)} async-done(((bf16[8,1024]{1,0:T(8,128)(2,1)}), bf16[1024,1024]{1,0:T(8,128)(2,1)}) %all-gather.5.cloned.1.call-update) | async-done | bytes 2097168 | tf_op jit(solution)/shard_map/all_gather | solution.py:89
  418.6 4.4 select_reduce_fusion
  423.7 2.9 fusion.40
  426.6 0.8 fusion.76
  440.3 0.7 subtract_divide_fusion
  441.1 1.3 fusion.214
  442.4 2.5 fusion.108
  445.3 1.1 fusion.118
  446.8 1.1 fusion.116
  448.4 1.1 fusion.114
  449.9 1.1 fusion.112
  451.4 1.1 fusion.110
  452.9 1.4 fusion.120
  455.1 0.7 convolution_add_fusion.5
  455.9 0.7 convolution_add_fusion.4
  458.4 0.7 convolution_add_fusion.1
  460.0 5.0 select_add_fusion
  465.1 5.9 fusion.77
  477.5 71.4 %reduce-scatter.6.cloned.1.call-done = f32[1,1,128,1024]{2,3,1,0:T(8,128)} async-done(((f32[8,1,128,1024]{2,3,1,0:T(8,128)}), f32[1,1,128,1024]{2,3,1,0:T(8,128)}) %reduce-scatter.6.cloned.1.call-update) | async-done | bytes 524304 | tf_op jit(solution)/shard_map/reduce_scatter | solution.py:154
  548.9 9.1 convolution_bitcast_fusion
  558.0 17.5 copy.271
  575.5 617.9 %reduce-scatter.8.cloned.1.call-done = f32[8,1024]{1,0:T(8,128)} async-done(((f32[1024,1024]{1,0:T(8,128)}), f32[8,1024]{1,0:T(8,128)}) %reduce-scatter.8.cloned.1.call-update) | async-done | bytes 32784 | tf_op jit(solution)/shard_map/reduce_scatter | solution.py:111
  1193.4 661.6 %reduce-scatter.10.cloned.1.call-done = f32[32,1024]{1,0:T(8,128)} async-done(((f32[4096,1024]{1,0:T(8,128)}), f32[32,1024]{1,0:T(8,128)}) %reduce-scatter.10.cloned.1.call-update) | async-done | bytes 131088
  (373 shorter events, 35.2 us)
Async XLA Ops:
  7.2 208.3 %copy-start = (bf16[1,1,128,4096]{3,2,1,0:T(8,128)(2,1)S(1)}, bf16[1,1,128,4096]{3,2,1,0:T(8,128)(2,1)}, u32[]{:S(2)}) copy-start(bf16[1,1,128,4096]{3,2,1,0:T(8,128)(2,1)} %param.11) | copy-start | bytes 3145732
  7.2 208.3 %all-gather.3.cloned.1.call-start = ((), (), s32[]{:S(2)}) async-start(), calls=%async_computation.3 | async-start | bytes 8454144 | tf_op jit(solution)/shard_map/all_gather | solution.py:53
  7.9 410.7 %all-gather.5.cloned.1.call-start = ((), (), s32[]{:S(2)}) async-start(), calls=%async_computation.4 | async-start | bytes 2113536 | tf_op jit(solution)/shard_map/all_gather | solution.py:89
  8.7 540.2 %reduce-scatter.6.cloned.1.call-start = ((), (), s32[]{:S(2)}) async-start(), calls=%async_computation.5 | async-start | bytes 4718592 | tf_op jit(solution)/shard_map/reduce_scatter | solution.py:154
  10.2 320.6 %copy-start.90 = (pred[8]{0:T(512)(128)(4,1)}, pred[8]{0:T(512)(128)(4,1)S(1)}, u32[]{:S(2)}) copy-start(pred[8]{0:T(512)(128)(4,1)S(1)} %iota_compare_fusion.16) | copy-start | bytes 28
  10.2 320.6 %copy-start.57 = (pred[8]{0:T(512)(128)(4,1)}, pred[8]{0:T(512)(128)(4,1)S(1)}, u32[]{:S(2)}) copy-start(pred[8]{0:T(512)(128)(4,1)S(1)} %get-tuple-element.62) | copy-start | bytes 28
  10.2 320.6 %copy-start.59 = (pred[8]{0:T(512)(128)(4,1)}, pred[8]{0:T(512)(128)(4,1)S(1)}, u32[]{:S(2)}) copy-start(pred[8]{0:T(512)(128)(4,1)S(1)} %get-tuple-element.63) | copy-start | bytes 28
  13.0 269.3 %copy-start.133 = (pred[128]{0:T(512)(128)(4,1)}, pred[128]{0:T(512)(128)(4,1)S(1)}, u32[]{:S(2)}) copy-start(pred[128]{0:T(512)(128)(4,1)S(1)} %iota_compare_fusion.15) | copy-start | bytes 388
  14.4 266.2 %copy-start.108 = (f32[128]{0:T(128)}, f32[128]{0:T(128)S(1)}, u32[]{:S(2)}) copy-start(f32[128]{0:T(128)S(1)} %select_divide_fusion) | copy-start | bytes 1540
  18.1 204.2 %copy-start.34 = (s32[28]{0:T(128)S(1)}, s32[28]{0:T(128)}, u32[]{:S(2)}) copy-start(s32[28]{0:T(128)} %constant.182) | copy-start | bytes 340
  18.1 206.2 %copy-start.33 = (s32[28]{0:T(128)S(1)}, s32[28]{0:T(128)}, u32[]{:S(2)}) copy-start(s32[28]{0:T(128)} %constant.194) | copy-start | bytes 340
  220.2 11.5 collective-permute-start
  226.3 104.5 %copy-start.61 = (pred[8]{0:T(512)(128)(4,1)}, pred[8]{0:T(512)(128)(4,1)S(1)}, u32[]{:S(2)}) copy-start(pred[8]{0:T(512)(128)(4,1)S(1)} %get-tuple-element.60) | copy-start | bytes 28
  226.3 104.5 %copy-start.63 = (pred[8]{0:T(512)(128)(4,1)}, pred[8]{0:T(512)(128)(4,1)S(1)}, u32[]{:S(2)}) copy-start(pred[8]{0:T(512)(128)(4,1)S(1)} %get-tuple-element.61) | copy-start | bytes 28
  226.4 104.4 %copy-start.65 = (pred[8]{0:T(512)(128)(4,1)}, pred[8]{0:T(512)(128)(4,1)S(1)}, u32[]{:S(2)}) copy-start(pred[8]{0:T(512)(128)(4,1)S(1)} %get-tuple-element.58) | copy-start | bytes 28
  226.4 104.4 %copy-start.67 = (pred[8]{0:T(512)(128)(4,1)}, pred[8]{0:T(512)(128)(4,1)S(1)}, u32[]{:S(2)}) copy-start(pred[8]{0:T(512)(128)(4,1)S(1)} %get-tuple-element.59) | copy-start | bytes 28
  231.8 4.1 copy-start.16
  232.2 3.7 copy-start.37
  232.4 3.5 copy-start.69
  234.0 10.6 collective-permute-start.1
  245.4 3.3 copy-start.19
  245.4 3.3 copy-start.36
  248.7 10.4 collective-permute-start.2
  262.2 7.6 copy-start.41
  263.1 6.6 copy-start.75
  266.4 10.7 collective-permute-start.3
  278.9 3.3 copy-start.24
  282.3 10.5 collective-permute-start.4
  282.7 17.8 copy-start.109
  295.9 7.5 copy-start.45
  296.9 6.5 copy-start.81
  296.9 15.7 copy-start.93
  300.2 10.6 collective-permute-start.5
  303.4 12.5 copy-start.134
  312.6 3.3 copy-start.29
  312.6 10.5 collective-permute-start.6
  314.2 10.7 copy-start.92
  316.0 11.3 copy-start.135
  326.3 44.3 %copy-start.49 = (f32[16,128]{1,0:T(8,128)}, f32[16,128]{1,0:T(8,128)S(1)}, u32[]{:S(2)}) copy-start(f32[16,128]{1,0:T(8,128)S(1)} %get-tuple-element.37) | copy-start | bytes 24580
  327.3 43.3 %copy-start.87 = (f32[16,128]{1,0:T(8,128)}, f32[16,128]{1,0:T(8,128)S(1)}, u32[]{:S(2)}) copy-start(f32[16,128]{1,0:T(8,128)S(1)} %fusion.58) | copy-start | bytes 24580
  430.1 15.1 copy-start.40
  440.3 4.6 copy-start.55
  440.3 4.6 copy-start.20
  440.3 4.9 copy-start.73
  442.3 16.8 copy-start.94
  442.3 4.1 copy-start.54
  442.3 4.1 copy-start.22
  442.4 4.4 copy-start.2
  442.4 4.4 copy-start.42
  442.4 4.4 copy-start.76
  444.9 14.3 copy-start.118
  445.2 9.9 copy-start.96
  446.4 8.7 copy-start.121
  446.8 9.1 copy-start.98
  448.0 8.0 copy-start.123
  448.3 8.4 copy-start.100
  449.5 7.2 copy-start.125
  449.9 7.6 copy-start.102
  451.0 6.4 copy-start.127
  451.4 6.9 copy-start.104
  452.6 5.7 copy-start.129
  465.0 728.4 %reduce-scatter.8.cloned.1.call-start = ((), (), s32[]{:S(2)}) async-start(), calls=%async_computation.6 | async-start | bytes 4227072 | tf_op jit(solution)/shard_map/reduce_scatter | solution.py:111
  465.1 6.3 copy-start.18
  471.0 1384.0 %reduce-scatter.10.cloned.1.call-start = ((), (), s32[]{:S(2)}) async-start(), calls=%async_computation.7 | async-start | bytes 16908288
  (84 other events, 162.7 us)
Sparse Core Ops, SparseCore 0:
  9.7 205.7 all-gather.2
  217.2 201.3 all-gather.4
  465.1 83.6 reduce-scatter.5
  551.8 641.5 reduce-scatter.7
  1196.2 658.7 reduce-scatter.9
where the time goes:
time: 1870 us; the launch traced here: 1860 us
  waiting for transfers between devices  1650 us (88%)
  matrix products  79.7 us (4%)
  local copies, waits for them, and re-layouts  39.8 us (2%)
  blocking collectives  36.7 us (2%)
  between operations  25.9 us (1%)
  other arithmetic  25.1 us (1%)
    unnamed x6, waiting for transfers between devices  663 us
    reduce_scatter x1, waiting for transfers between devices, body(): lax.psum_scatter(bil_term, ('cand', 'prompt'), scatter_dimension=0, tiled...  618 us
    all_gather x1, waiting for transfers between devices, body(): lax.all_gather(proj_weight, ('cand', 'prompt'), axis=0, tiled=True)  197 us
    reduce_scatter x1, waiting for transfers between devices, body(): home = lax.psum_scatter(owners, 'cand', scatter_dimension=0, tiled=True)[0]  71.4 us
    ppermute x7, waiting for transfers between devices, shifted_2(): return lax.ppermute(value, axis, pairs)  55.2 us
    all_gather x1, waiting for transfers between devices, body(): lax.all_gather(bilinear, ('cand', 'prompt'), axis=0, tiled=True)  48 us
  transfers between devices with their start and end apart: 12, of which 12 were waited for; matrix products, arithmetic and copies ran while one was open for 5% of the time, Pallas kernels for 0%

commit v1 on v0

v1 whole, which is shorter than its diff:
```python
import jax
import jax.numpy as jnp
import numpy as np
from jax import lax
from jax.experimental import pallas as pl
from jax.experimental.pallas import tpu as pltpu
from jax.sharding import Mesh
from jax.sharding import PartitionSpec as P

HEAD_DIM = 64
CANDS = 8
ROWS = 128
SLICE = 128
WIDTH = 1024
PAIRS = CANDS * CANDS
EPSILON = 1e-06
FAR = 1e30
HIGH = lax.Precision.HIGHEST
BF = jnp.bfloat16
F32 = jnp.float32
NT = (((1,), (1,)), ((), ()))
NN = (((1,), (0,)), ((), ()))
TN = (((0,), (0,)), ((), ()))
CAND = ("xh", "z")
PROMPT = ("xl", "y", "core")


def mm(left, right, dims=NN, precision=None):
    return lax.dot_general(left, right, dims, precision=precision, preferred_element_type=F32)


def split(value):
    high = value.astype(BF)
    return high, (value - high.astype(F32)).astype(BF)


def lanes(shape):
    return lax.broadcasted_iota(jnp.int32, shape, len(shape) - 1)


def sublanes(shape):
    return lax.broadcasted_iota(jnp.int32, shape, len(shape) - 2)


def project_kernel(h_ref, w_ref, out_ref):
    depth = w_ref.shape[0] * w_ref.shape[2]
    h = h_ref[...].reshape(h_ref.shape[0] * ROWS, h_ref.shape[2])
    total = mm(h[:, :depth], w_ref[:, 0].reshape(depth, -1))
    total += mm(h[:, depth:], w_ref[:, 1].reshape(depth, -1))
    for dest in range(out_ref.shape[0]):
        out_ref[dest] = total[:, dest * SLICE : (dest + 1) * SLICE]


def project(h, w):
    steps = 4
    per = CANDS // steps
    dests = w.shape[3] // SLICE
    return pl.pallas_call(
        project_kernel,
        out_shape=jax.ShapeDtypeStruct((dests, CANDS * ROWS, SLICE), F32),
        grid=(steps,),
        in_specs=[
            pl.BlockSpec((per, ROWS, h.shape[2]), lambda s: (s, 0, 0)),
            pl.BlockSpec(w.shape, lambda s: (0, 0, 0, 0)),
        ],
        out_specs=pl.BlockSpec((dests, per * ROWS, SLICE), lambda s: (0, s, 0)),
        compiler_params=pltpu.CompilerParams(vmem_limit_bytes=24 << 20),
    )(h, w)


def head_queries(x_ref, i):
    rows = x_ref[pl.ds(pl.multiple_of(i * ROWS, ROWS), ROWS), :]
    lane = lanes(rows.shape)
    zero = jnp.zeros_like(rows)
    return jnp.concatenate(
        [jnp.where(lane < HEAD_DIM, rows, zero), jnp.where(lane < HEAD_DIM, zero, rows)], axis=0
    )


def forward_kernel(len_ref, p_ref, x_ref, mean_ref, col_ref, stat_ref, e_scr, m_scr, l_scr):
    total = p_ref[0]
    for source in range(1, p_ref.shape[0]):
        total += p_ref[source]
    x_ref[...] = total.astype(BF)
    wide = 2 * ROWS

    def one(i, carry):
        queries = head_queries(x_ref, i) * jnp.asarray(HEAD_DIM**-0.5, BF)
        own = len_ref[i]
        for j in range(CANDS):
            s = mm(x_ref[j * ROWS : (j + 1) * ROWS, :], queries, NT)
            s = jnp.where(sublanes(s.shape) < len_ref[j], s, -jnp.inf)
            m = jnp.max(s, axis=0, keepdims=True)
            e = jnp.exp(s - m)
            e_scr[j * ROWS : (j + 1) * ROWS, :] = e.astype(BF)
            m_scr[j : j + 1, :] = m
            l_scr[j : j + 1, :] = jnp.sum(e, axis=0, keepdims=True)
        shape = (CANDS, wide)
        token = jnp.bitwise_and(lanes(shape), ROWS - 1)
        live = jnp.logical_and(token < own, sublanes(shape) != i)
        weight = 1.0 / own.astype(F32)
        denom = l_scr[...]
        stat_ref[pl.ds(pl.multiple_of(i * CANDS, CANDS), CANDS), :] = jnp.where(
            live, m_scr[...] + jnp.log(denom) - jnp.log(weight * HEAD_DIM**-0.5), FAR
        )
        r = jnp.where(live, weight / denom, 0.0)
        first = lanes(shape) < ROWS
        r0h, r0l = split(jnp.where(first, r, 0.0))
        r1h, r1l = split(jnp.where(first, 0.0, r))
        got = mm(jnp.concatenate([r0h, r0l, r1h, r1l], axis=0), e_scr[...], NT)
        block = lanes((CANDS, CANDS * ROWS)) // ROWS == sublanes((CANDS, CANDS * ROWS))
        c0 = jnp.where(block, got[0:8] + got[8:16], 0.0)
        c1 = jnp.where(block, got[16:24] + got[24:32], 0.0)
        col_ref[i, 0:1, :] = jnp.sum(c0, axis=0, keepdims=True)
        col_ref[i, 1:2, :] = jnp.sum(c1, axis=0, keepdims=True)
        c0h, c0l = split(c0)
        c1h, c1l = split(c1)
        means = mm(jnp.concatenate([c0h, c0l, c1h, c1l], axis=0), x_ref[...])
        means = jnp.where(
            lanes((CANDS, SLICE)) < HEAD_DIM, means[0:8] + means[8:16], means[16:24] + means[24:32]
        )
        for dest in range(CANDS):
            mean_ref[dest, pl.ds(pl.multiple_of(i * CANDS, CANDS), CANDS), :] = means
        return carry

    lax.fori_loop(0, CANDS, one, 0)


def forward(lengths, parts):
    rows = CANDS * ROWS
    vmem = pl.BlockSpec(memory_space=pltpu.VMEM)
    return pl.pallas_call(
        forward_kernel,
        out_shape=(
            jax.ShapeDtypeStruct((rows, SLICE), BF),
            jax.ShapeDtypeStruct((CANDS, PAIRS, SLICE), F32),
            jax.ShapeDtypeStruct((CANDS, 2, rows), F32),
            jax.ShapeDtypeStruct((PAIRS, 2 * ROWS), F32),
        ),
        in_specs=[pl.BlockSpec(memory_space=pltpu.SMEM), vmem],
        out_specs=(vmem,) * 4,
        scratch_shapes=[
            pltpu.VMEM((rows, 2 * ROWS), BF),
            pltpu.VMEM((CANDS, 2 * ROWS), F32),
            pltpu.VMEM((CANDS, 2 * ROWS), F32),
        ],
        compiler_params=pltpu.CompilerParams(vmem_limit_bytes=16 << 20),
    )(lengths, parts)


def backward_kernel(
    len_ref, place_ref, mean_ref, bil_ref, x_ref, col_ref, stat_ref, sign_ref,
    dr_ref, logit_ref, term_ref,
    d_scr, along_scr, grad_scr,
):
    xh, z = place_ref[0], place_ref[1]
    here = xh * (CANDS // 2) + z
    means = jnp.concatenate([mean_ref[c] for c in range(CANDS)], axis=1)
    radius = jnp.sqrt(jnp.mean(means * means, axis=1, keepdims=True) + EPSILON)
    pooled = means / radius
    row, lane = sublanes((PAIRS, PAIRS)), lanes((PAIRS, PAIRS))
    swap = jnp.where(
        jnp.logical_and(row // CANDS == lane % CANDS, row % CANDS == lane // CANDS), 1.0, 0.0
    )
    reverse = mm(swap, pooled, precision=HIGH)
    rev_high, rev_low = split(reverse)
    both = mm(jnp.concatenate([rev_high, rev_low], axis=0), bil_ref[...], NT)
    toward = both[:PAIRS] + both[PAIRS:]
    logit = jnp.sum(pooled * toward, axis=1, keepdims=True)
    index = sublanes((PAIRS, 1))
    off = index // CANDS != index % CANDS
    logit = jnp.where(off, logit, 0.0)
    sign = sign_ref[...]
    dlogit = jnp.where(off, -sign * jax.nn.sigmoid(-sign * logit), 0.0)
    pick = lanes((PAIRS, SLICE))
    swapped = mm(
        swap, jnp.where(pick == 0, dlogit, jnp.where(pick == 1, logit, 0.0)), precision=HIGH
    )
    dlogit_rev, logit_rev = swapped[:, 0:1], swapped[:, 1:2]
    spread = jnp.where(
        lanes((PAIRS, SLICE)) == sublanes((PAIRS, SLICE)) % CANDS, logit, 0.0
    )
    gather = jnp.where(
        sublanes((CANDS, PAIRS)) == lanes((CANDS, PAIRS)) // CANDS, 1.0, 0.0
    )
    logit_ref[...] = mm(gather, spread, precision=HIGH)
    columns = pl.ds(pl.multiple_of(here * SLICE, SLICE), SLICE)
    back = mm(jnp.concatenate([rev_high, rev_low], axis=0), bil_ref[:, columns])
    back = back[:PAIRS] + back[PAIRS:]
    own_pooled = mean_ref[here] / radius
    own_toward = jnp.zeros((PAIRS, SLICE), F32)
    for c in range(CANDS):
        own_toward += jnp.where(here == c, toward[:, c * SLICE : (c + 1) * SLICE], 0.0)
    dpooled = dlogit * own_toward + dlogit_rev * back
    inner = (dlogit * logit + dlogit_rev * logit_rev) * (1.0 / WIDTH)
    dmeans = (dpooled - own_pooled * inner) / radius
    half = WIDTH // 2
    low_rows = jnp.concatenate(
        [mean_ref[z] / radius, mean_ref[z + CANDS // 2] / radius], axis=1
    ) * dlogit
    rev_half = jnp.where(xh == 0, reverse[:, :half], reverse[:, half:])
    ah, al = split(low_rows)
    bh, bl = split(rev_half)
    term_ref[...] = mm(
        jnp.concatenate([ah, al, ah], axis=0), jnp.concatenate([bh, bh, bl], axis=0), TN
    )
    dmeans_rev = mm(swap, dmeans, precision=HIGH)
    lane8 = lanes((CANDS, SLICE))
    turned = jnp.concatenate(
        [jnp.concatenate([col_ref[i] for i in range(CANDS)], axis=0)], axis=0
    ).T
    for j in range(CANDS):
        x = x_ref[j * ROWS : (j + 1) * ROWS, :]
        of_j = dmeans_rev[j * CANDS : (j + 1) * CANDS]
        heads = jnp.concatenate(
            [jnp.where(lane8 < HEAD_DIM, of_j, 0.0), jnp.where(lane8 < HEAD_DIM, 0.0, of_j)], axis=0
        )
        hh, hl = split(heads)
        along = mm(
            jnp.concatenate([x, x], axis=1),
            jnp.concatenate(
                [jnp.concatenate([hh, hl], axis=1), jnp.concatenate([hh, hl], axis=1)], axis=0
            ),
            NT,
        )
        ah, al = split(along)
        along_scr[j * ROWS : (j + 1) * ROWS, :] = jnp.where(lanes(along.shape) < 2 * CANDS, ah, al)
        spread_heads = jnp.zeros((2 * CANDS, SLICE), F32)
        order = sublanes((2 * CANDS, CANDS * 2)), lanes((2 * CANDS, CANDS * 2))
        to_heads = jnp.where(
            jnp.logical_and(order[0] // 2 == order[1] % CANDS, order[0] % 2 == order[1] // CANDS),
            1.0,
            0.0,
        )
        spread_heads = mm(to_heads, heads, precision=HIGH)
        grad_scr[j * ROWS : (j + 1) * ROWS, :] = mm(
            turned[j * ROWS : (j + 1) * ROWS, :], spread_heads, precision=HIGH
        )
    x_turned = x_ref[...].T
    wide = 2 * ROWS

    def one(i, carry):
        heads = head_queries(x_ref, i)
        queries = heads * jnp.asarray(HEAD_DIM**-0.5, BF)
        scale = len_ref[i].astype(F32) * HEAD_DIM**0.5
        shape = (4 * CANDS, wide)
        which = jnp.bitwise_and(sublanes(shape), 2 * CANDS - 1)
        chosen = jnp.where(
            which == jnp.where(lanes(shape) < ROWS, i, i + CANDS), 1.0, 0.0
        ).astype(BF)
        stats = stat_ref[pl.ds(pl.multiple_of(i * CANDS, CANDS), CANDS), :]
        for j in range(CANDS):
            s = mm(x_ref[j * ROWS : (j + 1) * ROWS, :], queries, NT)
            s = jnp.where(sublanes(s.shape) < len_ref[j], s, -jnp.inf)
            p = jnp.exp(s - stats[j : j + 1, :])
            along = mm(along_scr[j * ROWS : (j + 1) * ROWS, :], chosen)
            expected = jnp.sum(p * along, axis=0, keepdims=True) * scale
            d_scr[j * ROWS : (j + 1) * ROWS, :] = (p * (along - expected)).astype(BF)
        grad_scr[...] += mm(d_scr[...], heads)
        query = mm(x_turned, d_scr[...])
        query = jnp.concatenate([query[:HEAD_DIM, :ROWS], query[HEAD_DIM:, ROWS:]], axis=0)
        rows = pl.ds(pl.multiple_of(i * ROWS, ROWS), ROWS)
        grad_scr[rows, :] += query.T
        return carry

    lax.fori_loop(0, CANDS, one, 0)
    drows = grad_scr[...].astype(BF)
    for dest in range(dr_ref.shape[0]):
        dr_ref[dest] = drows


def backward(lengths, place, means, bil, x, col, stat, sign):
    rows = CANDS * ROWS
    vmem = pl.BlockSpec(memory_space=pltpu.VMEM)
    smem = pl.BlockSpec(memory_space=pltpu.SMEM)
    return pl.pallas_call(
        backward_kernel,
        out_shape=(
            jax.ShapeDtypeStruct((CANDS // 2, rows, SLICE), BF),
            jax.ShapeDtypeStruct((CANDS, SLICE), F32),
            jax.ShapeDtypeStruct((2 * SLICE, WIDTH // 2), F32),
        ),
        in_specs=[smem, smem] + [vmem] * 6,
        out_specs=(vmem,) * 3,
        scratch_shapes=[
            pltpu.VMEM((rows, 2 * ROWS), BF),
            pltpu.VMEM((rows, 4 * CANDS), BF),
            pltpu.VMEM((rows, SLICE), F32),
        ],
        compiler_params=pltpu.CompilerParams(vmem_limit_bytes=24 << 20),
    )(lengths, place, means, bil, x, col, stat, sign)


def gradient_kernel(h_ref, d_ref, term_ref, out_ref):
    count, rows, depth = h_ref.shape
    blocks, _, width = out_ref.shape
    h = h_ref[...].reshape(count * rows, depth)
    d = jnp.concatenate([d_ref[q] for q in range(d_ref.shape[0])], axis=1)
    total = mm(h, d, TN).reshape(blocks, depth // blocks, width)
    out_ref[...] = jnp.concatenate([total, term_ref[...]], axis=1).astype(BF)


def gradient(h, d, term):
    count, _, depth = h.shape
    steps = 4
    dests = term.shape[0]
    width = d.shape[0] * d.shape[2]
    block = depth // dests + term.shape[1]
    return pl.pallas_call(
        gradient_kernel,
        out_shape=jax.ShapeDtypeStruct((dests, block, width), BF),
        grid=(steps,),
        in_specs=[
            pl.BlockSpec((count, ROWS, depth // steps), lambda s: (0, 0, s)),
            pl.BlockSpec(d.shape, lambda s: (0, 0, 0)),
            pl.BlockSpec((dests // steps,) + term.shape[1:], lambda s: (s, 0, 0)),
        ],
        out_specs=pl.BlockSpec((dests // steps, block, width), lambda s: (s, 0, 0)),
        compiler_params=pltpu.CompilerParams(vmem_limit_bytes=24 << 20),
    )(h, d, term)


def finish_kernel(got_ref, proj_ref, bil_ref):
    half = got_ref.shape[2]
    count = got_ref.shape[0] // 2
    for part in range(2):
        total = got_ref[part * count].astype(F32)
        for source in range(1, count):
            total += got_ref[part * count + source].astype(F32)
        columns = slice(part * half, (part + 1) * half)
        proj_ref[:, columns] = total[: proj_ref.shape[0]]
        bil_ref[:, columns] = total[proj_ref.shape[0] :]


def finish(got, rows, bil_rows):
    vmem = pl.BlockSpec(memory_space=pltpu.VMEM)
    width = 2 * got.shape[2]
    return pl.pallas_call(
        finish_kernel,
        out_shape=(
            jax.ShapeDtypeStruct((rows, width), F32),
            jax.ShapeDtypeStruct((bil_rows, width), F32),
        ),
        in_specs=[vmem],
        out_specs=(vmem, vmem),
        compiler_params=pltpu.CompilerParams(vmem_limit_bytes=16 << 20),
    )(got)


def pair_signs():
    table = np.zeros((PAIRS, CANDS * (CANDS - 1) // 2), np.float32)
    upper_i, upper_j = np.triu_indices(CANDS, 1)
    for k, (i, j) in enumerate(zip(upper_i, upper_j)):
        table[i * CANDS + j, k] = 1.0
        table[j * CANDS + i, k] = -1.0
    return table


def body(hidden_states, proj_weight, bilinear, lengths, labels):
    xh, z = lax.axis_index("xh"), lax.axis_index("z")
    quarter = CANDS // 2
    lengths = lengths[0]
    hidden = hidden_states[0, 0]
    depth = hidden.shape[1]
    w = proj_weight.reshape(-1, 2, WIDTH // 2)
    other = lax.ppermute(jnp.where(xh == 0, w[:, 1], w[:, 0]), "xh", [(0, 1), (1, 0)])
    w = jnp.stack([jnp.where(xh == 0, w[:, 0], other), jnp.where(xh == 0, other, w[:, 1])])
    w = lax.all_gather(w, PROMPT, axis=0)
    h = hidden.reshape(ROWS, 2, quarter, depth // CANDS).transpose(2, 0, 1, 3)
    h = h.reshape(quarter, ROWS, depth // quarter)
    bil = jnp.broadcast_to(bilinear[None], (quarter,) + bilinear.shape)
    h = jnp.concatenate([h, bil], axis=1)
    h = jnp.broadcast_to(h[None], (2,) + h.shape).reshape((CANDS,) + h.shape[1:])
    h = lax.all_to_all(h, CAND, 0, 0)
    bil = lax.all_gather(h[:, ROWS:], PROMPT, axis=0)
    bil = bil.transpose(1, 0, 2, 3).reshape(WIDTH, WIDTH)
    parts = lax.all_to_all(project(h, w), "z", 0, 0)
    x, means, col, stat = forward(lengths, parts)
    means = lax.all_to_all(means, CAND, 0, 0)
    sign = 2.0 * labels[0].astype(F32) - 1.0
    sign = jnp.sum(pair_signs() * sign[None, :], axis=1, keepdims=True)
    drows, logits, term = backward(lengths, jnp.stack([xh, z]), means, bil, x, col, stat, sign)
    drows = lax.all_to_all(drows, "z", 0, 0)
    term = term.reshape(-1, bilinear.shape[0], term.shape[1])
    sent = gradient(h, drows, term)
    got = lax.all_to_all(sent, ("xh",) + PROMPT, 0, 0)
    grad_proj, grad_bil = finish(got, proj_weight.shape[0], bilinear.shape[0])
    return logits[None, :, :CANDS], grad_proj, grad_bil


def solution(mesh):
    parts = Mesh(mesh.devices.reshape(2, 4, 2, 4, 2), ("xh", "z", "xl", "y", "core"))
    in_specs = (
        P(PROMPT, CAND, None, None),
        P(CAND + PROMPT, None),
        P(CAND + PROMPT, None),
        P(PROMPT, None),
        P(PROMPT, None),
    )
    out_specs = (P(PROMPT, None, None), P(CAND + PROMPT, None), P(CAND + PROMPT, None))
    return jax.shard_map(body, mesh=parts, in_specs=in_specs, out_specs=out_specs, check_vma=False)
```

time: 1870 us -> 170 us (0.09)
  waiting for transfers between devices: 1650 us -> 25 us
  matrix products: 79.7 us -> 0 us
  blocking collectives: 36.7 us -> 80.9 us
  local copies, waits for them, and re-layouts: 39.8 us -> 11.8 us
  Pallas kernels: 0 us -> 23.9 us
  other arithmetic: 25.1 us -> 1.23 us
    reduce_scatter x2 -> x0, waiting for transfers between devices: 689 us -> none  [the longest x1 618 us: body(): lax.psum_scatter(bil_term, ('cand', 'prompt'), scatter_dimension=0, tiled...]
    unnamed x6 -> x2, waiting for transfers between devices: 663 us -> 0.03 us
    all_gather x2, waiting for transfers between devices: 245 us -> 0.02 us  [the longest x1 0.02 us: body(): w = lax.all_gather(w, PROMPT, axis=0)]
    all_to_all x0 -> x3, blocking collectives: none -> 80.9 us  [the longest x1 41.3 us: body(): h = lax.all_to_all(h, CAND, 0, 0)]
    dot_general x54 -> x0, matrix products: 79.7 us -> none  [the longest x7 15.8 us: body(): jnp.einsum('phts,pt->phs', backward_weights, row_weight, precision=HIGH)]
    ppermute x7 -> x1, waiting for transfers between devices: 55.2 us -> 0.43 us  [body(): lax.ppermute(jnp.where(xh == 0, w[:, 1], w[:, 0]), 'xh', [(0, 1), (1, 0)])]
    all_gather x1 -> x0, blocking collectives: 36.7 us -> none  [body(): everything = lax.all_gather(pooled[:, None], 'cand', axis=1, tiled=True)]
    all_to_all x0 -> x2, waiting for transfers between devices: none -> 24.6 us  [the longest x1 19.4 us: body(): got = lax.all_to_all(sent, ('xh',) + PROMPT, 0, 0)]
  transfers between devices with their start and end apart: 12 -> 5, of which waited for: 12 -> 3; matrix products, arithmetic and copies ran while one was open for 5% -> 5% of each run, Pallas kernels for 0% -> 6%
where the time goes in v1:
time: 170 us; the launch traced here: 169 us
  blocking collectives  80.9 us (48%)
  waiting for transfers between devices  25 us (15%)
  Pallas kernels  23.9 us (14%)
  between operations  14.2 us (8%)
  local copies, waits for them, and re-layouts  11.8 us (7%)
  starting transfers between devices  11.5 us (7%)
    all_to_all x1, blocking collectives, body(): h = lax.all_to_all(h, CAND, 0, 0)  41.3 us
    all_to_all x1, blocking collectives, body(): parts = lax.all_to_all(project(h, w), 'z', 0, 0)  26.4 us
    all_to_all x1, waiting for transfers between devices, body(): got = lax.all_to_all(sent, ('xh',) + PROMPT, 0, 0)  19.4 us
    all_to_all x1, blocking collectives, body(): drows = lax.all_to_all(drows, 'z', 0, 0)  13.3 us
    pallas_call x1, Pallas kernels, backward(): pl.pallas_call(backward_kernel, out_shape=(jax.ShapeDtypeStruct((CANDS //...  9.78 us
    pallas_call x1, Pallas kernels, forward(): pl.pallas_call(forward_kernel, out_shape=(jax.ShapeDtypeStruct((rows, SLI...  8.17 us
    all_to_all x1, waiting for transfers between devices, body(): means = lax.all_to_all(means, CAND, 0, 0)  5.21 us
    all_to_all x1, starting transfers between devices, body(): got = lax.all_to_all(sent, ('xh',) + PROMPT, 0, 0)  4.82 us
  transfers between devices with their start and end apart: 5, of which 3 were waited for; matrix products, arithmetic and copies ran while one was open for 5% of the time, Pallas kernels for 6%

profile of v1, /device:TPU:0, one launch (start us, length us, event | category | flops | bytes accessed | tf_op | source)
XLA Modules:
  0.0 168.7 jit_solution(7890173697571571518)
XLA Ops:
  7.2 0.0 all-gather.5.cloned.1.call-start
  7.2 0.9 reshape.25
  8.1 0.1 fusion.2
  8.2 0.0 copy-start.3
  8.2 3.2 %collective-permute-start = (bf16[32,512]{1,0:T(8,128)(2,1)S(1)}, bf16[32,512]{1,0:T(8,128)(2,1)S(1)}, u32[]{:S(2)}, u32[]{:S(2)}) collective-permute-start(bf16[32,512]{1,0:T(8,128)(2,1)S(1)} %bitcast_select_fusion.1), channel_id=1, source_target_pairs={{0,64},{64,0},{1,65},{65,1},{2,66},{66,2},{3,67},{67,3},{4,68},{68... | collective-permute-start | bytes 98312 | tf_op jit(solution)/shard_map/ppermute | solution.py:366
  11.4 1.6 copy.52
  13.0 0.1 copy.53
  13.1 0.0 copy-done.3
  13.1 0.2 copy.54
  13.3 0.4 collective-permute-done
  13.7 0.6 pad_maximum_fusion.1
  14.4 0.0 all-gather.5.cloned.1.call-update
  14.4 0.0 all-gather.7.cloned.1.call-start
  14.4 0.1 broadcast_in_dim.8
  14.6 0.4 pad_maximum_fusion
  15.0 1.3 copy.55
  16.3 0.3 broadcast_in_dim.9
  16.6 41.3 %all_to_all.25.h_ref = bf16[8,136,1024]{2,1,0:T(8,128)(2,1)S(1)} all-to-all(bf16[8,136,1024]{2,1,0:T(8,128)(2,1)S(1)} %bitcast.38), channel_id=1, replica_groups=mesh['xh'=2,'z'=4,'xl'=2,'y'=4,'core'=2] {'xh','z'}, dimensions={0} | all-to-all | bytes 4456448 | tf_op jit(solution)/shard_map/all_to_all | solution.py:374
  57.8 0.7 slice.20
  58.5 0.0 all-gather.7.cloned.1.call-update
  58.5 0.0 all-gather.5.cloned.1.call-done
  58.6 0.0 copy-start.1
  58.6 1.2 copy-done.1
  59.8 2.1 %shard_map.85 = f32[4,1024,128]{2,1,0:T(8,128)S(1)} custom-call(bf16[8,136,1024]{2,1,0:T(8,128)(2,1)S(1)} %all_to_all.25.h_ref, bf16[16,2,32,512]{3,2,1,0:T(8,128)(2,1)S(1)} %bitcast.34), custom_call_target="tpu_custom_call" | custom-call | tf_op jit(solution)/shard_map/pallas_call | solution.py:58
  61.9 0.0 copy-start.2
  61.9 26.4 %all_to_all.26.p_ref = f32[4,1024,128]{2,1,0:T(8,128)S(1)} all-to-all(f32[4,1024,128]{2,1,0:T(8,128)S(1)} %shard_map.85), channel_id=1, replica_groups=mesh['xh'=2,'z'=4,'xl'=2,'y'=4,'core'=2] {'z'}, dimensions={0} | all-to-all | bytes 4194304 | tf_op jit(solution)/shard_map/all_to_all | solution.py:377
  88.2 0.0 copy-start.5
  88.2 0.0 copy-start.4
  88.2 0.0 copy-done.2
  88.3 8.2 %shard_map.86 = (bf16[1024,128]{1,0:T(8,128)(2,1)S(1)}, f32[8,64,128]{2,1,0:T(8,128)}, f32[8,2,1024]{2,1,0:T(2,128)S(1)}, f32[64,256]{1,0:T(8,128)S(1)}) custom-call(s32[8]{0:T(128)S(1)} %bitcast.36, f32[4,1024,128]{2,1,0:T(8,128)S(1)} %all_to_all.26.p_ref), custom_call_target="tpu_custom_call" | custom-call | tf_op jit(solution)/shard_map/pallas_call | solution.py:132
  96.4 3.4 %all-to-all-start.2 = ((f32[8,64,128]{2,1,0:T(8,128)}), f32[8,64,128]{2,1,0:T(8,128)S(1)}, u32[]{:S(2)}, u32[]{:S(2)}) async-start(f32[8,64,128]{2,1,0:T(8,128)} %get-tuple-element.12), calls=%async_computation.2 | async-start | bytes 524288 | tf_op jit(solution)/shard_map/all_to_all | solution.py:379
  99.8 0.0 copy-done.5
  99.9 0.0 copy-done.4
  99.9 0.1 multiply_reduce_fusion
  100.0 0.1 copy.57.sign_ref
  100.1 0.1 pad_add_fusion.place_ref
  100.1 0.0 all-gather.7.cloned.1.call-done
  100.1 3.1 %copy.56 = bf16[16,8,8,1024]{3,2,0,1:T(8,128)(2,1)} copy(bf16[16,8,8,1024]{3,2,1,0:T(8,128)(2,1)} %bitcast.41) | data formatting | bytes 4194304 | tf_op jit(solution)/shard_map/all_gather | solution.py:375
  103.3 5.2 %all-to-all-done.2.mean_ref = f32[8,64,128]{2,1,0:T(8,128)S(1)} async-done(((f32[8,64,128]{2,1,0:T(8,128)}), f32[8,64,128]{2,1,0:T(8,128)S(1)}, u32[]{:S(2)}, u32[]{:S(2)}) %all-to-all-start.2) | async-done | bytes 262176 | tf_op jit(solution)/shard_map/all_to_all | solution.py:379
  108.5 0.0 copy-start
  108.5 1.6 copy-done
  110.1 9.8 %shard_map.87 = (bf16[4,1024,128]{2,1,0:T(8,128)(2,1)S(1)}, f32[8,128]{1,0:T(8,128)S(1)}, f32[256,512]{1,0:T(8,128)S(1)}) custom-call(s32[8]{0:T(128)S(1)} %bitcast.37, s32[2]{0:T(128)S(1)} %pad_add_fusion.place_ref, f32[8,64,128]{2,1,0:T(8,128)S(1)} %all-to-all-done.2.mean_ref, bf16[1024,1024]{1,0:T(8,128)(2,1)S(1)} %bitcast.33, ...), custom_call_target="tpu_custom_call" | custom-call | tf_op jit(solution)/shard_map/pallas_call | solution.py:276
  119.9 13.3 %all_to_all.27.d_ref = bf16[4,1024,128]{2,1,0:T(8,128)(2,1)S(1)} all-to-all(bf16[4,1024,128]{2,1,0:T(8,128)(2,1)S(1)} %get-tuple-element.17), channel_id=1, replica_groups=mesh['xh'=2,'z'=4,'xl'=2,'y'=4,'core'=2] {'z'}, dimensions={0} | all-to-all | bytes 2097152 | tf_op jit(solution)/shard_map/all_to_all | solution.py:383
  133.2 3.1 %shard_map.88 = bf16[32,40,512]{2,1,0:T(8,128)(2,1)} custom-call(bf16[8,136,1024]{2,1,0:T(8,128)(2,1)S(1)} %all_to_all.25.h_ref, bf16[4,1024,128]{2,1,0:T(8,128)(2,1)S(1)} %all_to_all.27.d_ref, f32[32,8,512]{2,1,0:T(8,128)S(1)} %bitcast.35), custom_call_target="tpu_custom_call" | custom-call | tf_op jit(solution)/shard_map/pallas_call | solution.py:309
  136.3 4.8 %all-to-all-start.4 = ((bf16[32,40,512]{2,1,0:T(8,128)(2,1)}), bf16[32,40,512]{2,1,0:T(8,128)(2,1)S(1)}, u32[]{:S(2)}, u32[]{:S(2)}) async-start(bf16[32,40,512]{2,1,0:T(8,128)(2,1)} %shard_map.88), calls=%async_computation.4 | async-start | bytes 2621440 | tf_op jit(solution)/shard_map/all_to_all | solution.py:386
  141.1 0.6 slice_bitcast_fusion
  141.7 19.4 %all-to-all-done.4.got_ref = bf16[32,40,512]{2,1,0:T(8,128)(2,1)S(1)} async-done(((bf16[32,40,512]{2,1,0:T(8,128)(2,1)}), bf16[32,40,512]{2,1,0:T(8,128)(2,1)S(1)}, u32[]{:S(2)}, u32[]{:S(2)}) %all-to-all-start.4) | async-done | bytes 1310752 | tf_op jit(solution)/shard_map/all_to_all | solution.py:386
  161.1 0.8 shard_map.89
  (3 shorter events, 0.0 us)
Async XLA Ops:
  7.2 51.4 %all-gather.5.cloned.1.call-start = ((), (), s32[]{:S(2)}) async-start(), calls=%async_computation.5 | async-start | bytes 1114112 | tf_op jit(solution)/shard_map/all_gather | solution.py:368
  8.2 4.9 %copy-start.3 = (bf16[8,1024]{1,0:T(8,128)(2,1)S(1)}, bf16[8,1024]{1,0:T(8,128)(2,1)}, u32[]{:S(2)}) copy-start(bf16[8,1024]{1,0:T(8,128)(2,1)} %param.8) | copy-start | bytes 49156
  8.2 5.5 %collective-permute-start = (bf16[32,512]{1,0:T(8,128)(2,1)S(1)}, bf16[32,512]{1,0:T(8,128)(2,1)S(1)}, u32[]{:S(2)}, u32[]{:S(2)}) collective-permute-start(bf16[32,512]{1,0:T(8,128)(2,1)S(1)} %bitcast_select_fusion.1), channel_id=1, source_target_pairs={{0,64},{64,0},{1,65},{65,1},{2,66},{66,2},{3,67},{67,3},{4,68},{68... | collective-permute-start | bytes 98312 | tf_op jit(solution)/shard_map/ppermute | solution.py:366
  14.4 85.7 %all-gather.7.cloned.1.call-start = ((), (), s32[]{:S(2)}) async-start(), calls=%async_computation.6 | async-start | bytes 2228224 | tf_op jit(solution)/shard_map/all_gather | solution.py:375
  58.6 1.2 copy-start.1
  61.9 26.4 %copy-start.2 = (s32[1,8]{1,0:T(1,128)S(1)}, s32[1,8]{1,0:T(1,128)}, u32[]{:S(2)}) copy-start(s32[1,8]{1,0:T(1,128)} %param.9) | copy-start | bytes 100
  88.2 11.6 %copy-start.5 = (s32[1,28]{1,0:T(1,128)S(1)}, s32[1,28]{1,0:T(1,128)}, u32[]{:S(2)}) copy-start(s32[1,28]{1,0:T(1,128)} %param.10) | copy-start | bytes 340
  88.2 11.6 %copy-start.4 = (f32[64,28]{0,1:T(8,128)S(1)}, f32[64,28]{0,1:T(8,128)}, u32[]{:S(2)}) copy-start(f32[64,28]{0,1:T(8,128)} %constant.23.clone) | copy-start | bytes 21508
  96.4 12.1 %all-to-all-start.2 = ((f32[8,64,128]{2,1,0:T(8,128)}), f32[8,64,128]{2,1,0:T(8,128)S(1)}, u32[]{:S(2)}, u32[]{:S(2)}) async-start(f32[8,64,128]{2,1,0:T(8,128)} %get-tuple-element.12), calls=%async_computation.2 | async-start | bytes 524288 | tf_op jit(solution)/shard_map/all_to_all | solution.py:379
  108.5 1.6 copy-start
  136.3 24.8 %all-to-all-start.4 = ((bf16[32,40,512]{2,1,0:T(8,128)(2,1)}), bf16[32,40,512]{2,1,0:T(8,128)(2,1)S(1)}, u32[]{:S(2)}, u32[]{:S(2)}) async-start(bf16[32,40,512]{2,1,0:T(8,128)(2,1)} %shard_map.88), calls=%async_computation.4 | async-start | bytes 2621440 | tf_op jit(solution)/shard_map/all_to_all | solution.py:386
Sparse Core Ops, SparseCore 0:
  14.5 36.3 all-gather.4
  58.7 30.8 all-gather.6

commit v2 on v1

v2 whole, which is shorter than its diff:
```python
import jax
import jax.numpy as jnp
import numpy as np
from jax import lax
from jax.experimental import pallas as pl
from jax.experimental.pallas import tpu as pltpu
from jax.sharding import Mesh
from jax.sharding import PartitionSpec as P

HEAD_DIM = 64
CANDS = 8
ROWS = 128
SLICE = 128
WIDTH = 1024
PAIRS = CANDS * CANDS
EPSILON = 1e-06
FAR = 1e30
HIGH = lax.Precision.HIGHEST
BF = jnp.bfloat16
F32 = jnp.float32
NT = (((1,), (1,)), ((), ()))
NN = (((1,), (0,)), ((), ()))
TN = (((0,), (0,)), ((), ()))
CAND = ("xh", "z")
PROMPT = ("xl", "y", "core")


def mm(left, right, dims=NN, precision=None):
    return lax.dot_general(left, right, dims, precision=precision, preferred_element_type=F32)


def split(value):
    high = value.astype(BF)
    return high, (value - high.astype(F32)).astype(BF)


def lanes(shape):
    return lax.broadcasted_iota(jnp.int32, shape, len(shape) - 1)


def sublanes(shape):
    return lax.broadcasted_iota(jnp.int32, shape, len(shape) - 2)


def pack_kernel(low_ref, high_ref, bil_ref, out_ref):
    half = low_ref.shape[1]
    bil = bil_ref[...]
    for dest in range(out_ref.shape[0]):
        out_ref[dest, 0, :ROWS, :half] = low_ref[...]
        out_ref[dest, 0, :ROWS, half:] = high_ref[...]
        out_ref[dest, 0, ROWS:, :] = jnp.concatenate([bil, bil], axis=0)


def pack(hidden, bil):
    quarter = CANDS // 2
    half = hidden.shape[1] // CANDS
    rows = ROWS + 2 * bil.shape[0]
    return pl.pallas_call(
        pack_kernel,
        out_shape=jax.ShapeDtypeStruct((2, quarter, rows, 2 * half), BF),
        grid=(quarter,),
        in_specs=[
            pl.BlockSpec((ROWS, half), lambda q: (0, q)),
            pl.BlockSpec((ROWS, half), lambda q: (0, q + CANDS // 2)),
            pl.BlockSpec(bil.shape, lambda q: (0, 0)),
        ],
        out_specs=pl.BlockSpec((2, 1, rows, 2 * half), lambda q: (0, q, 0, 0)),
        compiler_params=pltpu.CompilerParams(vmem_limit_bytes=16 << 20),
    )(hidden, hidden, bil)


def project_kernel(place_ref, h_ref, *refs):
    pieces, out_ref, w_scr = refs[:-2], refs[-2], refs[-1]
    count = len(pieces)

    @pl.when(pl.program_id(0) == 0)
    def _():
        for k, piece in enumerate(pieces):
            w_scr[:, :, lax.rem(place_ref[2] + count - k, count)] = piece[...]

    h = h_ref[...].reshape(h_ref.shape[0] * ROWS, h_ref.shape[2])
    total = mm(h, w_scr[...].reshape(h.shape[1], -1))
    for dest in range(out_ref.shape[0]):
        out_ref[dest] = total[:, dest * SLICE : (dest + 1) * SLICE]


def project(place, h, pieces):
    steps = 4
    per = CANDS // steps
    shape = pieces[0].shape
    dests = shape[3] // SLICE
    return pl.pallas_call(
        project_kernel,
        out_shape=jax.ShapeDtypeStruct((dests, CANDS * ROWS, SLICE), F32),
        grid=(steps,),
        in_specs=[
            pl.BlockSpec(memory_space=pltpu.SMEM),
            pl.BlockSpec((per, ROWS, h.shape[2]), lambda s: (s, 0, 0)),
        ]
        + [pl.BlockSpec(shape, lambda s: (0, 0, 0, 0))] * len(pieces),
        out_specs=pl.BlockSpec((dests, per * ROWS, SLICE), lambda s: (0, s, 0)),
        scratch_shapes=[pltpu.VMEM(shape[:2] + (len(pieces),) + shape[2:], BF)],
        compiler_params=pltpu.CompilerParams(vmem_limit_bytes=24 << 20),
    )(place, h, *pieces)


def extend(x, len_ref):
    blocks = []
    for j in range(CANDS):
        shape = (ROWS, SLICE)
        lane = lanes(shape)
        member = jnp.logical_and(lane < 3 * CANDS, jnp.bitwise_and(lane, CANDS - 1) == j)
        dead = jnp.logical_and(lane == 3 * CANDS, sublanes(shape) >= len_ref[j])
        blocks.append(jnp.where(dead, -FAR, jnp.where(member, 1.0, 0.0)).astype(BF))
    return jnp.concatenate([x, jnp.concatenate(blocks, axis=0)], axis=1)


def head_weights(xt_ref, i, shift=None):
    columns = xt_ref[:, i * ROWS : (i + 1) * ROWS] * jnp.asarray(HEAD_DIM**-0.5, BF)
    zero = jnp.zeros((HEAD_DIM, ROWS), BF)
    top = jnp.concatenate([columns[:HEAD_DIM], zero], axis=1)
    bottom = jnp.concatenate([zero, columns[HEAD_DIM:]], axis=1)
    wide = 2 * ROWS
    if shift is None:
        parts = [jnp.zeros((3 * CANDS, wide), F32)]
    else:
        high = shift.astype(BF).astype(F32)
        rest = shift - high
        middle = rest.astype(BF).astype(F32)
        parts = [-high, -middle, middle - rest]
    parts.append(jnp.where(sublanes((CANDS, wide)) == 0, 1.0, 0.0))
    extra = jnp.concatenate(parts, axis=0).astype(BF)
    return jnp.concatenate([top, bottom, extra, jnp.zeros((SLICE - 4 * CANDS, wide), BF)], axis=0)


def forward_kernel(len_ref, p_ref, x_ref, xt_ref, mean_ref, col_ref, stat_ref, e_scr, m_scr, l_scr):
    total = p_ref[0]
    for source in range(1, p_ref.shape[0]):
        total += p_ref[source]
    total = total.astype(BF)
    x_ref[...] = extend(total, len_ref)
    xt_ref[...] = total.T
    wide = 2 * ROWS
    for i in range(CANDS):
        weights = head_weights(xt_ref, i)
        for j in range(CANDS):
            s = mm(x_ref[j * ROWS : (j + 1) * ROWS, :], weights)
            m = jnp.max(s, axis=0, keepdims=True)
            e = jnp.exp(s - m)
            e_scr[i, j * ROWS : (j + 1) * ROWS, :] = e.astype(BF)
            m_scr[i, j : j + 1, :] = m
            l_scr[i, j : j + 1, :] = jnp.sum(e, axis=0, keepdims=True)
    for i in range(CANDS):
        own = len_ref[i]
        shape = (CANDS, wide)
        token = jnp.bitwise_and(lanes(shape), ROWS - 1)
        live = jnp.logical_and(token < own, sublanes(shape) != i)
        weight = 1.0 / own.astype(F32)
        denom = l_scr[i]
        stat_ref[i * CANDS : (i + 1) * CANDS, :] = jnp.where(
            live, m_scr[i] + jnp.log(denom) - jnp.log(weight * HEAD_DIM**-0.5), FAR
        )
        r = jnp.where(live, weight / denom, 0.0)
        first = lanes(shape) < ROWS
        r0h, r0l = split(jnp.where(first, r, 0.0))
        r1h, r1l = split(jnp.where(first, 0.0, r))
        got = mm(jnp.concatenate([r0h, r0l, r1h, r1l], axis=0), e_scr[i], NT)
        block = lanes((CANDS, CANDS * ROWS)) // ROWS == sublanes((CANDS, CANDS * ROWS))
        c0 = jnp.where(block, got[0:8] + got[8:16], 0.0)
        c1 = jnp.where(block, got[16:24] + got[24:32], 0.0)
        col_ref[0, i : i + 1, :] = jnp.sum(c0, axis=0, keepdims=True)
        col_ref[1, i : i + 1, :] = jnp.sum(c1, axis=0, keepdims=True)
        c0h, c0l = split(c0)
        c1h, c1l = split(c1)
        means = mm(jnp.concatenate([c0h, c0l, c1h, c1l], axis=0), x_ref[:, :SLICE])
        means = jnp.where(
            lanes((CANDS, SLICE)) < HEAD_DIM, means[0:8] + means[8:16], means[16:24] + means[24:32]
        )
        for dest in range(CANDS):
            mean_ref[dest, i * CANDS : (i + 1) * CANDS, :] = means


def forward(lengths, parts):
    rows = CANDS * ROWS
    vmem = pl.BlockSpec(memory_space=pltpu.VMEM)
    return pl.pallas_call(
        forward_kernel,
        out_shape=(
            jax.ShapeDtypeStruct((rows, 2 * SLICE), BF),
            jax.ShapeDtypeStruct((SLICE, rows), BF),
            jax.ShapeDtypeStruct((CANDS, PAIRS, SLICE), F32),
            jax.ShapeDtypeStruct((2, CANDS, rows), F32),
            jax.ShapeDtypeStruct((PAIRS, 2 * ROWS), F32),
        ),
        in_specs=[pl.BlockSpec(memory_space=pltpu.SMEM), vmem],
        out_specs=(vmem,) * 5,
        scratch_shapes=[
            pltpu.VMEM((CANDS, rows, 2 * ROWS), BF),
            pltpu.VMEM((CANDS, CANDS, 2 * ROWS), F32),
            pltpu.VMEM((CANDS, CANDS, 2 * ROWS), F32),
        ],
        compiler_params=pltpu.CompilerParams(vmem_limit_bytes=24 << 20),
    )(lengths, parts)


def backward_kernel(
    len_ref, place_ref, mean_ref, bil0_ref, bil1_ref, bil2_ref, bil3_ref,
    x_ref, xt_ref, col_ref, stat_ref, sign_ref, label_ref,
    dr_ref, logit_ref, term_ref,
    d_scr, along_scr, grad_scr, bil_scr,
):
    xh, z, y = place_ref[0], place_ref[1], place_ref[2]
    pieces = (bil0_ref, bil1_ref, bil2_ref, bil3_ref)
    for k, piece in enumerate(pieces):
        for part in range(2):
            bil_scr[:, part, lax.rem(y + len(pieces) - k, len(pieces))] = piece[part]
    here = xh * (CANDS // 2) + z
    means = jnp.concatenate([mean_ref[c] for c in range(CANDS)], axis=1)
    radius = jnp.sqrt(jnp.mean(means * means, axis=1, keepdims=True) + EPSILON)
    pooled = means / radius
    row, lane = sublanes((PAIRS, PAIRS)), lanes((PAIRS, PAIRS))
    swap = jnp.where(
        jnp.logical_and(row // CANDS == lane % CANDS, row % CANDS == lane // CANDS), 1.0, 0.0
    )
    reverse = mm(swap, pooled, precision=HIGH)
    rev_high, rev_low = split(reverse)
    both = mm(jnp.concatenate([rev_high, rev_low], axis=0), bil_scr[...].reshape(WIDTH, WIDTH), NT)
    toward = both[:PAIRS] + both[PAIRS:]
    logit = jnp.sum(pooled * toward, axis=1, keepdims=True)
    index = sublanes((PAIRS, 1))
    off = index // CANDS != index % CANDS
    logit = jnp.where(off, logit, 0.0)
    sign = jnp.sum(sign_ref[...] * (2.0 * label_ref[...].astype(F32) - 1.0), axis=1, keepdims=True)
    dlogit = jnp.where(off, -sign * jax.nn.sigmoid(-sign * logit), 0.0)
    pick = lanes((PAIRS, SLICE))
    swapped = mm(
        swap, jnp.where(pick == 0, dlogit, jnp.where(pick == 1, logit, 0.0)), precision=HIGH
    )
    dlogit_rev, logit_rev = swapped[:, 0:1], swapped[:, 1:2]
    spread = jnp.where(
        lanes((PAIRS, CANDS)) == sublanes((PAIRS, CANDS)) % CANDS, logit, 0.0
    )
    gather = jnp.where(
        sublanes((CANDS, PAIRS)) == lanes((CANDS, PAIRS)) // CANDS, 1.0, 0.0
    )
    logit_ref[...] = mm(gather, spread, precision=HIGH)
    columns = pl.ds(pl.multiple_of(here * SLICE, SLICE), SLICE)
    back = mm(
        jnp.concatenate([rev_high, rev_low], axis=0),
        bil_scr[:, :, :, :, columns].reshape(WIDTH, SLICE),
    )
    back = back[:PAIRS] + back[PAIRS:]
    own_pooled = mean_ref[here] / radius
    own_toward = jnp.zeros((PAIRS, SLICE), F32)
    for c in range(CANDS):
        own_toward += jnp.where(here == c, toward[:, c * SLICE : (c + 1) * SLICE], 0.0)
    dpooled = dlogit * own_toward + dlogit_rev * back
    inner = (dlogit * logit + dlogit_rev * logit_rev) * (1.0 / WIDTH)
    dmeans = (dpooled - own_pooled * inner) / radius
    half = WIDTH // 2
    low_rows = jnp.concatenate(
        [mean_ref[z] / radius, mean_ref[z + CANDS // 2] / radius], axis=1
    ) * dlogit
    rev_half = jnp.where(xh == 0, reverse[:, :half], reverse[:, half:])
    ah, al = split(low_rows)
    bh, bl = split(rev_half)
    term_ref[...] = mm(
        jnp.concatenate([ah, al, ah], axis=0), jnp.concatenate([bh, bh, bl], axis=0), TN
    )
    dmeans_rev = mm(swap, dmeans, precision=HIGH)
    lane8 = lanes((CANDS, SLICE))
    col = col_ref[...].reshape(2 * CANDS, CANDS * ROWS)
    col_high = col.astype(BF).astype(F32)
    turned = jnp.concatenate([col_high, col - col_high, col_high], axis=0).T.astype(BF)
    for j in range(CANDS):
        rows = slice(j * ROWS, (j + 1) * ROWS)
        x = x_ref[rows, :SLICE]
        of_j = dmeans_rev[j * CANDS : (j + 1) * CANDS]
        heads = jnp.concatenate(
            [jnp.where(lane8 < HEAD_DIM, of_j, 0.0), jnp.where(lane8 < HEAD_DIM, 0.0, of_j)], axis=0
        )
        hh, hl = split(heads)
        along = mm(
            jnp.concatenate([x, x], axis=1),
            jnp.concatenate(
                [jnp.concatenate([hh, hl], axis=1), jnp.concatenate([hh, hl], axis=1)], axis=0
            ),
            NT,
        )
        ah, al = split(along)
        along_scr[rows, :] = jnp.where(lanes(along.shape) < 2 * CANDS, ah, al)
        grad_scr[rows, :] = mm(turned[rows, :], jnp.concatenate([hh, hh, hl], axis=0))
    wide = 2 * ROWS
    for i in range(CANDS):
        weights = head_weights(xt_ref, i, stat_ref[i * CANDS : (i + 1) * CANDS, :])
        scale = len_ref[i].astype(F32) * HEAD_DIM**0.5
        shape = (4 * CANDS, wide)
        which = jnp.bitwise_and(sublanes(shape), 2 * CANDS - 1)
        chosen = jnp.where(
            which == jnp.where(lanes(shape) < ROWS, i, i + CANDS), 1.0, 0.0
        ).astype(BF)
        for j in range(CANDS):
            rows = slice(j * ROWS, (j + 1) * ROWS)
            p = jnp.exp(mm(x_ref[rows, :], weights))
            along = mm(along_scr[rows, :], chosen)
            expected = jnp.sum(p * along, axis=0, keepdims=True) * scale
            d_scr[i, rows, :] = (p * (along - expected)).astype(BF)
        lane = lanes((ROWS, SLICE))
        own = x_ref[i * ROWS : (i + 1) * ROWS, :SLICE]
        zero = jnp.zeros_like(own)
        heads = jnp.concatenate(
            [jnp.where(lane < HEAD_DIM, own, zero), jnp.where(lane < HEAD_DIM, zero, own)], axis=0
        )
        grad_scr[...] += mm(d_scr[i], heads)
        query = mm(xt_ref[...], d_scr[i])
        query = jnp.concatenate([query[:HEAD_DIM, :ROWS], query[HEAD_DIM:, ROWS:]], axis=0)
        grad_scr[i * ROWS : (i + 1) * ROWS, :] += query.T
    drows = grad_scr[...].astype(BF)
    for dest in range(dr_ref.shape[0]):
        dr_ref[dest] = drows


def backward(lengths, place, means, bil, x, xt, col, stat, labels):
    rows = CANDS * ROWS
    vmem = pl.BlockSpec(memory_space=pltpu.VMEM)
    smem = pl.BlockSpec(memory_space=pltpu.SMEM)
    return pl.pallas_call(
        backward_kernel,
        out_shape=(
            jax.ShapeDtypeStruct((CANDS // 2, rows, SLICE), BF),
            jax.ShapeDtypeStruct((CANDS, CANDS), F32),
            jax.ShapeDtypeStruct((2 * SLICE, WIDTH // 2), F32),
        ),
        in_specs=[smem, smem] + [vmem] * (7 + len(bil)),
        out_specs=(vmem,) * 3,
        scratch_shapes=[
            pltpu.VMEM((CANDS, rows, 2 * ROWS), BF),
            pltpu.VMEM((rows, 4 * CANDS), BF),
            pltpu.VMEM((rows, SLICE), F32),
            pltpu.VMEM((CANDS, 2, len(bil)) + bil[0].shape[2:], BF),
        ],
        compiler_params=pltpu.CompilerParams(vmem_limit_bytes=32 << 20),
    )(lengths, place, means, *bil, x, xt, col, stat, pair_signs(), labels)


def gradient_kernel(place_ref, h_ref, d_ref, term_ref, mine_ref, other_ref, scr):
    count, rows, depth = h_ref.shape
    groups, block, width = mine_ref.shape
    h = h_ref[...].reshape(count * rows, depth)
    d = jnp.concatenate([d_ref[q] for q in range(d_ref.shape[0])], axis=1)
    total = mm(h, d, TN).reshape(2 * groups, -1, width)
    total = jnp.concatenate([total, term_ref[...]], axis=1)
    scr[...] = total.reshape(groups, 2, block, width)
    core = place_ref[3]
    mine_ref[...] = scr[:, core]
    other_ref[...] = scr[:, 1 - core].astype(BF)


def gradient(place, h, d, term):
    count, _, depth = h.shape
    steps = 4
    dests = term.shape[0] // 2
    width = d.shape[0] * d.shape[2]
    block = depth // dests // 2 + term.shape[1]
    groups = dests // steps
    out = pl.BlockSpec((groups, block, width), lambda s: (s, 0, 0))
    return pl.pallas_call(
        gradient_kernel,
        out_shape=(
            jax.ShapeDtypeStruct((dests, block, width), F32),
            jax.ShapeDtypeStruct((dests, block, width), BF),
        ),
        grid=(steps,),
        in_specs=[
            pl.BlockSpec(memory_space=pltpu.SMEM),
            pl.BlockSpec((count, ROWS, depth // steps), lambda s: (0, 0, s)),
            pl.BlockSpec(d.shape, lambda s: (0, 0, 0)),
            pl.BlockSpec((2 * groups,) + term.shape[1:], lambda s: (s, 0, 0)),
        ],
        out_specs=(out, out),
        scratch_shapes=[pltpu.VMEM((groups, 2, block, width), F32)],
        compiler_params=pltpu.CompilerParams(vmem_limit_bytes=24 << 20),
    )(place, h, d, term)


def finish_kernel(got_ref, proj_ref, bil_ref):
    half = got_ref.shape[2]
    count = got_ref.shape[0] // 2
    for part in range(2):
        total = got_ref[part * count].astype(F32)
        for source in range(1, count):
            total += got_ref[part * count + source].astype(F32)
        columns = slice(part * half, (part + 1) * half)
        proj_ref[:, columns] = total[: proj_ref.shape[0]]
        bil_ref[:, columns] = total[proj_ref.shape[0] :]


def finish(got, rows, bil_rows):
    vmem = pl.BlockSpec(memory_space=pltpu.VMEM)
    width = 2 * got.shape[2]
    return pl.pallas_call(
        finish_kernel,
        out_shape=(
            jax.ShapeDtypeStruct((rows, width), F32),
            jax.ShapeDtypeStruct((bil_rows, width), F32),
        ),
        in_specs=[vmem],
        out_specs=(vmem, vmem),
        compiler_params=pltpu.CompilerParams(vmem_limit_bytes=16 << 20),
    )(got)


def pair_signs():
    table = np.zeros((PAIRS, CANDS * (CANDS - 1) // 2), np.float32)
    upper_i, upper_j = np.triu_indices(CANDS, 1)
    for k, (i, j) in enumerate(zip(upper_i, upper_j)):
        table[i * CANDS + j, k] = 1.0
        table[j * CANDS + i, k] = -1.0
    return table


def both(value, axis, dim):
    other = lax.ppermute(value, axis, [(0, 1), (1, 0)])
    first = lax.axis_index(axis) == 0
    return jnp.stack(
        [jnp.where(first, value, other), jnp.where(first, other, value)], axis=dim
    )


def around(value, axis):
    count = lax.axis_size(axis)
    return [value] + [
        lax.ppermute(value, axis, [(i, (i + k) % count) for i in range(count)])
        for k in range(1, count)
    ]


def gather_x(w):
    xh, xl = lax.axis_index("xh"), lax.axis_index("xl")
    half = w.shape[1] // 2
    keep = jnp.where(xh == 0, w[:, :half], w[:, half:])
    away = jnp.where(xh == 0, w[:, half:], w[:, :half])
    far, across, near = (
        lax.ppermute(value, ("xh", "xl"), [(i, i ^ flip) for i in range(4)])
        for value, flip in ((away, 2), (away, 3), (keep, 1))
    )
    same = jnp.where(xl == 0, jnp.stack([keep, near]), jnp.stack([near, keep]))
    cross = jnp.where(xl == 0, jnp.stack([far, across]), jnp.stack([across, far]))
    return jnp.where(xh == 0, jnp.stack([same, cross]), jnp.stack([cross, same]))


def body(hidden_states, proj_weight, bilinear, lengths, labels):
    xh, z, y, core = (lax.axis_index(axis) for axis in ("xh", "z", "y", "core"))
    lengths = lengths[0]
    w = gather_x(proj_weight)
    h = pack(hidden_states[0, 0], bilinear)
    h, w = lax.optimization_barrier((h, w))
    w = both(w, "core", 2)
    w = around(w.reshape(w.shape[:2] + (-1, w.shape[-1])), "y")
    h = lax.all_to_all(h.reshape((CANDS,) + h.shape[2:]), CAND, 0, 0)
    bil = both(h[:, ROWS : ROWS + bilinear.shape[0]], "core", 1)
    bil = both(bil.reshape(CANDS, -1, WIDTH), "xl", 0)
    bil = around(bil, "y")
    place = jnp.stack([xh, z, y, core])
    parts = lax.all_to_all(project(place, h, w), "z", 0, 0)
    x, xt, means, col, stat = forward(lengths, parts)
    means = lax.all_to_all(means, CAND, 0, 0)
    drows, logits, term = backward(lengths, place, means, bil, x, xt, col, stat, labels)
    drows = lax.all_to_all(drows, "z", 0, 0)
    term = term.reshape(-1, bilinear.shape[0], term.shape[1])
    mine, other = gradient(place, h, drows, term)
    other = lax.ppermute(other, "core", [(0, 1), (1, 0)])
    sent = (mine + other.astype(F32)).astype(BF)
    got = lax.all_to_all(sent, ("xh", "xl", "y"), 0, 0)
    grad_proj, grad_bil = finish(got, proj_weight.shape[0], bilinear.shape[0])
    return logits[None], grad_proj, grad_bil


def solution(mesh):
    parts = Mesh(mesh.devices.reshape(2, 4, 2, 4, 2), ("xh", "z", "xl", "y", "core"))
    in_specs = (
        P(PROMPT, CAND, None, None),
        P(CAND + PROMPT, None),
        P(CAND + PROMPT, None),
        P(PROMPT, None),
        P(PROMPT, None),
    )
    out_specs = (P(PROMPT, None, None), P(CAND + PROMPT, None), P(CAND + PROMPT, None))
    return jax.shard_map(body, mesh=parts, in_specs=in_specs, out_specs=out_specs, check_vma=False)
```

time: 170 us -> 151 us (0.89)
  blocking collectives: 80.9 us -> 32.9 us
  waiting for transfers between devices: 25 us -> 52.5 us
  starting transfers between devices: 11.5 us -> 33.7 us
  between operations: 14.2 us -> 0.86 us
  local copies, waits for them, and re-layouts: 11.8 us -> 7.3 us
  Pallas kernels: 23.9 us -> 21.8 us
    all_to_all x2 -> x1, blocking collectives: 67.6 us -> 17.5 us  [body(): got = lax.all_to_all(sent, ('xh', 'xl', 'y'), 0, 0)]
    ppermute x1 -> x13, waiting for transfers between devices: 0.43 us -> 23.3 us  [the longest x6 10.5 us: around(): lax.ppermute(value, axis, [(i, (i + k) % count) for i in range(count)])]
    ppermute x1 -> x13, starting transfers between devices: 3.19 us -> 16.8 us  [the longest x6 11.8 us: around(): lax.ppermute(value, axis, [(i, (i + k) % count) for i in range(count)])]
    all_to_all x1 -> x2, starting transfers between devices: 4.82 us -> 12 us  [the longest x1 7.61 us: body(): h = lax.all_to_all(h.reshape((CANDS,) + h.shape[2:]), CAND, 0, 0)]
    all_to_all x1, waiting for transfers between devices: 5.21 us -> 8.7 us  [body(): means = lax.all_to_all(means, CAND, 0, 0)]
    all_gather x1 -> x0, local copies, waits for them, and re-layouts: 3.15 us -> none  [body(): bil = lax.all_gather(h[:, ROWS:], PROMPT, axis=0)]
    unnamed x14 -> x18, local copies, waits for them, and re-layouts: 4.61 us -> 7.27 us
    all_to_all x1, blocking collectives: 13.3 us -> 15.4 us  [body(): drows = lax.all_to_all(drows, 'z', 0, 0)]
  transfers between devices with their start and end apart: 5 -> 16, of which waited for: 3 -> 10; matrix products, arithmetic and copies ran while one was open for 5% -> 0% of each run, Pallas kernels for 6% -> 5%
where the time goes in v2:
time: 151 us; the launch traced here: 150 us
  waiting for transfers between devices  52.5 us (35%)
  starting transfers between devices  33.7 us (22%)
  blocking collectives  32.9 us (22%)
  Pallas kernels  21.8 us (14%)
  local copies, waits for them, and re-layouts  7.3 us (5%)
    all_to_all x1, blocking collectives, body(): got = lax.all_to_all(sent, ('xh', 'xl', 'y'), 0, 0)  17.5 us
    all_to_all x1, blocking collectives, body(): drows = lax.all_to_all(drows, 'z', 0, 0)  15.4 us
    ppermute x6, starting transfers between devices, around(): lax.ppermute(value, axis, [(i, (i + k) % count) for i in range(count)])  11.8 us
    ppermute x6, waiting for transfers between devices, around(): lax.ppermute(value, axis, [(i, (i + k) % count) for i in range(count)])  10.5 us
    all_to_all x1, waiting for transfers between devices, body(): h = lax.all_to_all(h.reshape((CANDS,) + h.shape[2:]), CAND, 0, 0)  10.4 us
    ppermute x3, waiting for transfers between devices, both(): other = lax.ppermute(value, axis, [(0, 1), (1, 0)])  10.4 us
    all_to_all x1, waiting for transfers between devices, body(): parts = lax.all_to_all(project(place, h, w), 'z', 0, 0)  10.1 us
    all_to_all x1, waiting for transfers between devices, body(): means = lax.all_to_all(means, CAND, 0, 0)  8.7 us
  transfers between devices with their start and end apart: 16, of which 10 were waited for; matrix products, arithmetic and copies ran while one was open for 0% of the time, Pallas kernels for 5%

profile of v2, /device:TPU:0, one launch (start us, length us, event | category | flops | bytes accessed | tf_op | source)
XLA Modules:
  0.0 150.5 jit_solution(5068170682105804837)
XLA Ops:
  0.6 0.8 broadcast_select_fusion.1
  1.4 2.9 %collective-permute-start.2 = (bf16[32,512]{1,0:T(8,128)(2,1)S(1)}, bf16[32,512]{1,0:T(8,128)(2,1)S(1)}, u32[]{:S(2)}, u32[]{:S(2)}) collective-permute-start(bf16[32,512]{1,0:T(8,128)(2,1)S(1)} %get-tuple-element.38), channel_id=1, source_target_pairs={{0,72},{8,64},{64,8},{72,0},{1,73},{9,65},{65,9},{73,1},{2,74},{10... | collective-permute-start | bytes 98312 | tf_op jit(solution)/shard_map/ppermute | solution.py:444
  4.3 0.8 collective-permute-start.1
  5.1 0.5 collective-permute-start
  5.6 0.0 copy-start.2
  5.6 1.2 copy-done.2
  6.8 0.0 copy-start.6
  6.8 0.7 copy-done.6
  7.5 0.5 shard_map.85
  8.1 0.0 copy-start
  8.1 1.4 copy-done
  9.5 0.0 collective-permute-done.2
  9.5 0.3 collective-permute-done.1
  9.8 0.0 collective-permute-done
  9.8 7.6 %all-to-all-start = ((bf16[8,144,1024]{2,1,0:T(8,128)(2,1)}), bf16[8,144,1024]{2,1,0:T(8,128)(2,1)S(1)}, u32[]{:S(2)}, u32[]{:S(2)}) async-start(bf16[8,144,1024]{2,1,0:T(8,128)(2,1)} %bitcast.32), calls=%async_computation | async-start | bytes 4718592 | tf_op jit(solution)/shard_map/all_to_all | solution.py:460
  17.4 0.0 collective-permute-start.3
  17.4 1.3 collective-permute-done.3
  18.9 1.6 %collective-permute-start.4 = (bf16[2,2,64,512]{3,2,1,0:T(8,128)(2,1)S(1)}, bf16[2,2,64,512]{3,2,1,0:T(8,128)(2,1)S(1)}, u32[]{:S(2)}, u32[]{:S(2)}) collective-permute-start(bf16[2,2,64,512]{3,2,1,0:T(8,128)(2,1)S(1)} %bitcast.35), channel_id=1, source_target_pairs={{0,2},{2,4},{4,6},{6,0},{1,3},{3,5},{5,7},{7,1},{8,10},{10,12},{12... | collective-permute-start | bytes 786440 | tf_op jit(solution)/shard_map/ppermute | solution.py:433
  20.5 2.9 %collective-permute-start.5 = (bf16[2,2,64,512]{3,2,1,0:T(8,128)(2,1)S(1)}, bf16[2,2,64,512]{3,2,1,0:T(8,128)(2,1)S(1)}, u32[]{:S(2)}, u32[]{:S(2)}) collective-permute-start(bf16[2,2,64,512]{3,2,1,0:T(8,128)(2,1)S(1)} %bitcast.36), channel_id=1, source_target_pairs={{0,4},{2,6},{4,0},{6,2},{1,5},{3,7},{5,1},{7,3},{8,12},{10,14},{12... | collective-permute-start | bytes 786440 | tf_op jit(solution)/shard_map/ppermute | solution.py:433
  23.4 1.3 collective-permute-start.6
  24.8 0.1 pad_add_fusion.place_ref
  24.8 3.7 %collective-permute-done.4.refs_1_ = bf16[2,2,64,512]{3,2,1,0:T(8,128)(2,1)S(1)} collective-permute-done((bf16[2,2,64,512]{3,2,1,0:T(8,128)(2,1)S(1)}, bf16[2,2,64,512]{3,2,1,0:T(8,128)(2,1)S(1)}, u32[]{:S(2)}, u32[]{:S(2)}) %collective-permute-start.4) | collective-permute-done | bytes 262176 | tf_op jit(solution)/shard_map/ppermute | solution.py:433
  28.6 6.8 %collective-permute-done.5.refs_2_ = bf16[2,2,64,512]{3,2,1,0:T(8,128)(2,1)S(1)} collective-permute-done((bf16[2,2,64,512]{3,2,1,0:T(8,128)(2,1)S(1)}, bf16[2,2,64,512]{3,2,1,0:T(8,128)(2,1)S(1)}, u32[]{:S(2)}, u32[]{:S(2)}) %collective-permute-start.5) | collective-permute-done | bytes 262176 | tf_op jit(solution)/shard_map/ppermute | solution.py:433
  35.4 0.0 collective-permute-done.6.refs_3_
  35.4 10.4 %all-to-all-done.h_ref = bf16[8,144,1024]{2,1,0:T(8,128)(2,1)S(1)} async-done(((bf16[8,144,1024]{2,1,0:T(8,128)(2,1)}), bf16[8,144,1024]{2,1,0:T(8,128)(2,1)S(1)}, u32[]{:S(2)}, u32[]{:S(2)}) %all-to-all-start) | async-done | bytes 2359328 | tf_op jit(solution)/shard_map/all_to_all | solution.py:460
  45.8 2.7 %shard_map.86 = f32[4,1024,128]{2,1,0:T(8,128)S(1)} custom-call(s32[4]{0:T(128)S(1)} %pad_add_fusion.place_ref, bf16[8,144,1024]{2,1,0:T(8,128)(2,1)S(1)} %all-to-all-done.h_ref, bf16[2,2,64,512]{3,2,1,0:T(8,128)(2,1)S(1)} %bitcast.38, bf16[2,2,64,512]{3,2,1,0:T(8,128)(2,1)S(1)} %collective-permute-done.4.refs_1_, ...), custom_call_target="tpu_custom_call" | custom-call | tf_op jit(solution)/shard_map/pallas_call | solution.py:92
  48.5 0.0 copy-start.1
  48.5 1.3 copy-done.1
  49.8 4.4 %all-to-all-start.1 = ((f32[4,1024,128]{2,1,0:T(8,128)}), f32[4,1024,128]{2,1,0:T(8,128)}, u32[]{:S(2)}, u32[]{:S(2)}) async-start(f32[4,1024,128]{2,1,0:T(8,128)} %copy-done.1), calls=%async_computation.1 | async-start | bytes 4194304 | tf_op jit(solution)/shard_map/all_to_all | solution.py:465
  54.3 0.0 copy-start.7
  54.3 0.1 collective-permute-start.7
  54.4 1.3 collective-permute-done.7
  55.8 0.7 collective-permute-start.8
  56.5 7.8 %collective-permute-done.8 = bf16[8,16,1024]{2,1,0:T(8,128)(2,1)S(1)} collective-permute-done((bf16[8,16,1024]{2,1,0:T(8,128)(2,1)S(1)}, bf16[8,16,1024]{2,1,0:T(8,128)(2,1)S(1)}, u32[]{:S(2)}, u32[]{:S(2)}) %collective-permute-start.8) | collective-permute-done | bytes 262176 | tf_op jit(solution)/shard_map/ppermute | solution.py:423
  64.2 0.1 select_bitcast_fusion.1
  64.4 0.0 copy-start.8
  64.4 0.1 pad_maximum_fusion.bil0_ref
  64.4 1.6 %collective-permute-start.9 = (bf16[2,8,16,1024]{3,2,1,0:T(8,128)(2,1)S(1)}, bf16[2,8,16,1024]{3,2,1,0:T(8,128)(2,1)}, u32[]{:S(2)}, u32[]{:S(2)}) collective-permute-start(bf16[2,8,16,1024]{3,2,1,0:T(8,128)(2,1)S(1)} %pad_maximum_fusion.bil0_ref), channel_id=1, source_target_pairs={{0,2},{2,4},{4,6},{6,0},{1,3},{3,5},{5,7},{7,1},{8,10},{10,12},{12... | collective-permute-start | bytes 1572872 | tf_op jit(solution)/shard_map/ppermute | solution.py:433
  66.1 2.9 %collective-permute-start.10 = (bf16[2,8,16,1024]{3,2,1,0:T(8,128)(2,1)S(1)}, bf16[2,8,16,1024]{3,2,1,0:T(8,128)(2,1)}, u32[]{:S(2)}, u32[]{:S(2)}) collective-permute-start(bf16[2,8,16,1024]{3,2,1,0:T(8,128)(2,1)S(1)} %pad_maximum_fusion.bil0_ref), channel_id=1, source_target_pairs={{0,4},{2,6},{4,0},{6,2},{1,5},{3,7},{5,1},{7,3},{8,12},{10,14},{12... | collective-permute-start | bytes 1572872 | tf_op jit(solution)/shard_map/ppermute | solution.py:433
  69.0 1.3 collective-permute-start.11
  70.3 10.1 %all-to-all-done.1.p_ref = f32[4,1024,128]{2,1,0:T(8,128)} async-done(((f32[4,1024,128]{2,1,0:T(8,128)}), f32[4,1024,128]{2,1,0:T(8,128)}, u32[]{:S(2)}, u32[]{:S(2)}) %all-to-all-start.1) | async-done | bytes 2097184 | tf_op jit(solution)/shard_map/all_to_all | solution.py:465
  80.4 0.0 copy-done.7
  80.4 6.9 %shard_map.87 = (bf16[1024,256]{1,0:T(8,128)(2,1)S(1)}, bf16[128,1024]{1,0:T(8,128)(2,1)S(1)}, f32[8,64,128]{2,1,0:T(8,128)}, f32[2,8,1024]{2,1,0:T(8,128)S(1)}, f32[64,256]{1,0:T(8,128)S(1)}) custom-call(s32[8]{0:T(128)S(1)} %bitcast.40, f32[4,1024,128]{2,1,0:T(8,128)} %all-to-all-done.1.p_ref), custom_call_target="tpu_custom_call" | custom-call | tf_op jit(solution)/shard_map/pallas_call | solution.py:186
  87.4 0.0 copy-start.3
  87.4 0.8 copy-done.3
  88.1 4.9 %all-to-all-start.2 = ((f32[8,64,128]{2,1,0:T(8,128)}), f32[8,64,128]{2,1,0:T(8,128)S(1)}, u32[]{:S(2)}, u32[]{:S(2)}) async-start(f32[8,64,128]{2,1,0:T(8,128)} %get-tuple-element.19), calls=%async_computation.2 | async-start | bytes 524288 | tf_op jit(solution)/shard_map/all_to_all | solution.py:467
  93.0 0.0 collective-permute-done.9.bil1_ref
  93.0 0.0 collective-permute-done.10.bil2_ref
  93.0 0.0 collective-permute-done.11.bil3_ref
  93.0 8.7 %all-to-all-done.2.mean_ref = f32[8,64,128]{2,1,0:T(8,128)S(1)} async-done(((f32[8,64,128]{2,1,0:T(8,128)}), f32[8,64,128]{2,1,0:T(8,128)S(1)}, u32[]{:S(2)}, u32[]{:S(2)}) %all-to-all-start.2) | async-done | bytes 262176 | tf_op jit(solution)/shard_map/all_to_all | solution.py:467
  101.7 0.0 copy-done.8
  101.7 0.0 copy-start.4
  101.7 1.0 copy-done.4
  102.8 0.0 copy-start.5
  102.8 0.8 copy-done.5
  103.5 8.0 %shard_map.88 = (bf16[4,1024,128]{2,1,0:T(8,128)(2,1)S(1)}, f32[8,8]{1,0:T(8,128)}, f32[256,512]{1,0:T(8,128)S(1)}) custom-call(s32[8]{0:T(128)S(1)} %bitcast.41, s32[4]{0:T(128)S(1)} %pad_add_fusion.place_ref, f32[8,64,128]{2,1,0:T(8,128)S(1)} %all-to-all-done.2.mean_ref, bf16[2,8,16,1024]{3,2,1,0:T(8,128)(2,1)S(1)} %pad_maximum_fusion.bil0_ref, ...), custom_call_target="tpu_custom_call" | custom-call | tf_op jit(solution)/shard_map/pallas_call | solution.py:327
  111.5 15.4 %all_to_all.25.d_ref = bf16[4,1024,128]{2,1,0:T(8,128)(2,1)S(1)} all-to-all(bf16[4,1024,128]{2,1,0:T(8,128)(2,1)S(1)} %get-tuple-element.25), channel_id=1, replica_groups=mesh['xh'=2,'z'=4,'xl'=2,'y'=4,'core'=2] {'z'}, dimensions={0} | all-to-all | bytes 2097152 | tf_op jit(solution)/shard_map/all_to_all | solution.py:469
  127.0 2.8 %shard_map.89 = (f32[16,40,512]{2,1,0:T(8,128)S(1)}, bf16[16,40,512]{2,1,0:T(8,128)(2,1)S(1)}) custom-call(s32[4]{0:T(128)S(1)} %pad_add_fusion.place_ref, bf16[8,144,1024]{2,1,0:T(8,128)(2,1)S(1)} %all-to-all-done.h_ref, bf16[4,1024,128]{2,1,0:T(8,128)(2,1)S(1)} %all_to_all.25.d_ref, f32[32,8,512]{2,1,0:T(8,128)S(1)} %bitcast.39), custom_call_target="tpu_custom_call" | custom-call | tf_op jit(solution)/shard_map/pallas_call | solution.py:367
  129.8 0.1 collective-permute-start.12
  129.9 2.1 %collective-permute-done.12 = bf16[16,40,512]{2,1,0:T(8,128)(2,1)S(1)} collective-permute-done((bf16[16,40,512]{2,1,0:T(8,128)(2,1)S(1)}, bf16[16,40,512]{2,1,0:T(8,128)(2,1)S(1)}, u32[]{:S(2)}, u32[]{:S(2)}) %collective-permute-start.12) | collective-permute-done | bytes 655392 | tf_op jit(solution)/shard_map/ppermute | solution.py:472
  132.0 0.2 add_convert_fusion
  132.2 17.5 %all_to_all.26.got_ref = bf16[16,40,512]{2,1,0:T(8,128)(2,1)S(1)} all-to-all(bf16[16,40,512]{2,1,0:T(8,128)(2,1)S(1)} %add_convert_fusion), channel_id=1, replica_groups=mesh['xh'=2,'z'=4,'xl'=2,'y'=4,'core'=2] {'xh','xl','y'}, dimensions={0} | all-to-all | bytes 1310720 | tf_op jit(solution)/shard_map/all_to_all | solution.py:474
  149.7 0.7 shard_map.90
  (9 shorter events, 0.2 us)
Async XLA Ops:
  1.4 8.1 %collective-permute-start.2 = (bf16[32,512]{1,0:T(8,128)(2,1)S(1)}, bf16[32,512]{1,0:T(8,128)(2,1)S(1)}, u32[]{:S(2)}, u32[]{:S(2)}) collective-permute-start(bf16[32,512]{1,0:T(8,128)(2,1)S(1)} %get-tuple-element.38), channel_id=1, source_target_pairs={{0,72},{8,64},{64,8},{72,0},{1,73},{9,65},{65,9},{73,1},{2,74},{10... | collective-permute-start | bytes 98312 | tf_op jit(solution)/shard_map/ppermute | solution.py:444
  4.3 5.4 %collective-permute-start.1 = (bf16[32,512]{1,0:T(8,128)(2,1)S(1)}, bf16[32,512]{1,0:T(8,128)(2,1)S(1)}, u32[]{:S(2)}, u32[]{:S(2)}) collective-permute-start(bf16[32,512]{1,0:T(8,128)(2,1)S(1)} %get-tuple-element.38), channel_id=1, source_target_pairs={{0,64},{8,72},{64,0},{72,8},{1,65},{9,73},{65,1},{73,9},{2,66},{10... | collective-permute-start | bytes 98312 | tf_op jit(solution)/shard_map/ppermute | solution.py:444
  5.1 4.6 %collective-permute-start = (bf16[32,512]{1,0:T(8,128)(2,1)S(1)}, bf16[32,512]{1,0:T(8,128)(2,1)S(1)}, u32[]{:S(2)}, u32[]{:S(2)}) collective-permute-start(bf16[32,512]{1,0:T(8,128)(2,1)S(1)} %get-tuple-element.37), channel_id=1, source_target_pairs={{0,8},{8,0},{64,72},{72,64},{1,9},{9,1},{65,73},{73,65},{2,10},{10... | collective-permute-start | bytes 98312 | tf_op jit(solution)/shard_map/ppermute | solution.py:444
  5.6 1.2 copy-start.2
  6.8 0.7 copy-start.6
  8.1 1.4 copy-start
  9.8 36.0 %all-to-all-start = ((bf16[8,144,1024]{2,1,0:T(8,128)(2,1)}), bf16[8,144,1024]{2,1,0:T(8,128)(2,1)S(1)}, u32[]{:S(2)}, u32[]{:S(2)}) async-start(bf16[8,144,1024]{2,1,0:T(8,128)(2,1)} %bitcast.32), calls=%async_computation | async-start | bytes 4718592 | tf_op jit(solution)/shard_map/all_to_all | solution.py:460
  17.4 1.3 collective-permute-start.3
  18.9 9.7 %collective-permute-start.4 = (bf16[2,2,64,512]{3,2,1,0:T(8,128)(2,1)S(1)}, bf16[2,2,64,512]{3,2,1,0:T(8,128)(2,1)S(1)}, u32[]{:S(2)}, u32[]{:S(2)}) collective-permute-start(bf16[2,2,64,512]{3,2,1,0:T(8,128)(2,1)S(1)} %bitcast.35), channel_id=1, source_target_pairs={{0,2},{2,4},{4,6},{6,0},{1,3},{3,5},{5,7},{7,1},{8,10},{10,12},{12... | collective-permute-start | bytes 786440 | tf_op jit(solution)/shard_map/ppermute | solution.py:433
  20.5 14.9 %collective-permute-start.5 = (bf16[2,2,64,512]{3,2,1,0:T(8,128)(2,1)S(1)}, bf16[2,2,64,512]{3,2,1,0:T(8,128)(2,1)S(1)}, u32[]{:S(2)}, u32[]{:S(2)}) collective-permute-start(bf16[2,2,64,512]{3,2,1,0:T(8,128)(2,1)S(1)} %bitcast.36), channel_id=1, source_target_pairs={{0,4},{2,6},{4,0},{6,2},{1,5},{3,7},{5,1},{7,3},{8,12},{10,14},{12... | collective-permute-start | bytes 786440 | tf_op jit(solution)/shard_map/ppermute | solution.py:433
  23.4 12.0 %collective-permute-start.6 = (bf16[2,2,64,512]{3,2,1,0:T(8,128)(2,1)S(1)}, bf16[2,2,64,512]{3,2,1,0:T(8,128)(2,1)S(1)}, u32[]{:S(2)}, u32[]{:S(2)}) collective-permute-start(bf16[2,2,64,512]{3,2,1,0:T(8,128)(2,1)S(1)} %bitcast.37), channel_id=1, source_target_pairs={{0,6},{2,0},{4,2},{6,4},{1,7},{3,1},{5,3},{7,5},{8,14},{10,8},{12,... | collective-permute-start | bytes 786440 | tf_op jit(solution)/shard_map/ppermute | solution.py:433
  48.5 1.3 copy-start.1
  49.8 30.6 %all-to-all-start.1 = ((f32[4,1024,128]{2,1,0:T(8,128)}), f32[4,1024,128]{2,1,0:T(8,128)}, u32[]{:S(2)}, u32[]{:S(2)}) async-start(f32[4,1024,128]{2,1,0:T(8,128)} %copy-done.1), calls=%async_computation.1 | async-start | bytes 4194304 | tf_op jit(solution)/shard_map/all_to_all | solution.py:465
  54.3 26.1 %copy-start.7 = (s32[1,8]{1,0:T(1,128)S(1)}, s32[1,8]{1,0:T(1,128)}, u32[]{:S(2)}) copy-start(s32[1,8]{1,0:T(1,128)} %param.9) | copy-start | bytes 100
  54.3 1.4 collective-permute-start.7
  55.8 8.4 %collective-permute-start.8 = (bf16[8,16,1024]{2,1,0:T(8,128)(2,1)S(1)}, bf16[8,16,1024]{2,1,0:T(8,128)(2,1)S(1)}, u32[]{:S(2)}, u32[]{:S(2)}) collective-permute-start(bf16[8,16,1024]{2,1,0:T(8,128)(2,1)S(1)} %copy_bitcast_fusion), channel_id=1, source_target_pairs={{0,8},{8,0},{1,9},{9,1},{2,10},{10,2},{3,11},{11,3},{4,12},{12,4},... | collective-permute-start | bytes 786440 | tf_op jit(solution)/shard_map/ppermute | solution.py:423
  64.4 37.4 %copy-start.8 = (s32[1,28]{1,0:T(1,128)S(1)}, s32[1,28]{1,0:T(1,128)}, u32[]{:S(2)}) copy-start(s32[1,28]{1,0:T(1,128)} %label_ref.1) | copy-start | bytes 340
  64.4 28.6 %collective-permute-start.9 = (bf16[2,8,16,1024]{3,2,1,0:T(8,128)(2,1)S(1)}, bf16[2,8,16,1024]{3,2,1,0:T(8,128)(2,1)}, u32[]{:S(2)}, u32[]{:S(2)}) collective-permute-start(bf16[2,8,16,1024]{3,2,1,0:T(8,128)(2,1)S(1)} %pad_maximum_fusion.bil0_ref), channel_id=1, source_target_pairs={{0,2},{2,4},{4,6},{6,0},{1,3},{3,5},{5,7},{7,1},{8,10},{10,12},{12... | collective-permute-start | bytes 1572872 | tf_op jit(solution)/shard_map/ppermute | solution.py:433
  66.1 26.9 %collective-permute-start.10 = (bf16[2,8,16,1024]{3,2,1,0:T(8,128)(2,1)S(1)}, bf16[2,8,16,1024]{3,2,1,0:T(8,128)(2,1)}, u32[]{:S(2)}, u32[]{:S(2)}) collective-permute-start(bf16[2,8,16,1024]{3,2,1,0:T(8,128)(2,1)S(1)} %pad_maximum_fusion.bil0_ref), channel_id=1, source_target_pairs={{0,4},{2,6},{4,0},{6,2},{1,5},{3,7},{5,1},{7,3},{8,12},{10,14},{12... | collective-permute-start | bytes 1572872 | tf_op jit(solution)/shard_map/ppermute | solution.py:433
  69.0 24.0 %collective-permute-start.11 = (bf16[2,8,16,1024]{3,2,1,0:T(8,128)(2,1)S(1)}, bf16[2,8,16,1024]{3,2,1,0:T(8,128)(2,1)}, u32[]{:S(2)}, u32[]{:S(2)}) collective-permute-start(bf16[2,8,16,1024]{3,2,1,0:T(8,128)(2,1)S(1)} %pad_maximum_fusion.bil0_ref), channel_id=1, source_target_pairs={{0,6},{2,0},{4,2},{6,4},{1,7},{3,1},{5,3},{7,5},{8,14},{10,8},{12,... | collective-permute-start | bytes 1572872 | tf_op jit(solution)/shard_map/ppermute | solution.py:433
  87.4 0.8 copy-start.3
  88.1 13.6 %all-to-all-start.2 = ((f32[8,64,128]{2,1,0:T(8,128)}), f32[8,64,128]{2,1,0:T(8,128)S(1)}, u32[]{:S(2)}, u32[]{:S(2)}) async-start(f32[8,64,128]{2,1,0:T(8,128)} %get-tuple-element.19), calls=%async_computation.2 | async-start | bytes 524288 | tf_op jit(solution)/shard_map/all_to_all | solution.py:467
  101.7 1.0 copy-start.4
  102.8 0.8 copy-start.5
  129.8 2.2 %collective-permute-start.12 = (bf16[16,40,512]{2,1,0:T(8,128)(2,1)S(1)}, bf16[16,40,512]{2,1,0:T(8,128)(2,1)S(1)}, u32[]{:S(2)}, u32[]{:S(2)}) collective-permute-start(bf16[16,40,512]{2,1,0:T(8,128)(2,1)S(1)} %get-tuple-element.28), channel_id=1, source_target_pairs={{0,1},{1,0},{2,3},{3,2},{4,5},{5,4},{6,7},{7,6},{8,9},{9,8},{10,11... | collective-permute-start | bytes 1966088 | tf_op jit(solution)/shard_map/ppermute | solution.py:472

commit v3 on v2

--- a/solution.py
+++ b/solution.py
@@ -1,6 +1,5 @@
 import jax
 import jax.numpy as jnp
-import numpy as np
 from jax import lax
 from jax.experimental import pallas as pl
 from jax.experimental.pallas import tpu as pltpu
@@ -15,6 +14,7 @@
 PAIRS = CANDS * CANDS
 EPSILON = 1e-06
 FAR = 1e30
+SCALE = 64.0
 HIGH = lax.Precision.HIGHEST
 BF = jnp.bfloat16
 F32 = jnp.float32
@@ -55,6 +55,8 @@
     quarter = CANDS // 2
     half = hidden.shape[1] // CANDS
     rows = ROWS + 2 * bil.shape[0]
+    hidden = pltpu.with_memory_space_constraint(hidden, pltpu.HBM)
+    bil = pltpu.with_memory_space_constraint(bil, pltpu.HBM)
     return pl.pallas_call(
         pack_kernel,
         out_shape=jax.ShapeDtypeStruct((2, quarter, rows, 2 * half), BF),
@@ -70,7 +72,7 @@
 
 
 def project_kernel(place_ref, h_ref, *refs):
-    pieces, out_ref, w_scr = refs[:-2], refs[-2], refs[-1]
+    pieces, (out_ref, w_scr) = refs[:-2], refs[-2:]
     count = len(pieces)
 
     @pl.when(pl.program_id(0) == 0)
@@ -88,6 +90,7 @@
     steps = 4
     per = CANDS // steps
     shape = pieces[0].shape
+    depth = h.shape[2]
     dests = shape[3] // SLICE
     return pl.pallas_call(
         project_kernel,
@@ -95,7 +98,7 @@
         grid=(steps,),
         in_specs=[
             pl.BlockSpec(memory_space=pltpu.SMEM),
-            pl.BlockSpec((per, ROWS, h.shape[2]), lambda s: (s, 0, 0)),
+            pl.BlockSpec((per, ROWS, depth), lambda s: (s, 0, 0)),
         ]
         + [pl.BlockSpec(shape, lambda s: (0, 0, 0, 0))] * len(pieces),
         out_specs=pl.BlockSpec((dests, per * ROWS, SLICE), lambda s: (0, s, 0)),
@@ -133,18 +136,17 @@
     return jnp.concatenate([top, bottom, extra, jnp.zeros((SLICE - 4 * CANDS, wide), BF)], axis=0)
 
 
-def forward_kernel(len_ref, p_ref, x_ref, xt_ref, mean_ref, col_ref, stat_ref, e_scr, m_scr, l_scr):
-    total = p_ref[0]
-    for source in range(1, p_ref.shape[0]):
-        total += p_ref[source]
-    total = total.astype(BF)
-    x_ref[...] = extend(total, len_ref)
-    xt_ref[...] = total.T
+def forward_kernel(
+    len_ref, x_ref, xt_ref, mean_ref, col_ref, stat_ref, e_scr, m_scr, l_scr, key_scr
+):
+    x = x_ref[...]
+    key_scr[...] = extend(x, len_ref)
+    xt_ref[...] = x.T
     wide = 2 * ROWS
     for i in range(CANDS):
         weights = head_weights(xt_ref, i)
         for j in range(CANDS):
-            s = mm(x_ref[j * ROWS : (j + 1) * ROWS, :], weights)
+            s = mm(key_scr[j * ROWS : (j + 1) * ROWS, :], weights)
             m = jnp.max(s, axis=0, keepdims=True)
             e = jnp.exp(s - m)
             e_scr[i, j * ROWS : (j + 1) * ROWS, :] = e.astype(BF)
@@ -172,7 +174,7 @@
         col_ref[1, i : i + 1, :] = jnp.sum(c1, axis=0, keepdims=True)
         c0h, c0l = split(c0)
         c1h, c1l = split(c1)
-        means = mm(jnp.concatenate([c0h, c0l, c1h, c1l], axis=0), x_ref[:, :SLICE])
+        means = mm(jnp.concatenate([c0h, c0l, c1h, c1l], axis=0), x_ref[...])
         means = jnp.where(
             lanes((CANDS, SLICE)) < HEAD_DIM, means[0:8] + means[8:16], means[16:24] + means[24:32]
         )
@@ -180,40 +182,41 @@
             mean_ref[dest, i * CANDS : (i + 1) * CANDS, :] = means
 
 
-def forward(lengths, parts):
+def forward(lengths, x):
     rows = CANDS * ROWS
     vmem = pl.BlockSpec(memory_space=pltpu.VMEM)
     return pl.pallas_call(
         forward_kernel,
         out_shape=(
-            jax.ShapeDtypeStruct((rows, 2 * SLICE), BF),
             jax.ShapeDtypeStruct((SLICE, rows), BF),
             jax.ShapeDtypeStruct((CANDS, PAIRS, SLICE), F32),
             jax.ShapeDtypeStruct((2, CANDS, rows), F32),
             jax.ShapeDtypeStruct((PAIRS, 2 * ROWS), F32),
         ),
         in_specs=[pl.BlockSpec(memory_space=pltpu.SMEM), vmem],
-        out_specs=(vmem,) * 5,
+        out_specs=(vmem,) * 4,
         scratch_shapes=[
             pltpu.VMEM((CANDS, rows, 2 * ROWS), BF),
             pltpu.VMEM((CANDS, CANDS, 2 * ROWS), F32),
             pltpu.VMEM((CANDS, CANDS, 2 * ROWS), F32),
+            pltpu.VMEM((rows, 2 * SLICE), BF),
         ],
+        cost_estimate=pl.CostEstimate(flops=12 << 30, bytes_accessed=16 << 20, transcendentals=2 << 20),
         compiler_params=pltpu.CompilerParams(vmem_limit_bytes=24 << 20),
-    )(lengths, parts)
-
-
-def backward_kernel(
-    len_ref, place_ref, mean_ref, bil0_ref, bil1_ref, bil2_ref, bil3_ref,
-    x_ref, xt_ref, col_ref, stat_ref, sign_ref, label_ref,
-    dr_ref, logit_ref, term_ref,
-    d_scr, along_scr, grad_scr, bil_scr,
-):
-    xh, z, y = place_ref[0], place_ref[1], place_ref[2]
-    pieces = (bil0_ref, bil1_ref, bil2_ref, bil3_ref)
-    for k, piece in enumerate(pieces):
-        for part in range(2):
-            bil_scr[:, part, lax.rem(y + len(pieces) - k, len(pieces))] = piece[part]
+    )(lengths, x)
+
+
+def backward_kernel(len_ref, place_ref, mean_ref, x_ref, xt_ref, col_ref, stat_ref, label_ref, *refs):
+    bil_refs, refs = refs[:CANDS], refs[CANDS:]
+    dr_ref, logit_ref, term_ref, d_scr, along_scr, grad_scr, key_scr, bil_scr = refs
+    xh, z, y, core = place_ref[0], place_ref[1], place_ref[2], place_ref[3]
+    count, half = len(bil_refs) // 2, WIDTH // 2
+    for k in range(count):
+        for piece, side in ((bil_refs[k], core), (bil_refs[count + k], 1 - core)):
+            columns = pl.ds(pl.multiple_of(side * half, half), half)
+            for part in range(2):
+                bil_scr[:, part, lax.rem(y + count - k, count), :, columns] = piece[part]
+    key_scr[...] = extend(x_ref[...], len_ref)
     here = xh * (CANDS // 2) + z
     means = jnp.concatenate([mean_ref[c] for c in range(CANDS)], axis=1)
     radius = jnp.sqrt(jnp.mean(means * means, axis=1, keepdims=True) + EPSILON)
@@ -230,7 +233,13 @@
     index = sublanes((PAIRS, 1))
     off = index // CANDS != index % CANDS
     logit = jnp.where(off, logit, 0.0)
-    sign = jnp.sum(sign_ref[...] * (2.0 * label_ref[...].astype(F32) - 1.0), axis=1, keepdims=True)
+    labels = label_ref[...]
+    shape = (PAIRS, labels.shape[1])
+    left, right = sublanes(shape) // CANDS, sublanes(shape) % CANDS
+    low, high = jnp.minimum(left, right), jnp.maximum(left, right)
+    spot = low * (2 * CANDS - 1 - low) // 2 + high - low - 1
+    wins = (2.0 * labels.astype(F32) - 1.0) * jnp.where(left < right, 1.0, -1.0)
+    sign = jnp.sum(jnp.where(spot == lanes(shape), wins, 0.0), axis=1, keepdims=True)
     dlogit = jnp.where(off, -sign * jax.nn.sigmoid(-sign * logit), 0.0)
     pick = lanes((PAIRS, SLICE))
     swapped = mm(
@@ -257,7 +266,6 @@
     dpooled = dlogit * own_toward + dlogit_rev * back
     inner = (dlogit * logit + dlogit_rev * logit_rev) * (1.0 / WIDTH)
     dmeans = (dpooled - own_pooled * inner) / radius
-    half = WIDTH // 2
     low_rows = jnp.concatenate(
         [mean_ref[z] / radius, mean_ref[z + CANDS // 2] / radius], axis=1
     ) * dlogit
@@ -274,7 +282,7 @@
     turned = jnp.concatenate([col_high, col - col_high, col_high], axis=0).T.astype(BF)
     for j in range(CANDS):
         rows = slice(j * ROWS, (j + 1) * ROWS)
-        x = x_ref[rows, :SLICE]
+        x = x_ref[rows, :]
         of_j = dmeans_rev[j * CANDS : (j + 1) * CANDS]
         heads = jnp.concatenate(
             [jnp.where(lane8 < HEAD_DIM, of_j, 0.0), jnp.where(lane8 < HEAD_DIM, 0.0, of_j)], axis=0
@@ -301,12 +309,12 @@
         ).astype(BF)
         for j in range(CANDS):
             rows = slice(j * ROWS, (j + 1) * ROWS)
-            p = jnp.exp(mm(x_ref[rows, :], weights))
+            p = jnp.exp(mm(key_scr[rows, :], weights))
             along = mm(along_scr[rows, :], chosen)
             expected = jnp.sum(p * along, axis=0, keepdims=True) * scale
             d_scr[i, rows, :] = (p * (along - expected)).astype(BF)
         lane = lanes((ROWS, SLICE))
-        own = x_ref[i * ROWS : (i + 1) * ROWS, :SLICE]
+        own = x_ref[i * ROWS : (i + 1) * ROWS, :]
         zero = jnp.zeros_like(own)
         heads = jnp.concatenate(
             [jnp.where(lane < HEAD_DIM, own, zero), jnp.where(lane < HEAD_DIM, zero, own)], axis=0
@@ -331,16 +339,17 @@
             jax.ShapeDtypeStruct((CANDS, CANDS), F32),
             jax.ShapeDtypeStruct((2 * SLICE, WIDTH // 2), F32),
         ),
-        in_specs=[smem, smem] + [vmem] * (7 + len(bil)),
+        in_specs=[smem, smem] + [vmem] * (6 + len(bil)),
         out_specs=(vmem,) * 3,
         scratch_shapes=[
             pltpu.VMEM((CANDS, rows, 2 * ROWS), BF),
             pltpu.VMEM((rows, 4 * CANDS), BF),
             pltpu.VMEM((rows, SLICE), F32),
-            pltpu.VMEM((CANDS, 2, len(bil)) + bil[0].shape[2:], BF),
+            pltpu.VMEM((rows, 2 * SLICE), BF),
+            pltpu.VMEM((CANDS, 2, len(bil) // 2, 2 * CANDS, WIDTH), BF),
         ],
         compiler_params=pltpu.CompilerParams(vmem_limit_bytes=32 << 20),
-    )(lengths, place, means, *bil, x, xt, col, stat, pair_signs(), labels)
+    )(lengths, place, means, x, xt, col, stat, labels, *bil)
 
 
 def gradient_kernel(place_ref, h_ref, d_ref, term_ref, mine_ref, other_ref, scr):
@@ -410,15 +419,6 @@
     )(got)
 
 
-def pair_signs():
-    table = np.zeros((PAIRS, CANDS * (CANDS - 1) // 2), np.float32)
-    upper_i, upper_j = np.triu_indices(CANDS, 1)
-    for k, (i, j) in enumerate(zip(upper_i, upper_j)):
-        table[i * CANDS + j, k] = 1.0
-        table[j * CANDS + i, k] = -1.0
-    return table
-
-
 def both(value, axis, dim):
     other = lax.ppermute(value, axis, [(0, 1), (1, 0)])
     first = lax.axis_index(axis) == 0
@@ -449,8 +449,19 @@
     return jnp.where(xh == 0, jnp.stack([same, cross]), jnp.stack([cross, same]))
 
 
+def gather_half(bil):
+    core = lax.axis_index("core")
+    half = bil.shape[2] // 2
+    keep = jnp.where(core == 0, bil[:, :, :half], bil[:, :, half:])
+    away = jnp.where(core == 0, bil[:, :, half:], bil[:, :, :half])
+    other = lax.ppermute(away, "core", [(0, 1), (1, 0)])
+    pair = [jnp.where(core == 0, keep, other), jnp.where(core == 0, other, keep)]
+    return both(jnp.stack(pair, axis=1).reshape(bil.shape[0], -1, half), "xl", 0)
+
+
 def body(hidden_states, proj_weight, bilinear, lengths, labels):
     xh, z, y, core = (lax.axis_index(axis) for axis in ("xh", "z", "y", "core"))
+    place = jnp.stack([xh, z, y, core])
     lengths = lengths[0]
     w = gather_x(proj_weight)
     h = pack(hidden_states[0, 0], bilinear)
@@ -458,12 +469,13 @@
     w = both(w, "core", 2)
     w = around(w.reshape(w.shape[:2] + (-1, w.shape[-1])), "y")
     h = lax.all_to_all(h.reshape((CANDS,) + h.shape[2:]), CAND, 0, 0)
-    bil = both(h[:, ROWS : ROWS + bilinear.shape[0]], "core", 1)
-    bil = both(bil.reshape(CANDS, -1, WIDTH), "xl", 0)
-    bil = around(bil, "y")
-    place = jnp.stack([xh, z, y, core])
-    parts = lax.all_to_all(project(place, h, w), "z", 0, 0)
-    x, xt, means, col, stat = forward(lengths, parts)
+    bil = around(gather_half(h[:, ROWS : ROWS + bilinear.shape[0]]), "y")
+    parts = project(place, h, w)
+    parts = lax.all_to_all((parts * SCALE).astype(jnp.float16), "z", 0, 0)
+    x = (jnp.sum(parts.astype(F32), axis=0) * (1.0 / SCALE)).astype(BF)
+    xt, means, col, stat = forward(lengths, x)
+    bil, means = lax.optimization_barrier((bil, means))
+    bil = bil + [lax.ppermute(piece, "core", [(0, 1), (1, 0)]) for piece in bil]
     means = lax.all_to_all(means, CAND, 0, 0)
     drows, logits, term = backward(lengths, place, means, bil, x, xt, col, stat, labels)
     drows = lax.all_to_all(drows, "z", 0, 0)

time: 151 us -> 140 us (0.927)
  blocking collectives: 32.9 us -> 47.1 us
  waiting for transfers between devices: 52.5 us -> 38.5 us
  starting transfers between devices: 33.7 us -> 26.6 us
  local copies, waits for them, and re-layouts: 7.3 us -> 1.45 us
  other arithmetic: 1.37 us -> 3.88 us
    all_to_all x0 -> x1, blocking collectives: none -> 14.9 us  [body(): means = lax.all_to_all(means, CAND, 0, 0)]
    all_to_all x2 -> x1, waiting for transfers between devices: 18.8 us -> 5.27 us  [body(): parts = lax.all_to_all((parts * SCALE).astype(jnp.float16), 'z', 0, 0)]
    all_to_all x1, waiting for transfers between devices: 10.4 us -> 22.2 us  [body(): h = lax.all_to_all(h.reshape((CANDS,) + h.shape[2:]), CAND, 0, 0)]
    ppermute x6, waiting for transfers between devices: 10.5 us -> 1.35 us  [around(): lax.ppermute(value, axis, [(i, (i + k) % count) for i in range(count)])]
    unnamed x18 -> x6, local copies, waits for them, and re-layouts: 7.27 us -> 1.44 us
    all_to_all x2 -> x1, starting transfers between devices: 9.29 us -> 4.24 us  [body(): parts = lax.all_to_all((parts * SCALE).astype(jnp.float16), 'z', 0, 0)]
    ppermute x3 -> x2, waiting for transfers between devices: 10.4 us -> 6.59 us  [both(): other = lax.ppermute(value, axis, [(0, 1), (1, 0)])]
    ppermute x6, starting transfers between devices: 11.8 us -> 9.37 us  [around(): lax.ppermute(value, axis, [(i, (i + k) % count) for i in range(count)])]
  transfers between devices with their start and end apart: 16 -> 19, of which waited for: 10 -> 7; matrix products, arithmetic and copies ran while one was open for 0% -> 2% of each run, Pallas kernels for 5% -> 7%
where the time goes in v3:
time: 140 us; the launch traced here: 139 us
  blocking collectives  47.1 us (34%)
  waiting for transfers between devices  38.5 us (28%)
  starting transfers between devices  26.6 us (19%)
  Pallas kernels  20.9 us (15%)
  other arithmetic  3.88 us (3%)
  local copies, waits for them, and re-layouts  1.45 us (1%)
    all_to_all x1, waiting for transfers between devices, body(): h = lax.all_to_all(h.reshape((CANDS,) + h.shape[2:]), CAND, 0, 0)  22.2 us
    all_to_all x1, blocking collectives, body(): drows = lax.all_to_all(drows, 'z', 0, 0)  16.4 us
    all_to_all x1, blocking collectives, body(): got = lax.all_to_all(sent, ('xh', 'xl', 'y'), 0, 0)  15.9 us
    all_to_all x1, blocking collectives, body(): means = lax.all_to_all(means, CAND, 0, 0)  14.9 us
    ppermute x6, starting transfers between devices, around(): lax.ppermute(value, axis, [(i, (i + k) % count) for i in range(count)])  9.37 us
    pallas_call x1, Pallas kernels, backward(): pl.pallas_call(backward_kernel, out_shape=(jax.ShapeDtypeStruct((CANDS //...  7.13 us
    all_to_all x1, starting transfers between devices, body(): h = lax.all_to_all(h.reshape((CANDS,) + h.shape[2:]), CAND, 0, 0)  6.7 us
    ppermute x2, waiting for transfers between devices, both(): other = lax.ppermute(value, axis, [(0, 1), (1, 0)])  6.59 us
  transfers between devices with their start and end apart: 19, of which 7 were waited for; matrix products, arithmetic and copies ran while one was open for 2% of the time, Pallas kernels for 7%

profile of v3, /device:TPU:0, one launch (start us, length us, event | category | flops | bytes accessed | tf_op | source)
XLA Modules:
  0.0 139.3 jit_solution(12271242792411898048)
XLA Ops:
  0.6 0.8 broadcast_select_fusion.3
  1.4 1.6 %collective-permute-start = (bf16[32,512]{1,0:T(8,128)(2,1)S(1)}, bf16[32,512]{1,0:T(8,128)(2,1)S(1)}, u32[]{:S(2)}, u32[]{:S(2)}) collective-permute-start(bf16[32,512]{1,0:T(8,128)(2,1)S(1)} %get-tuple-element.45), channel_id=1, source_target_pairs={{0,8},{8,0},{64,72},{72,64},{1,9},{9,1},{65,73},{73,65},{2,10},{10... | collective-permute-start | bytes 98312 | tf_op jit(solution)/shard_map/ppermute | solution.py:444
  3.1 2.1 %collective-permute-start.2 = (bf16[32,512]{1,0:T(8,128)(2,1)S(1)}, bf16[32,512]{1,0:T(8,128)(2,1)S(1)}, u32[]{:S(2)}, u32[]{:S(2)}) collective-permute-start(bf16[32,512]{1,0:T(8,128)(2,1)S(1)} %get-tuple-element.46), channel_id=1, source_target_pairs={{0,72},{8,64},{64,8},{72,0},{1,73},{9,65},{65,9},{73,1},{2,74},{10... | collective-permute-start | bytes 98312 | tf_op jit(solution)/shard_map/ppermute | solution.py:444
  5.2 0.6 collective-permute-start.1
  5.8 2.3 %shard_map.76 = bf16[2,4,144,1024]{3,2,1,0:T(8,128)(2,1)S(1)} custom-call(bf16[128,4096]{1,0:T(8,128)(2,1)} %bitcast.40, bf16[128,4096]{1,0:T(8,128)(2,1)} %bitcast.41, bf16[8,1024]{1,0:T(8,128)(2,1)} %bil_ref.1), custom_call_target="tpu_custom_call" | custom-call | tf_op jit(solution)/shard_map/pallas_call | solution.py:60
  8.2 0.0 copy-start
  8.2 1.4 %copy-done = bf16[2,4,144,1024]{3,2,1,0:T(8,128)(2,1)} copy-done((bf16[2,4,144,1024]{3,2,1,0:T(8,128)(2,1)}, bf16[2,4,144,1024]{3,2,1,0:T(8,128)(2,1)S(1)}, u32[]{:S(2)}) %copy-start) | copy-done | bytes 2359320
  9.6 0.0 collective-permute-done
  9.6 0.0 collective-permute-done.2
  9.6 1.0 collective-permute-done.1
  10.6 6.7 %all-to-all-start = ((bf16[8,144,1024]{2,1,0:T(8,128)(2,1)}), bf16[8,144,1024]{2,1,0:T(8,128)(2,1)S(1)}, u32[]{:S(2)}, u32[]{:S(2)}) async-start(bf16[8,144,1024]{2,1,0:T(8,128)(2,1)} %bitcast.32), calls=%async_computation | async-start | bytes 4718592 | tf_op jit(solution)/shard_map/all_to_all | solution.py:471
  17.3 0.0 collective-permute-start.8
  17.3 1.3 collective-permute-done.8
  18.8 3.1 %collective-permute-start.11 = (bf16[2,2,64,512]{3,2,1,0:T(8,128)(2,1)S(1)}, bf16[2,2,64,512]{3,2,1,0:T(8,128)(2,1)S(1)}, u32[]{:S(2)}, u32[]{:S(2)}) collective-permute-start(bf16[2,2,64,512]{3,2,1,0:T(8,128)(2,1)S(1)} %bitcast.33), channel_id=1, source_target_pairs={{0,6},{2,0},{4,2},{6,4},{1,7},{3,1},{5,3},{7,5},{8,14},{10,8},{12,... | collective-permute-start | bytes 786440 | tf_op jit(solution)/shard_map/ppermute | solution.py:433
  21.8 0.6 collective-permute-start.10
  22.5 1.0 collective-permute-start.9
  23.4 0.1 pad_add_fusion.place_ref
  23.5 22.2 %all-to-all-done.h_ref = bf16[8,144,1024]{2,1,0:T(8,128)(2,1)S(1)} async-done(((bf16[8,144,1024]{2,1,0:T(8,128)(2,1)}), bf16[8,144,1024]{2,1,0:T(8,128)(2,1)S(1)}, u32[]{:S(2)}, u32[]{:S(2)}) %all-to-all-start) | async-done | bytes 2359328 | tf_op jit(solution)/shard_map/all_to_all | solution.py:471
  45.7 0.1 collective-permute-start.3
  45.8 0.0 collective-permute-done.11.refs_3_
  45.8 0.0 collective-permute-done.10.refs_2_
  45.8 0.0 collective-permute-done.9.refs_1_
  45.8 2.7 %shard_map.77 = f32[4,1024,128]{2,1,0:T(8,128)S(1)} custom-call(s32[4]{0:T(128)S(1)} %pad_add_fusion.place_ref, bf16[8,144,1024]{2,1,0:T(8,128)(2,1)S(1)} %all-to-all-done.h_ref, bf16[2,2,64,512]{3,2,1,0:T(8,128)(2,1)S(1)} %bitcast.36, bf16[2,2,64,512]{3,2,1,0:T(8,128)(2,1)S(1)} %collective-permute-done.9.refs_1_, ...), custom_call_target="tpu_custom_call" | custom-call | tf_op jit(solution)/shard_map/pallas_call | solution.py:95
  48.6 1.2 multiply_convert_fusion
  49.7 4.2 %all-to-all-start.1 = ((f16[4,1024,128]{2,1,0:T(8,128)(2,1)}), f16[4,1024,128]{2,1,0:T(8,128)(2,1)}, u32[]{:S(2)}, u32[]{:S(2)}) async-start(f16[4,1024,128]{2,1,0:T(8,128)(2,1)} %multiply_convert_fusion), calls=%async_computation.1 | async-start | bytes 2097152 | tf_op jit(solution)/shard_map/all_to_all | solution.py:474
  54.0 0.0 copy-start.1
  54.0 0.0 collective-permute-done.3
  54.0 0.7 collective-permute-start.4
  54.7 5.3 %collective-permute-done.4 = bf16[8,16,512]{2,1,0:T(8,128)(2,1)S(1)} collective-permute-done((bf16[8,16,512]{2,1,0:T(8,128)(2,1)S(1)}, bf16[8,16,512]{2,1,0:T(8,128)(2,1)S(1)}, u32[]{:S(2)}, u32[]{:S(2)}) %collective-permute-start.4) | collective-permute-done | bytes 131104 | tf_op jit(solution)/shard_map/ppermute | solution.py:423
  60.1 3.1 %collective-permute-start.7 = (bf16[2,8,16,512]{3,2,1,0:T(8,128)(2,1)S(1)}, bf16[2,8,16,512]{3,2,1,0:T(8,128)(2,1)S(1)}, u32[]{:S(2)}, u32[]{:S(2)}) collective-permute-start(bf16[2,8,16,512]{3,2,1,0:T(8,128)(2,1)S(1)} %pad_maximum_fusion.refs_0_), channel_id=1, source_target_pairs={{0,6},{2,0},{4,2},{6,4},{1,7},{3,1},{5,3},{7,5},{8,14},{10,8},{12,... | collective-permute-start | bytes 786440 | tf_op jit(solution)/shard_map/ppermute | solution.py:433
  63.2 0.6 collective-permute-start.6
  63.8 1.0 collective-permute-start.5
  64.8 5.3 %all-to-all-done.1 = f16[4,1024,128]{2,1,0:T(8,128)(2,1)} async-done(((f16[4,1024,128]{2,1,0:T(8,128)(2,1)}), f16[4,1024,128]{2,1,0:T(8,128)(2,1)}, u32[]{:S(2)}, u32[]{:S(2)}) %all-to-all-start.1) | async-done | bytes 1048608 | tf_op jit(solution)/shard_map/all_to_all | solution.py:474
  70.1 1.4 %convert_reduce_fusion = f32[1024,128]{1,0:T(8,128)S(1)} fusion(f16[4,1024,128]{2,1,0:T(8,128)(2,1)} %all-to-all-done.1), kind=kLoop, calls=%fused_computation | loop fusion | flops 917504 | bytes 1572864 | tf_op jit(solution)/shard_map/reduce_sum | solution.py:475
  71.5 0.0 copy-done.1
  71.5 0.0 copy-start.2
  71.5 5.1 %shard_map.78 = (bf16[128,1024]{1,0:T(8,128)(2,1)S(1)}, f32[8,64,128]{2,1,0:T(8,128)S(1)}, f32[2,8,1024]{2,1,0:T(8,128)S(1)}, f32[64,256]{1,0:T(8,128)S(1)}) custom-call(s32[8]{0:T(128)S(1)} %bitcast.38, bf16[1024,128]{1,0:T(8,128)(2,1)S(1)} %multiply_convert_fusion.1.x_ref), custom_call_target="tpu_custom_call" | custom-call | flops 12884901888 | bytes 16777216 | tf_op jit(solution)/shard_map/pallas_call | solution.py:188
  76.7 0.0 collective-permute-done.7.refs_3_
  76.7 0.0 collective-permute-done.6.refs_2_
  76.7 1.3 collective-permute-done.5.refs_1_
  78.0 0.0 collective-permute-start.12
  78.1 0.5 collective-permute-start.13
  78.5 0.0 collective-permute-start.14
  78.6 0.5 collective-permute-start.15
  79.1 14.9 %all_to_all.25.mean_ref = f32[8,64,128]{2,1,0:T(8,128)S(1)} all-to-all(f32[8,64,128]{2,1,0:T(8,128)S(1)} %get-tuple-element.24), channel_id=1, replica_groups=mesh['xh'=2,'z'=4,'xl'=2,'y'=4,'core'=2] {'xh','z'}, dimensions={0} | all-to-all | bytes 524288 | tf_op jit(solution)/shard_map/all_to_all | solution.py:479
  93.9 0.0 collective-permute-done.12.refs_4_
  93.9 0.0 collective-permute-done.13.refs_5_
  93.9 0.0 collective-permute-done.14.refs_6_
  93.9 0.0 collective-permute-done.15.refs_7_
  93.9 0.0 copy-done.2
  93.9 7.1 %shard_map.79 = (bf16[4,1024,128]{2,1,0:T(8,128)(2,1)S(1)}, f32[8,8]{1,0:T(8,128)}, f32[256,512]{1,0:T(8,128)S(1)}) custom-call(s32[8]{0:T(128)S(1)} %bitcast.39, s32[4]{0:T(128)S(1)} %pad_add_fusion.place_ref, f32[8,64,128]{2,1,0:T(8,128)S(1)} %all_to_all.25.mean_ref, bf16[1024,128]{1,0:T(8,128)(2,1)S(1)} %multiply_convert_fusion.1.x_ref, ...), custom_call_target="tpu_custom_call" | custom-call | tf_op jit(solution)/shard_map/pallas_call | solution.py:335
  101.1 16.4 %all_to_all.26.d_ref = bf16[4,1024,128]{2,1,0:T(8,128)(2,1)S(1)} all-to-all(bf16[4,1024,128]{2,1,0:T(8,128)(2,1)S(1)} %get-tuple-element.33), channel_id=1, replica_groups=mesh['xh'=2,'z'=4,'xl'=2,'y'=4,'core'=2] {'z'}, dimensions={0} | all-to-all | bytes 2097152 | tf_op jit(solution)/shard_map/all_to_all | solution.py:481
  117.5 2.8 %shard_map.80 = (f32[16,40,512]{2,1,0:T(8,128)S(1)}, bf16[16,40,512]{2,1,0:T(8,128)(2,1)S(1)}) custom-call(s32[4]{0:T(128)S(1)} %pad_add_fusion.place_ref, bf16[8,144,1024]{2,1,0:T(8,128)(2,1)S(1)} %all-to-all-done.h_ref, bf16[4,1024,128]{2,1,0:T(8,128)(2,1)S(1)} %all_to_all.26.d_ref, f32[32,8,512]{2,1,0:T(8,128)S(1)} %bitcast.37), custom_call_target="tpu_custom_call" | custom-call | tf_op jit(solution)/shard_map/pallas_call | solution.py:376
  120.3 0.1 collective-permute-start.16
  120.4 2.1 %collective-permute-done.16 = bf16[16,40,512]{2,1,0:T(8,128)(2,1)S(1)} collective-permute-done((bf16[16,40,512]{2,1,0:T(8,128)(2,1)S(1)}, bf16[16,40,512]{2,1,0:T(8,128)(2,1)S(1)}, u32[]{:S(2)}, u32[]{:S(2)}) %collective-permute-start.16) | collective-permute-done | bytes 655392 | tf_op jit(solution)/shard_map/ppermute | solution.py:484
  122.5 0.2 add_convert_fusion
  122.7 15.9 %all_to_all.27.got_ref = bf16[16,40,512]{2,1,0:T(8,128)(2,1)S(1)} all-to-all(bf16[16,40,512]{2,1,0:T(8,128)(2,1)S(1)} %add_convert_fusion), channel_id=1, replica_groups=mesh['xh'=2,'z'=4,'xl'=2,'y'=4,'core'=2] {'xh','xl','y'}, dimensions={0} | all-to-all | bytes 1310720 | tf_op jit(solution)/shard_map/all_to_all | solution.py:486
  138.6 0.7 shard_map.81
  (12 shorter events, 0.3 us)
Async XLA Ops:
  1.4 8.2 %collective-permute-start = (bf16[32,512]{1,0:T(8,128)(2,1)S(1)}, bf16[32,512]{1,0:T(8,128)(2,1)S(1)}, u32[]{:S(2)}, u32[]{:S(2)}) collective-permute-start(bf16[32,512]{1,0:T(8,128)(2,1)S(1)} %get-tuple-element.45), channel_id=1, source_target_pairs={{0,8},{8,0},{64,72},{72,64},{1,9},{9,1},{65,73},{73,65},{2,10},{10... | collective-permute-start | bytes 98312 | tf_op jit(solution)/shard_map/ppermute | solution.py:444
  3.1 6.5 %collective-permute-start.2 = (bf16[32,512]{1,0:T(8,128)(2,1)S(1)}, bf16[32,512]{1,0:T(8,128)(2,1)S(1)}, u32[]{:S(2)}, u32[]{:S(2)}) collective-permute-start(bf16[32,512]{1,0:T(8,128)(2,1)S(1)} %get-tuple-element.46), channel_id=1, source_target_pairs={{0,72},{8,64},{64,8},{72,0},{1,73},{9,65},{65,9},{73,1},{2,74},{10... | collective-permute-start | bytes 98312 | tf_op jit(solution)/shard_map/ppermute | solution.py:444
  5.2 5.4 %collective-permute-start.1 = (bf16[32,512]{1,0:T(8,128)(2,1)S(1)}, bf16[32,512]{1,0:T(8,128)(2,1)S(1)}, u32[]{:S(2)}, u32[]{:S(2)}) collective-permute-start(bf16[32,512]{1,0:T(8,128)(2,1)S(1)} %get-tuple-element.46), channel_id=1, source_target_pairs={{0,64},{8,72},{64,0},{72,8},{1,65},{9,73},{65,1},{73,9},{2,66},{10... | collective-permute-start | bytes 98312 | tf_op jit(solution)/shard_map/ppermute | solution.py:444
  8.2 1.4 %copy-start = (bf16[2,4,144,1024]{3,2,1,0:T(8,128)(2,1)}, bf16[2,4,144,1024]{3,2,1,0:T(8,128)(2,1)S(1)}, u32[]{:S(2)}) copy-start(bf16[2,4,144,1024]{3,2,1,0:T(8,128)(2,1)S(1)} %shard_map.76) | copy-start | bytes 7077892
  10.6 35.1 %all-to-all-start = ((bf16[8,144,1024]{2,1,0:T(8,128)(2,1)}), bf16[8,144,1024]{2,1,0:T(8,128)(2,1)S(1)}, u32[]{:S(2)}, u32[]{:S(2)}) async-start(bf16[8,144,1024]{2,1,0:T(8,128)(2,1)} %bitcast.32), calls=%async_computation | async-start | bytes 4718592 | tf_op jit(solution)/shard_map/all_to_all | solution.py:471
  17.3 1.3 collective-permute-start.8
  18.8 27.1 %collective-permute-start.11 = (bf16[2,2,64,512]{3,2,1,0:T(8,128)(2,1)S(1)}, bf16[2,2,64,512]{3,2,1,0:T(8,128)(2,1)S(1)}, u32[]{:S(2)}, u32[]{:S(2)}) collective-permute-start(bf16[2,2,64,512]{3,2,1,0:T(8,128)(2,1)S(1)} %bitcast.33), channel_id=1, source_target_pairs={{0,6},{2,0},{4,2},{6,4},{1,7},{3,1},{5,3},{7,5},{8,14},{10,8},{12,... | collective-permute-start | bytes 786440 | tf_op jit(solution)/shard_map/ppermute | solution.py:433
  21.8 24.0 %collective-permute-start.10 = (bf16[2,2,64,512]{3,2,1,0:T(8,128)(2,1)S(1)}, bf16[2,2,64,512]{3,2,1,0:T(8,128)(2,1)S(1)}, u32[]{:S(2)}, u32[]{:S(2)}) collective-permute-start(bf16[2,2,64,512]{3,2,1,0:T(8,128)(2,1)S(1)} %bitcast.34), channel_id=1, source_target_pairs={{0,4},{2,6},{4,0},{6,2},{1,5},{3,7},{5,1},{7,3},{8,12},{10,14},{12... | collective-permute-start | bytes 786440 | tf_op jit(solution)/shard_map/ppermute | solution.py:433
  22.5 23.4 %collective-permute-start.9 = (bf16[2,2,64,512]{3,2,1,0:T(8,128)(2,1)S(1)}, bf16[2,2,64,512]{3,2,1,0:T(8,128)(2,1)S(1)}, u32[]{:S(2)}, u32[]{:S(2)}) collective-permute-start(bf16[2,2,64,512]{3,2,1,0:T(8,128)(2,1)S(1)} %bitcast.35), channel_id=1, source_target_pairs={{0,2},{2,4},{4,6},{6,0},{1,3},{3,5},{5,7},{7,1},{8,10},{10,12},{12... | collective-permute-start | bytes 786440 | tf_op jit(solution)/shard_map/ppermute | solution.py:433
  45.7 8.3 %collective-permute-start.3 = (bf16[8,8,512]{2,1,0:T(8,128)(2,1)S(1)}, bf16[8,8,512]{2,1,0:T(8,128)(2,1)S(1)}, u32[]{:S(2)}, u32[]{:S(2)}) collective-permute-start(bf16[8,8,512]{2,1,0:T(8,128)(2,1)S(1)} %broadcast_select_fusion), channel_id=1, source_target_pairs={{0,1},{1,0},{2,3},{3,2},{4,5},{5,4},{6,7},{7,6},{8,9},{9,8},{10,11... | collective-permute-start | bytes 196616 | tf_op jit(solution)/shard_map/ppermute | solution.py:457
  49.7 20.3 %all-to-all-start.1 = ((f16[4,1024,128]{2,1,0:T(8,128)(2,1)}), f16[4,1024,128]{2,1,0:T(8,128)(2,1)}, u32[]{:S(2)}, u32[]{:S(2)}) async-start(f16[4,1024,128]{2,1,0:T(8,128)(2,1)} %multiply_convert_fusion), calls=%async_computation.1 | async-start | bytes 2097152 | tf_op jit(solution)/shard_map/all_to_all | solution.py:474
  54.0 17.5 %copy-start.1 = (s32[1,8]{1,0:T(1,128)S(1)}, s32[1,8]{1,0:T(1,128)}, u32[]{:S(2)}) copy-start(s32[1,8]{1,0:T(1,128)} %param.8) | copy-start | bytes 100
  54.0 6.0 %collective-permute-start.4 = (bf16[8,16,512]{2,1,0:T(8,128)(2,1)S(1)}, bf16[8,16,512]{2,1,0:T(8,128)(2,1)S(1)}, u32[]{:S(2)}, u32[]{:S(2)}) collective-permute-start(bf16[8,16,512]{2,1,0:T(8,128)(2,1)S(1)} %copy_bitcast_fusion), channel_id=1, source_target_pairs={{0,8},{8,0},{1,9},{9,1},{2,10},{10,2},{3,11},{11,3},{4,12},{12,4},... | collective-permute-start | bytes 393224 | tf_op jit(solution)/shard_map/ppermute | solution.py:423
  60.1 16.6 %collective-permute-start.7 = (bf16[2,8,16,512]{3,2,1,0:T(8,128)(2,1)S(1)}, bf16[2,8,16,512]{3,2,1,0:T(8,128)(2,1)S(1)}, u32[]{:S(2)}, u32[]{:S(2)}) collective-permute-start(bf16[2,8,16,512]{3,2,1,0:T(8,128)(2,1)S(1)} %pad_maximum_fusion.refs_0_), channel_id=1, source_target_pairs={{0,6},{2,0},{4,2},{6,4},{1,7},{3,1},{5,3},{7,5},{8,14},{10,8},{12,... | collective-permute-start | bytes 786440 | tf_op jit(solution)/shard_map/ppermute | solution.py:433
  63.2 13.5 %collective-permute-start.6 = (bf16[2,8,16,512]{3,2,1,0:T(8,128)(2,1)S(1)}, bf16[2,8,16,512]{3,2,1,0:T(8,128)(2,1)S(1)}, u32[]{:S(2)}, u32[]{:S(2)}) collective-permute-start(bf16[2,8,16,512]{3,2,1,0:T(8,128)(2,1)S(1)} %pad_maximum_fusion.refs_0_), channel_id=1, source_target_pairs={{0,4},{2,6},{4,0},{6,2},{1,5},{3,7},{5,1},{7,3},{8,12},{10,14},{12... | collective-permute-start | bytes 786440 | tf_op jit(solution)/shard_map/ppermute | solution.py:433
  63.8 14.2 %collective-permute-start.5 = (bf16[2,8,16,512]{3,2,1,0:T(8,128)(2,1)S(1)}, bf16[2,8,16,512]{3,2,1,0:T(8,128)(2,1)S(1)}, u32[]{:S(2)}, u32[]{:S(2)}) collective-permute-start(bf16[2,8,16,512]{3,2,1,0:T(8,128)(2,1)S(1)} %pad_maximum_fusion.refs_0_), channel_id=1, source_target_pairs={{0,2},{2,4},{4,6},{6,0},{1,3},{3,5},{5,7},{7,1},{8,10},{10,12},{12... | collective-permute-start | bytes 786440 | tf_op jit(solution)/shard_map/ppermute | solution.py:433
  71.5 22.4 %copy-start.2 = (s32[1,28]{1,0:T(1,128)S(1)}, s32[1,28]{1,0:T(1,128)}, u32[]{:S(2)}) copy-start(s32[1,28]{1,0:T(1,128)} %label_ref.1) | copy-start | bytes 340
  78.0 15.9 %collective-permute-start.12 = (bf16[2,8,16,512]{3,2,1,0:T(8,128)(2,1)S(1)}, bf16[2,8,16,512]{3,2,1,0:T(8,128)(2,1)S(1)}, u32[]{:S(2)}, u32[]{:S(2)}) collective-permute-start(bf16[2,8,16,512]{3,2,1,0:T(8,128)(2,1)S(1)} %pad_maximum_fusion.refs_0_), channel_id=1, source_target_pairs={{0,1},{1,0},{2,3},{3,2},{4,5},{5,4},{6,7},{7,6},{8,9},{9,8},{10,11... | collective-permute-start | bytes 786440 | tf_op jit(solution)/shard_map/ppermute | solution.py:478
  78.1 15.9 %collective-permute-start.13 = (bf16[2,8,16,512]{3,2,1,0:T(8,128)(2,1)S(1)}, bf16[2,8,16,512]{3,2,1,0:T(8,128)(2,1)S(1)}, u32[]{:S(2)}, u32[]{:S(2)}) collective-permute-start(bf16[2,8,16,512]{3,2,1,0:T(8,128)(2,1)S(1)} %collective-permute-done.5.refs_1_), channel_id=1, source_target_pairs={{0,1},{1,0},{2,3},{3,2},{4,5},{5,4},{6,7},{7,6},{8,9},{9,8},{10,11... | collective-permute-start | bytes 786440 | tf_op jit(solution)/shard_map/ppermute | solution.py:478
  78.5 15.4 %collective-permute-start.14 = (bf16[2,8,16,512]{3,2,1,0:T(8,128)(2,1)S(1)}, bf16[2,8,16,512]{3,2,1,0:T(8,128)(2,1)S(1)}, u32[]{:S(2)}, u32[]{:S(2)}) collective-permute-start(bf16[2,8,16,512]{3,2,1,0:T(8,128)(2,1)S(1)} %collective-permute-done.6.refs_2_), channel_id=1, source_target_pairs={{0,1},{1,0},{2,3},{3,2},{4,5},{5,4},{6,7},{7,6},{8,9},{9,8},{10,11... | collective-permute-start | bytes 786440 | tf_op jit(solution)/shard_map/ppermute | solution.py:478
  78.6 15.4 %collective-permute-start.15 = (bf16[2,8,16,512]{3,2,1,0:T(8,128)(2,1)S(1)}, bf16[2,8,16,512]{3,2,1,0:T(8,128)(2,1)S(1)}, u32[]{:S(2)}, u32[]{:S(2)}) collective-permute-start(bf16[2,8,16,512]{3,2,1,0:T(8,128)(2,1)S(1)} %collective-permute-done.7.refs_3_), channel_id=1, source_target_pairs={{0,1},{1,0},{2,3},{3,2},{4,5},{5,4},{6,7},{7,6},{8,9},{9,8},{10,11... | collective-permute-start | bytes 786440 | tf_op jit(solution)/shard_map/ppermute | solution.py:478
  120.3 2.2 %collective-permute-start.16 = (bf16[16,40,512]{2,1,0:T(8,128)(2,1)S(1)}, bf16[16,40,512]{2,1,0:T(8,128)(2,1)S(1)}, u32[]{:S(2)}, u32[]{:S(2)}) collective-permute-start(bf16[16,40,512]{2,1,0:T(8,128)(2,1)S(1)} %get-tuple-element.36), channel_id=1, source_target_pairs={{0,1},{1,0},{2,3},{3,2},{4,5},{5,4},{6,7},{7,6},{8,9},{9,8},{10,11... | collective-permute-start | bytes 1966088 | tf_op jit(solution)/shard_map/ppermute | solution.py:484

commit v4 on v3

--- a/solution.py
+++ b/solution.py
@@ -42,43 +42,41 @@
     return lax.broadcasted_iota(jnp.int32, shape, len(shape) - 2)
 
 
-def pack_kernel(low_ref, high_ref, bil_ref, out_ref):
+def pack_kernel(low_ref, high_ref, out_ref):
     half = low_ref.shape[1]
-    bil = bil_ref[...]
-    for dest in range(out_ref.shape[0]):
-        out_ref[dest, 0, :ROWS, :half] = low_ref[...]
-        out_ref[dest, 0, :ROWS, half:] = high_ref[...]
-        out_ref[dest, 0, ROWS:, :] = jnp.concatenate([bil, bil], axis=0)
-
-
-def pack(hidden, bil):
+    out_ref[0, :, :half] = low_ref[...]
+    out_ref[0, :, half:] = high_ref[...]
+
+
+def pack(hidden):
     quarter = CANDS // 2
     half = hidden.shape[1] // CANDS
-    rows = ROWS + 2 * bil.shape[0]
     hidden = pltpu.with_memory_space_constraint(hidden, pltpu.HBM)
-    bil = pltpu.with_memory_space_constraint(bil, pltpu.HBM)
     return pl.pallas_call(
         pack_kernel,
-        out_shape=jax.ShapeDtypeStruct((2, quarter, rows, 2 * half), BF),
+        out_shape=jax.ShapeDtypeStruct((quarter, ROWS, 2 * half), BF),
         grid=(quarter,),
         in_specs=[
             pl.BlockSpec((ROWS, half), lambda q: (0, q)),
             pl.BlockSpec((ROWS, half), lambda q: (0, q + CANDS // 2)),
-            pl.BlockSpec(bil.shape, lambda q: (0, 0)),
         ],
-        out_specs=pl.BlockSpec((2, 1, rows, 2 * half), lambda q: (0, q, 0, 0)),
+        out_specs=pl.BlockSpec((1, ROWS, 2 * half), lambda q: (q, 0, 0)),
         compiler_params=pltpu.CompilerParams(vmem_limit_bytes=16 << 20),
-    )(hidden, hidden, bil)
+    )(hidden, hidden)
 
 
 def project_kernel(place_ref, h_ref, *refs):
     pieces, (out_ref, w_scr) = refs[:-2], refs[-2:]
-    count = len(pieces)
+    count = len(pieces) // 2
+    half = pieces[0].shape[3]
 
     @pl.when(pl.program_id(0) == 0)
     def _():
-        for k, piece in enumerate(pieces):
-            w_scr[:, :, lax.rem(place_ref[2] + count - k, count)] = piece[...]
+        for k in range(count):
+            source = lax.rem(place_ref[2] + count - k, count)
+            for piece, side in ((pieces[k], place_ref[3]), (pieces[count + k], 1 - place_ref[3])):
+                columns = pl.ds(pl.multiple_of(side * half, half), half)
+                w_scr[:, :, source, :, columns] = piece[...]
 
     h = h_ref[...].reshape(h_ref.shape[0] * ROWS, h_ref.shape[2])
     total = mm(h, w_scr[...].reshape(h.shape[1], -1))
@@ -87,14 +85,16 @@
 
 
 def project(place, h, pieces):
-    steps = 4
-    per = CANDS // steps
+    steps = 2
+    per = h.shape[0] // steps
     shape = pieces[0].shape
     depth = h.shape[2]
-    dests = shape[3] // SLICE
+    count = len(pieces) // 2
+    width = 2 * shape[3]
+    dests = width // SLICE
     return pl.pallas_call(
         project_kernel,
-        out_shape=jax.ShapeDtypeStruct((dests, CANDS * ROWS, SLICE), F32),
+        out_shape=jax.ShapeDtypeStruct((dests, h.shape[0] * ROWS, SLICE), F32),
         grid=(steps,),
         in_specs=[
             pl.BlockSpec(memory_space=pltpu.SMEM),
@@ -102,8 +102,8 @@
         ]
         + [pl.BlockSpec(shape, lambda s: (0, 0, 0, 0))] * len(pieces),
         out_specs=pl.BlockSpec((dests, per * ROWS, SLICE), lambda s: (0, s, 0)),
-        scratch_shapes=[pltpu.VMEM(shape[:2] + (len(pieces),) + shape[2:], BF)],
-        compiler_params=pltpu.CompilerParams(vmem_limit_bytes=24 << 20),
+        scratch_shapes=[pltpu.VMEM(shape[:2] + (count, shape[2], width), BF)],
+        compiler_params=pltpu.CompilerParams(vmem_limit_bytes=32 << 20),
     )(place, h, *pieces)
 
 
@@ -214,8 +214,10 @@
     for k in range(count):
         for piece, side in ((bil_refs[k], core), (bil_refs[count + k], 1 - core)):
             columns = pl.ds(pl.multiple_of(side * half, half), half)
-            for part in range(2):
-                bil_scr[:, part, lax.rem(y + count - k, count), :, columns] = piece[part]
+            for hi, lo in ((0, 0), (0, 1), (1, 0), (1, 1)):
+                for back in range(piece.shape[2]):
+                    level = lax.rem(z + piece.shape[2] - back, piece.shape[2])
+                    bil_scr[hi, level, lo, lax.rem(y + count - k, count), :, columns] = piece[hi, lo, back]
     key_scr[...] = extend(x_ref[...], len_ref)
     here = xh * (CANDS // 2) + z
     means = jnp.concatenate([mean_ref[c] for c in range(CANDS)], axis=1)
@@ -256,7 +258,7 @@
     columns = pl.ds(pl.multiple_of(here * SLICE, SLICE), SLICE)
     back = mm(
         jnp.concatenate([rev_high, rev_low], axis=0),
-        bil_scr[:, :, :, :, columns].reshape(WIDTH, SLICE),
+        bil_scr[:, :, :, :, :, columns].reshape(WIDTH, SLICE),
     )
     back = back[:PAIRS] + back[PAIRS:]
     own_pooled = mean_ref[here] / radius
@@ -346,18 +348,27 @@
             pltpu.VMEM((rows, 4 * CANDS), BF),
             pltpu.VMEM((rows, SLICE), F32),
             pltpu.VMEM((rows, 2 * SLICE), BF),
-            pltpu.VMEM((CANDS, 2, len(bil) // 2, 2 * CANDS, WIDTH), BF),
+            pltpu.VMEM((2, CANDS // 2, 2, len(bil) // 2, 2 * CANDS, WIDTH), BF),
         ],
+        cost_estimate=pl.CostEstimate(flops=8 << 30, bytes_accessed=8 << 20, transcendentals=2 << 20),
         compiler_params=pltpu.CompilerParams(vmem_limit_bytes=32 << 20),
     )(lengths, place, means, x, xt, col, stat, labels, *bil)
 
 
-def gradient_kernel(place_ref, h_ref, d_ref, term_ref, mine_ref, other_ref, scr):
+def gradient_kernel(place_ref, h_ref, far_ref, d_ref, term_ref, mine_ref, other_ref, d_scr, scr):
     count, rows, depth = h_ref.shape
     groups, block, width = mine_ref.shape
-    h = h_ref[...].reshape(count * rows, depth)
-    d = jnp.concatenate([d_ref[q] for q in range(d_ref.shape[0])], axis=1)
-    total = mm(h, d, TN).reshape(2 * groups, -1, width)
+    rows *= count
+
+    @pl.when(pl.program_id(0) == 0)
+    def _():
+        for part, side in ((0, place_ref[0]), (1, 1 - place_ref[0])):
+            source = pl.ds(pl.multiple_of(side * rows, rows), rows)
+            for q in range(d_ref.shape[0]):
+                d_scr[part * rows : (part + 1) * rows, q * SLICE : (q + 1) * SLICE] = d_ref[q, source, :]
+
+    h = jnp.concatenate([h_ref[...].reshape(rows, depth), far_ref[...].reshape(rows, depth)], axis=0)
+    total = mm(h, d_scr[...], TN).reshape(2 * groups, -1, width)
     total = jnp.concatenate([total, term_ref[...]], axis=1)
     scr[...] = total.reshape(groups, 2, block, width)
     core = place_ref[3]
@@ -365,7 +376,7 @@
     other_ref[...] = scr[:, 1 - core].astype(BF)
 
 
-def gradient(place, h, d, term):
+def gradient(place, h, far, d, term):
     count, _, depth = h.shape
     steps = 4
     dests = term.shape[0] // 2
@@ -373,6 +384,7 @@
     block = depth // dests // 2 + term.shape[1]
     groups = dests // steps
     out = pl.BlockSpec((groups, block, width), lambda s: (s, 0, 0))
+    hidden = pl.BlockSpec((count, ROWS, depth // steps), lambda s: (0, 0, s))
     return pl.pallas_call(
         gradient_kernel,
         out_shape=(
@@ -382,14 +394,18 @@
         grid=(steps,),
         in_specs=[
             pl.BlockSpec(memory_space=pltpu.SMEM),
-            pl.BlockSpec((count, ROWS, depth // steps), lambda s: (0, 0, s)),
+            hidden,
+            hidden,
             pl.BlockSpec(d.shape, lambda s: (0, 0, 0)),
             pl.BlockSpec((2 * groups,) + term.shape[1:], lambda s: (s, 0, 0)),
         ],
         out_specs=(out, out),
-        scratch_shapes=[pltpu.VMEM((groups, 2, block, width), F32)],
+        scratch_shapes=[
+            pltpu.VMEM((d.shape[1], width), BF),
+            pltpu.VMEM((groups, 2, block, width), F32),
+        ],
         compiler_params=pltpu.CompilerParams(vmem_limit_bytes=24 << 20),
-    )(place, h, d, term)
+    )(place, h, far, d, term)
 
 
 def finish_kernel(got_ref, proj_ref, bil_ref):
@@ -419,12 +435,32 @@
     )(got)
 
 
-def both(value, axis, dim):
-    other = lax.ppermute(value, axis, [(0, 1), (1, 0)])
-    first = lax.axis_index(axis) == 0
-    return jnp.stack(
-        [jnp.where(first, value, other), jnp.where(first, other, value)], axis=dim
-    )
+SWAP = [(0, 1), (1, 0)]
+
+
+def gather_core(value):
+    first = lax.axis_index("core") == 0
+    half = value.shape[-1] // 2
+    keep = jnp.where(first, value[..., :half], value[..., half:])
+    away = jnp.where(first, value[..., half:], value[..., :half])
+    other = lax.ppermute(away, "core", SWAP)
+    return jnp.concatenate(
+        [jnp.where(first, keep, other), jnp.where(first, other, keep)], axis=-2
+    )
+
+
+def gather_x(value):
+    xh, xl = lax.axis_index("xh"), lax.axis_index("xl")
+    far, across, near = (
+        lax.ppermute(value, ("xh", "xl"), [(i, i ^ flip) for i in range(4)]) for flip in (2, 3, 1)
+    )
+    same = jnp.where(xl == 0, jnp.stack([value, near]), jnp.stack([near, value]))
+    cross = jnp.where(xl == 0, jnp.stack([far, across]), jnp.stack([across, far]))
+    return jnp.where(xh == 0, jnp.stack([same, cross]), jnp.stack([cross, same]))
+
+
+def with_other_core(pieces):
+    return pieces + [lax.ppermute(piece, "core", SWAP) for piece in pieces]
 
 
 def around(value, axis):
@@ -435,53 +471,40 @@
     ]
 
 
-def gather_x(w):
-    xh, xl = lax.axis_index("xh"), lax.axis_index("xl")
-    half = w.shape[1] // 2
-    keep = jnp.where(xh == 0, w[:, :half], w[:, half:])
-    away = jnp.where(xh == 0, w[:, half:], w[:, :half])
-    far, across, near = (
-        lax.ppermute(value, ("xh", "xl"), [(i, i ^ flip) for i in range(4)])
-        for value, flip in ((away, 2), (away, 3), (keep, 1))
-    )
-    same = jnp.where(xl == 0, jnp.stack([keep, near]), jnp.stack([near, keep]))
-    cross = jnp.where(xl == 0, jnp.stack([far, across]), jnp.stack([across, far]))
-    return jnp.where(xh == 0, jnp.stack([same, cross]), jnp.stack([cross, same]))
-
-
-def gather_half(bil):
-    core = lax.axis_index("core")
-    half = bil.shape[2] // 2
-    keep = jnp.where(core == 0, bil[:, :, :half], bil[:, :, half:])
-    away = jnp.where(core == 0, bil[:, :, half:], bil[:, :, :half])
-    other = lax.ppermute(away, "core", [(0, 1), (1, 0)])
-    pair = [jnp.where(core == 0, keep, other), jnp.where(core == 0, other, keep)]
-    return both(jnp.stack(pair, axis=1).reshape(bil.shape[0], -1, half), "xl", 0)
-
-
 def body(hidden_states, proj_weight, bilinear, lengths, labels):
     xh, z, y, core = (lax.axis_index(axis) for axis in ("xh", "z", "y", "core"))
     place = jnp.stack([xh, z, y, core])
     lengths = lengths[0]
-    w = gather_x(proj_weight)
-    h = pack(hidden_states[0, 0], bilinear)
+    rows = proj_weight.shape[0]
+    w = gather_core(jnp.concatenate([proj_weight, bilinear], axis=0))
+    w = w.reshape(2, -1, w.shape[1])
+    w, bil = (v.reshape(-1, v.shape[2]) for v in (w[:, :rows], w[:, rows:]))
+    bil = around(bil, "z")
+    rows = w.shape[0]
+    w = jnp.concatenate([w] + bil, axis=0)
+    h = pack(hidden_states[0, 0])
     h, w = lax.optimization_barrier((h, w))
-    w = both(w, "core", 2)
-    w = around(w.reshape(w.shape[:2] + (-1, w.shape[-1])), "y")
-    h = lax.all_to_all(h.reshape((CANDS,) + h.shape[2:]), CAND, 0, 0)
-    bil = around(gather_half(h[:, ROWS : ROWS + bilinear.shape[0]]), "y")
-    parts = project(place, h, w)
-    parts = lax.all_to_all((parts * SCALE).astype(jnp.float16), "z", 0, 0)
-    x = (jnp.sum(parts.astype(F32), axis=0) * (1.0 / SCALE)).astype(BF)
+    w = gather_x(w)
+    bil = w[:, :, rows:].reshape(2, 2, len(bil), -1, w.shape[3])
+    w = with_other_core(around(w[:, :, :rows], "y"))
+    h = lax.all_to_all(h, "z", 0, 0)
+    parts = (project(place, h, w) * SCALE).astype(jnp.float16)
+    parts, bil = lax.optimization_barrier((parts, bil))
+    bil = around(bil, "y")
+    parts = lax.all_to_all(parts, CAND, 0, 0)
+    parts = parts.reshape((2, -1) + parts.shape[1:]).astype(F32)
+    x = (jnp.sum(parts, axis=1) * (1.0 / SCALE)).astype(BF).reshape(CANDS * ROWS, SLICE)
     xt, means, col, stat = forward(lengths, x)
     bil, means = lax.optimization_barrier((bil, means))
-    bil = bil + [lax.ppermute(piece, "core", [(0, 1), (1, 0)]) for piece in bil]
+    bil = with_other_core(bil)
     means = lax.all_to_all(means, CAND, 0, 0)
+    far, means = lax.optimization_barrier((h, means))
+    far = lax.ppermute(far, "xh", SWAP)
     drows, logits, term = backward(lengths, place, means, bil, x, xt, col, stat, labels)
     drows = lax.all_to_all(drows, "z", 0, 0)
     term = term.reshape(-1, bilinear.shape[0], term.shape[1])
-    mine, other = gradient(place, h, drows, term)
-    other = lax.ppermute(other, "core", [(0, 1), (1, 0)])
+    mine, other = gradient(place, h, far, drows, term)
+    other = lax.ppermute(other, "core", SWAP)
     sent = (mine + other.astype(F32)).astype(BF)
     got = lax.all_to_all(sent, ("xh", "xl", "y"), 0, 0)
     grad_proj, grad_bil = finish(got, proj_weight.shape[0], bilinear.shape[0])

time: 140 us -> 135 us (0.964)
  waiting for transfers between devices: 38.5 us -> 34.3 us
  other arithmetic: 3.88 us -> 1.87 us
    all_to_all x2, waiting for transfers between devices: 27.5 us -> 13.8 us  [the longest x1 13.8 us: body(): parts = lax.all_to_all(parts, CAND, 0, 0)]
    ppermute x6 -> x9, waiting for transfers between devices: 1.35 us -> 14.5 us  [around(): lax.ppermute(value, axis, [(i, (i + k) % count) for i in range(count)])]
    ppermute x8 -> x11, waiting for transfers between devices: 8.69 us -> 3.71 us  [the longest x1 2.08 us: body(): other = lax.ppermute(other, 'core', SWAP)]
    ppermute x6 -> x9, starting transfers between devices: 9.37 us -> 12.2 us  [around(): lax.ppermute(value, axis, [(i, (i + k) % count) for i in range(count)])]
    all_to_all x1, blocking collectives: 14.9 us -> 13.1 us  [body(): means = lax.all_to_all(means, CAND, 0, 0)]
    all_to_all x2, starting transfers between devices: 10.9 us -> 9.47 us  [the longest x1 5.96 us: body(): parts = lax.all_to_all(parts, CAND, 0, 0)]
  transfers between devices with their start and end apart: 19 -> 25, of which waited for: 7 -> 10; matrix products, arithmetic and copies ran while one was open for 2% -> 0% of each run, Pallas kernels for 7% -> 12%
where the time goes in v4:
time: 135 us
  blocking collectives  46.4 us (34%)
  waiting for transfers between devices  34.3 us (25%)
  starting transfers between devices  27.7 us (21%)
  Pallas kernels  21.9 us (16%)
  other arithmetic  1.87 us (1%)
  local copies, waits for them, and re-layouts  1.64 us (1%)
    all_to_all x1, blocking collectives, body(): drows = lax.all_to_all(drows, 'z', 0, 0)  16.9 us
    all_to_all x1, blocking collectives, body(): got = lax.all_to_all(sent, ('xh', 'xl', 'y'), 0, 0)  16.3 us
    ppermute x9, waiting for transfers between devices, around(): lax.ppermute(value, axis, [(i, (i + k) % count) for i in range(count)])  14.5 us
    all_to_all x1, waiting for transfers between devices, body(): parts = lax.all_to_all(parts, CAND, 0, 0)  13.8 us
    all_to_all x1, blocking collectives, body(): means = lax.all_to_all(means, CAND, 0, 0)  13.1 us
    ppermute x9, starting transfers between devices, around(): lax.ppermute(value, axis, [(i, (i + k) % count) for i in range(count)])  12.2 us
    pallas_call x1, Pallas kernels, backward(): pl.pallas_call(backward_kernel, out_shape=(jax.ShapeDtypeStruct((CANDS //...  7.24 us
    all_to_all x1, starting transfers between devices, body(): parts = lax.all_to_all(parts, CAND, 0, 0)  5.96 us
  transfers between devices with their start and end apart: 25, of which 10 were waited for; matrix products, arithmetic and copies ran while one was open for 0% of the time, Pallas kernels for 12%

profile of v4, /device:TPU:0, one launch (start us, length us, event | category | flops | bytes accessed | tf_op | source)
XLA Modules:
  0.0 134.6 jit_solution(6583341892593425750)
XLA Ops:
  0.6 0.8 constant_dynamic-update-slice_fusion.1
  1.5 0.7 constant_dynamic-update-slice_fusion
  2.2 0.1 collective-permute-start
  2.3 3.4 %shard_map.76 = bf16[4,128,1024]{2,1,0:T(8,128)(2,1)} custom-call(bf16[128,4096]{1,0:T(8,128)(2,1)} %bitcast.33, bf16[128,4096]{1,0:T(8,128)(2,1)} %bitcast.34), custom_call_target="tpu_custom_call" | custom-call | tf_op jit(solution)/shard_map/pallas_call | solution.py:55
  5.7 0.0 collective-permute-done
  5.8 4.2 %collective-permute-start.3 = (bf16[16,512]{1,0:T(8,128)(2,1)S(1)}, bf16[16,512]{1,0:T(8,128)(2,1)S(1)}, u32[]{:S(2)}, u32[]{:S(2)}) collective-permute-start(bf16[16,512]{1,0:T(8,128)(2,1)S(1)} %slice_bitcast_fusion), channel_id=1, source_target_pairs={{0,48},{16,0},{32,16},{48,32},{1,49},{17,1},{33,17},{49,33},{2,50}... | collective-permute-start | bytes 49160 | tf_op jit(solution)/shard_map/ppermute | solution.py:469
  10.0 0.0 collective-permute-start.2
  10.0 1.3 collective-permute-start.1
  11.3 3.7 %collective-permute-done.1 = bf16[16,512]{1,0:T(8,128)(2,1)S(1)} collective-permute-done((bf16[16,512]{1,0:T(8,128)(2,1)S(1)}, bf16[16,512]{1,0:T(8,128)(2,1)S(1)}, u32[]{:S(2)}, u32[]{:S(2)}) %collective-permute-start.1) | collective-permute-done | bytes 16416 | tf_op jit(solution)/shard_map/ppermute | solution.py:469
  14.9 0.3 collective-permute-done.2
  15.2 0.0 collective-permute-done.3
  15.2 2.8 %collective-permute-start.6 = (bf16[128,512]{1,0:T(8,128)(2,1)S(1)}, bf16[128,512]{1,0:T(8,128)(2,1)S(1)}, u32[]{:S(2)}, u32[]{:S(2)}) collective-permute-start(bf16[128,512]{1,0:T(8,128)(2,1)S(1)} %constant_dynamic-update-slice_fusion.2), channel_id=1, source_target_pairs={{0,72},{8,64},{64,8},{72,0},{1,73},{9,65},{65,9},{73,1},{2,74},{10... | collective-permute-start | bytes 393224 | tf_op jit(solution)/shard_map/ppermute | solution.py:455
  18.1 0.8 collective-permute-start.5
  18.9 0.5 collective-permute-start.4
  19.4 3.5 %all-to-all-start = ((bf16[4,128,1024]{2,1,0:T(8,128)(2,1)}), bf16[4,128,1024]{2,1,0:T(8,128)(2,1)S(1)}, u32[]{:S(2)}, u32[]{:S(2)}) async-start(bf16[4,128,1024]{2,1,0:T(8,128)(2,1)} %shard_map.76), calls=%async_computation | async-start | bytes 2097152 | tf_op jit(solution)/shard_map/all_to_all | solution.py:490
  22.9 0.0 collective-permute-done.6
  22.9 2.3 %collective-permute-done.5 = bf16[128,512]{1,0:T(8,128)(2,1)S(1)} collective-permute-done((bf16[128,512]{1,0:T(8,128)(2,1)S(1)}, bf16[128,512]{1,0:T(8,128)(2,1)S(1)}, u32[]{:S(2)}, u32[]{:S(2)}) %collective-permute-start.5) | collective-permute-done | bytes 131104 | tf_op jit(solution)/shard_map/ppermute | solution.py:455
  25.2 0.0 collective-permute-done.4
  25.3 0.1 maximum_select_fusion
  25.4 3.1 %collective-permute-start.9 = (bf16[2,2,64,512]{3,2,1,0:T(8,128)(2,1)S(1)}, bf16[2,2,64,512]{3,2,1,0:T(8,128)(2,1)S(1)}, u32[]{:S(2)}, u32[]{:S(2)}) collective-permute-start(bf16[2,2,64,512]{3,2,1,0:T(8,128)(2,1)S(1)} %get-tuple-element.48.refs_0_), channel_id=1, source_target_pairs={{0,6},{2,0},{4,2},{6,4},{1,7},{3,1},{5,3},{7,5},{8,14},{10,8},{12,... | collective-permute-start | bytes 786440 | tf_op jit(solution)/shard_map/ppermute | solution.py:469
  28.5 0.6 collective-permute-start.8
  29.1 1.0 collective-permute-start.7
  30.1 0.0 collective-permute-start.10
  30.1 6.8 %collective-permute-done.9.refs_3_ = bf16[2,2,64,512]{3,2,1,0:T(8,128)(2,1)S(1)} collective-permute-done((bf16[2,2,64,512]{3,2,1,0:T(8,128)(2,1)S(1)}, bf16[2,2,64,512]{3,2,1,0:T(8,128)(2,1)S(1)}, u32[]{:S(2)}, u32[]{:S(2)}) %collective-permute-start.9) | collective-permute-done | bytes 262176 | tf_op jit(solution)/shard_map/ppermute | solution.py:469
  36.9 0.0 collective-permute-start.13
  36.9 1.0 collective-permute-done.8.refs_2_
  38.0 0.0 collective-permute-start.12
  38.0 2.7 %collective-permute-done.7.refs_1_ = bf16[2,2,64,512]{3,2,1,0:T(8,128)(2,1)S(1)} collective-permute-done((bf16[2,2,64,512]{3,2,1,0:T(8,128)(2,1)S(1)}, bf16[2,2,64,512]{3,2,1,0:T(8,128)(2,1)S(1)}, u32[]{:S(2)}, u32[]{:S(2)}) %collective-permute-start.7) | collective-permute-done | bytes 262176 | tf_op jit(solution)/shard_map/ppermute | solution.py:469
  40.6 0.0 collective-permute-start.11
  40.6 0.1 pad_add_fusion.place_ref
  40.7 0.0 collective-permute-done.10.refs_4_
  40.7 0.0 collective-permute-done.13.refs_7_
  40.7 0.0 collective-permute-done.12.refs_6_
  40.7 1.4 %collective-permute-done.11.refs_5_ = bf16[2,2,64,512]{3,2,1,0:T(8,128)(2,1)S(1)} collective-permute-done((bf16[2,2,64,512]{3,2,1,0:T(8,128)(2,1)S(1)}, bf16[2,2,64,512]{3,2,1,0:T(8,128)(2,1)S(1)}, u32[]{:S(2)}, u32[]{:S(2)}) %collective-permute-start.11) | collective-permute-done | bytes 262176 | tf_op jit(solution)/shard_map/ppermute | solution.py:463
  42.2 0.0 all-to-all-done.h_ref
  42.2 2.3 %shard_map.77 = f32[8,512,128]{2,1,0:T(8,128)S(1)} custom-call(s32[4]{0:T(128)S(1)} %pad_add_fusion.place_ref, bf16[4,128,1024]{2,1,0:T(8,128)(2,1)S(1)} %all-to-all-done.h_ref, bf16[2,2,64,512]{3,2,1,0:T(8,128)(2,1)S(1)} %get-tuple-element.48.refs_0_, bf16[2,2,64,512]{3,2,1,0:T(8,128)(2,1)S(1)} %collective-permute-done.7.refs_1_, ...), custom_call_target="tpu_custom_call" | custom-call | tf_op jit(solution)/shard_map/pallas_call | solution.py:95
  44.4 1.2 multiply_convert_fusion
  45.7 6.0 %all-to-all-start.1 = ((f16[8,512,128]{2,1,0:T(8,128)(2,1)}), f16[8,512,128]{2,1,0:T(8,128)(2,1)S(1)}, u32[]{:S(2)}, u32[]{:S(2)}) async-start(f16[8,512,128]{2,1,0:T(8,128)(2,1)} %multiply_convert_fusion), calls=%async_computation.1 | async-start | bytes 2097152 | tf_op jit(solution)/shard_map/all_to_all | solution.py:494
  51.6 0.7 collective-permute-start.16
  52.4 0.5 collective-permute-start.15
  52.8 0.8 collective-permute-start.14
  53.7 13.8 %all-to-all-done.1 = f16[8,512,128]{2,1,0:T(8,128)(2,1)S(1)} async-done(((f16[8,512,128]{2,1,0:T(8,128)(2,1)}), f16[8,512,128]{2,1,0:T(8,128)(2,1)S(1)}, u32[]{:S(2)}, u32[]{:S(2)}) %all-to-all-start.1) | async-done | bytes 1048608 | tf_op jit(solution)/shard_map/all_to_all | solution.py:494
  67.5 0.1 convert_reduce_fusion
  67.7 0.0 copy-start.1
  67.7 5.1 %shard_map.78 = (bf16[128,1024]{1,0:T(8,128)(2,1)S(1)}, f32[8,64,128]{2,1,0:T(8,128)S(1)}, f32[2,8,1024]{2,1,0:T(8,128)S(1)}, f32[64,256]{1,0:T(8,128)S(1)}) custom-call(s32[8]{0:T(128)S(1)} %bitcast.31, bf16[1024,128]{1,0:T(8,128)(2,1)S(1)} %bitcast.24), custom_call_target="tpu_custom_call" | custom-call | flops 12884901888 | bytes 16777216 | tf_op jit(solution)/shard_map/pallas_call | solution.py:188
  72.9 0.0 collective-permute-done.15.refs_2_
  72.9 0.0 collective-permute-done.14.refs_1_
  72.9 0.1 collective-permute-start.17
  73.0 0.5 collective-permute-start.18
  73.5 0.1 collective-permute-start.19
  73.6 0.4 collective-permute-start.20
  74.0 13.1 %all_to_all.25.mean_ref = f32[8,64,128]{2,1,0:T(8,128)S(1)} all-to-all(f32[8,64,128]{2,1,0:T(8,128)S(1)} %get-tuple-element.30), channel_id=1, replica_groups=mesh['xh'=2,'z'=4,'xl'=2,'y'=4,'core'=2] {'xh','z'}, dimensions={0} | all-to-all | bytes 524288 | tf_op jit(solution)/shard_map/all_to_all | solution.py:500
  87.1 0.6 collective-permute-start.21
  87.8 0.0 collective-permute-done.19.refs_6_
  87.8 0.0 collective-permute-done.20.refs_7_
  87.8 7.2 %shard_map.79 = (bf16[4,1024,128]{2,1,0:T(8,128)(2,1)S(1)}, f32[8,8]{1,0:T(8,128)}, f32[256,512]{1,0:T(8,128)S(1)}) custom-call(s32[8]{0:T(128)S(1)} %bitcast.32, s32[4]{0:T(128)S(1)} %pad_add_fusion.place_ref, f32[8,64,128]{2,1,0:T(8,128)S(1)} %all_to_all.25.mean_ref, bf16[1024,128]{1,0:T(8,128)(2,1)S(1)} %bitcast.25, ...), custom_call_target="tpu_custom_call" | custom-call | flops 8589934592 | bytes 8388608 | tf_op jit(solution)/shard_map/pallas_call | solution.py:337
  95.0 16.9 %all_to_all.26.d_ref = bf16[4,1024,128]{2,1,0:T(8,128)(2,1)S(1)} all-to-all(bf16[4,1024,128]{2,1,0:T(8,128)(2,1)S(1)} %get-tuple-element.41), channel_id=1, replica_groups=mesh['xh'=2,'z'=4,'xl'=2,'y'=4,'core'=2] {'z'}, dimensions={0} | all-to-all | bytes 2097152 | tf_op jit(solution)/shard_map/all_to_all | solution.py:504
  112.0 0.2 collective-permute-done.21.far_ref
  112.1 3.1 %shard_map.80 = (f32[16,40,512]{2,1,0:T(8,128)S(1)}, bf16[16,40,512]{2,1,0:T(8,128)(2,1)S(1)}) custom-call(s32[4]{0:T(128)S(1)} %pad_add_fusion.place_ref, bf16[4,128,1024]{2,1,0:T(8,128)(2,1)S(1)} %all-to-all-done.h_ref, bf16[4,128,1024]{2,1,0:T(8,128)(2,1)S(1)} %collective-permute-done.21.far_ref, bf16[4,1024,128]{2,1,0:T(8,128)(2,1)S(1)} %all_to_all.26.d_ref, ...), custom_call_target="tpu_custom_call" | custom-call | tf_op jit(solution)/shard_map/pallas_call | solution.py:388
  115.2 0.1 collective-permute-start.22
  115.3 2.1 %collective-permute-done.22 = bf16[16,40,512]{2,1,0:T(8,128)(2,1)S(1)} collective-permute-done((bf16[16,40,512]{2,1,0:T(8,128)(2,1)S(1)}, bf16[16,40,512]{2,1,0:T(8,128)(2,1)S(1)}, u32[]{:S(2)}, u32[]{:S(2)}) %collective-permute-start.22) | collective-permute-done | bytes 655392 | tf_op jit(solution)/shard_map/ppermute | solution.py:507
  117.4 0.2 add_convert_fusion
  117.6 16.3 %all_to_all.27.got_ref = bf16[16,40,512]{2,1,0:T(8,128)(2,1)S(1)} all-to-all(bf16[16,40,512]{2,1,0:T(8,128)(2,1)S(1)} %add_convert_fusion), channel_id=1, replica_groups=mesh['xh'=2,'z'=4,'xl'=2,'y'=4,'core'=2] {'xh','xl','y'}, dimensions={0} | all-to-all | bytes 1310720 | tf_op jit(solution)/shard_map/all_to_all | solution.py:509
  133.9 0.7 shard_map.81
  (20 shorter events, 0.2 us)
Async XLA Ops:
  2.2 3.5 %collective-permute-start = (bf16[40,512]{1,0:T(8,128)(2,1)S(1)}, bf16[40,512]{1,0:T(8,128)(2,1)S(1)}, u32[]{:S(2)}, u32[]{:S(2)}) collective-permute-start(bf16[40,512]{1,0:T(8,128)(2,1)S(1)} %broadcast_select_fusion.2), channel_id=1, source_target_pairs={{0,1},{1,0},{2,3},{3,2},{4,5},{5,4},{6,7},{7,6},{8,9},{9,8},{10,11... | collective-permute-start | bytes 122888 | tf_op jit(solution)/shard_map/ppermute | solution.py:446
  5.8 9.4 %collective-permute-start.3 = (bf16[16,512]{1,0:T(8,128)(2,1)S(1)}, bf16[16,512]{1,0:T(8,128)(2,1)S(1)}, u32[]{:S(2)}, u32[]{:S(2)}) collective-permute-start(bf16[16,512]{1,0:T(8,128)(2,1)S(1)} %slice_bitcast_fusion), channel_id=1, source_target_pairs={{0,48},{16,0},{32,16},{48,32},{1,49},{17,1},{33,17},{49,33},{2,50}... | collective-permute-start | bytes 49160 | tf_op jit(solution)/shard_map/ppermute | solution.py:469
  10.0 5.2 %collective-permute-start.2 = (bf16[16,512]{1,0:T(8,128)(2,1)S(1)}, bf16[16,512]{1,0:T(8,128)(2,1)S(1)}, u32[]{:S(2)}, u32[]{:S(2)}) collective-permute-start(bf16[16,512]{1,0:T(8,128)(2,1)S(1)} %slice_bitcast_fusion), channel_id=1, source_target_pairs={{0,32},{16,48},{32,0},{48,16},{1,33},{17,49},{33,1},{49,17},{2,34}... | collective-permute-start | bytes 49160 | tf_op jit(solution)/shard_map/ppermute | solution.py:469
  10.0 4.9 %collective-permute-start.1 = (bf16[16,512]{1,0:T(8,128)(2,1)S(1)}, bf16[16,512]{1,0:T(8,128)(2,1)S(1)}, u32[]{:S(2)}, u32[]{:S(2)}) collective-permute-start(bf16[16,512]{1,0:T(8,128)(2,1)S(1)} %slice_bitcast_fusion), channel_id=1, source_target_pairs={{0,16},{16,32},{32,48},{48,0},{1,17},{17,33},{33,49},{49,1},{2,18}... | collective-permute-start | bytes 49160 | tf_op jit(solution)/shard_map/ppermute | solution.py:469
  15.2 7.7 %collective-permute-start.6 = (bf16[128,512]{1,0:T(8,128)(2,1)S(1)}, bf16[128,512]{1,0:T(8,128)(2,1)S(1)}, u32[]{:S(2)}, u32[]{:S(2)}) collective-permute-start(bf16[128,512]{1,0:T(8,128)(2,1)S(1)} %constant_dynamic-update-slice_fusion.2), channel_id=1, source_target_pairs={{0,72},{8,64},{64,8},{72,0},{1,73},{9,65},{65,9},{73,1},{2,74},{10... | collective-permute-start | bytes 393224 | tf_op jit(solution)/shard_map/ppermute | solution.py:455
  18.1 7.1 %collective-permute-start.5 = (bf16[128,512]{1,0:T(8,128)(2,1)S(1)}, bf16[128,512]{1,0:T(8,128)(2,1)S(1)}, u32[]{:S(2)}, u32[]{:S(2)}) collective-permute-start(bf16[128,512]{1,0:T(8,128)(2,1)S(1)} %constant_dynamic-update-slice_fusion.2), channel_id=1, source_target_pairs={{0,64},{8,72},{64,0},{72,8},{1,65},{9,73},{65,1},{73,9},{2,66},{10... | collective-permute-start | bytes 393224 | tf_op jit(solution)/shard_map/ppermute | solution.py:455
  18.9 6.4 %collective-permute-start.4 = (bf16[128,512]{1,0:T(8,128)(2,1)S(1)}, bf16[128,512]{1,0:T(8,128)(2,1)S(1)}, u32[]{:S(2)}, u32[]{:S(2)}) collective-permute-start(bf16[128,512]{1,0:T(8,128)(2,1)S(1)} %constant_dynamic-update-slice_fusion.2), channel_id=1, source_target_pairs={{0,8},{8,0},{64,72},{72,64},{1,9},{9,1},{65,73},{73,65},{2,10},{10... | collective-permute-start | bytes 393224 | tf_op jit(solution)/shard_map/ppermute | solution.py:455
  19.4 22.8 %all-to-all-start = ((bf16[4,128,1024]{2,1,0:T(8,128)(2,1)}), bf16[4,128,1024]{2,1,0:T(8,128)(2,1)S(1)}, u32[]{:S(2)}, u32[]{:S(2)}) async-start(bf16[4,128,1024]{2,1,0:T(8,128)(2,1)} %shard_map.76), calls=%async_computation | async-start | bytes 2097152 | tf_op jit(solution)/shard_map/all_to_all | solution.py:490
  25.4 11.5 %collective-permute-start.9 = (bf16[2,2,64,512]{3,2,1,0:T(8,128)(2,1)S(1)}, bf16[2,2,64,512]{3,2,1,0:T(8,128)(2,1)S(1)}, u32[]{:S(2)}, u32[]{:S(2)}) collective-permute-start(bf16[2,2,64,512]{3,2,1,0:T(8,128)(2,1)S(1)} %get-tuple-element.48.refs_0_), channel_id=1, source_target_pairs={{0,6},{2,0},{4,2},{6,4},{1,7},{3,1},{5,3},{7,5},{8,14},{10,8},{12,... | collective-permute-start | bytes 786440 | tf_op jit(solution)/shard_map/ppermute | solution.py:469
  28.5 9.5 %collective-permute-start.8 = (bf16[2,2,64,512]{3,2,1,0:T(8,128)(2,1)S(1)}, bf16[2,2,64,512]{3,2,1,0:T(8,128)(2,1)S(1)}, u32[]{:S(2)}, u32[]{:S(2)}) collective-permute-start(bf16[2,2,64,512]{3,2,1,0:T(8,128)(2,1)S(1)} %get-tuple-element.48.refs_0_), channel_id=1, source_target_pairs={{0,4},{2,6},{4,0},{6,2},{1,5},{3,7},{5,1},{7,3},{8,12},{10,14},{12... | collective-permute-start | bytes 786440 | tf_op jit(solution)/shard_map/ppermute | solution.py:469
  29.1 11.5 %collective-permute-start.7 = (bf16[2,2,64,512]{3,2,1,0:T(8,128)(2,1)S(1)}, bf16[2,2,64,512]{3,2,1,0:T(8,128)(2,1)S(1)}, u32[]{:S(2)}, u32[]{:S(2)}) collective-permute-start(bf16[2,2,64,512]{3,2,1,0:T(8,128)(2,1)S(1)} %get-tuple-element.48.refs_0_), channel_id=1, source_target_pairs={{0,2},{2,4},{4,6},{6,0},{1,3},{3,5},{5,7},{7,1},{8,10},{10,12},{12... | collective-permute-start | bytes 786440 | tf_op jit(solution)/shard_map/ppermute | solution.py:469
  30.1 10.6 %collective-permute-start.10 = (bf16[2,2,64,512]{3,2,1,0:T(8,128)(2,1)S(1)}, bf16[2,2,64,512]{3,2,1,0:T(8,128)(2,1)S(1)}, u32[]{:S(2)}, u32[]{:S(2)}) collective-permute-start(bf16[2,2,64,512]{3,2,1,0:T(8,128)(2,1)S(1)} %get-tuple-element.48.refs_0_), channel_id=1, source_target_pairs={{0,1},{1,0},{2,3},{3,2},{4,5},{5,4},{6,7},{7,6},{8,9},{9,8},{10,11... | collective-permute-start | bytes 786440 | tf_op jit(solution)/shard_map/ppermute | solution.py:463
  36.9 3.8 %collective-permute-start.13 = (bf16[2,2,64,512]{3,2,1,0:T(8,128)(2,1)S(1)}, bf16[2,2,64,512]{3,2,1,0:T(8,128)(2,1)S(1)}, u32[]{:S(2)}, u32[]{:S(2)}) collective-permute-start(bf16[2,2,64,512]{3,2,1,0:T(8,128)(2,1)S(1)} %collective-permute-done.9.refs_3_), channel_id=1, source_target_pairs={{0,1},{1,0},{2,3},{3,2},{4,5},{5,4},{6,7},{7,6},{8,9},{9,8},{10,11... | collective-permute-start | bytes 786440 | tf_op jit(solution)/shard_map/ppermute | solution.py:463
  38.0 2.8 %collective-permute-start.12 = (bf16[2,2,64,512]{3,2,1,0:T(8,128)(2,1)S(1)}, bf16[2,2,64,512]{3,2,1,0:T(8,128)(2,1)S(1)}, u32[]{:S(2)}, u32[]{:S(2)}) collective-permute-start(bf16[2,2,64,512]{3,2,1,0:T(8,128)(2,1)S(1)} %collective-permute-done.8.refs_2_), channel_id=1, source_target_pairs={{0,1},{1,0},{2,3},{3,2},{4,5},{5,4},{6,7},{7,6},{8,9},{9,8},{10,11... | collective-permute-start | bytes 786440 | tf_op jit(solution)/shard_map/ppermute | solution.py:463
  40.6 1.5 %collective-permute-start.11 = (bf16[2,2,64,512]{3,2,1,0:T(8,128)(2,1)S(1)}, bf16[2,2,64,512]{3,2,1,0:T(8,128)(2,1)S(1)}, u32[]{:S(2)}, u32[]{:S(2)}) collective-permute-start(bf16[2,2,64,512]{3,2,1,0:T(8,128)(2,1)S(1)} %collective-permute-done.7.refs_1_), channel_id=1, source_target_pairs={{0,1},{1,0},{2,3},{3,2},{4,5},{5,4},{6,7},{7,6},{8,9},{9,8},{10,11... | collective-permute-start | bytes 786440 | tf_op jit(solution)/shard_map/ppermute | solution.py:463
  45.7 22.0 %copy-start = (s32[1,8]{1,0:T(1,128)S(1)}, s32[1,8]{1,0:T(1,128)}, u32[]{:S(2)}) copy-start(s32[1,8]{1,0:T(1,128)} %param.8) | copy-start | bytes 100
  45.7 21.8 %all-to-all-start.1 = ((f16[8,512,128]{2,1,0:T(8,128)(2,1)}), f16[8,512,128]{2,1,0:T(8,128)(2,1)S(1)}, u32[]{:S(2)}, u32[]{:S(2)}) async-start(f16[8,512,128]{2,1,0:T(8,128)(2,1)} %multiply_convert_fusion), calls=%async_computation.1 | async-start | bytes 2097152 | tf_op jit(solution)/shard_map/all_to_all | solution.py:494
  51.6 21.2 %collective-permute-start.16 = (bf16[2,2,4,16,512]{4,3,2,1,0:T(8,128)(2,1)S(1)}, bf16[2,2,4,16,512]{4,3,2,1,0:T(8,128)(2,1)S(1)}, u32[]{:S(2)}, u32[]{:S(2)}) collective-permute-start(bf16[2,2,4,16,512]{4,3,2,1,0:T(8,128)(2,1)S(1)} %bitcast.26), channel_id=1, source_target_pairs={{0,6},{2,0},{4,2},{6,4},{1,7},{3,1},{5,3},{7,5},{8,14},{10,8},{12,... | collective-permute-start | bytes 786440 | tf_op jit(solution)/shard_map/ppermute | solution.py:469
  52.4 20.5 %collective-permute-start.15 = (bf16[2,2,4,16,512]{4,3,2,1,0:T(8,128)(2,1)S(1)}, bf16[2,2,4,16,512]{4,3,2,1,0:T(8,128)(2,1)S(1)}, u32[]{:S(2)}, u32[]{:S(2)}) collective-permute-start(bf16[2,2,4,16,512]{4,3,2,1,0:T(8,128)(2,1)S(1)} %bitcast.27), channel_id=1, source_target_pairs={{0,4},{2,6},{4,0},{6,2},{1,5},{3,7},{5,1},{7,3},{8,12},{10,14},{12... | collective-permute-start | bytes 786440 | tf_op jit(solution)/shard_map/ppermute | solution.py:469
  52.8 20.0 %collective-permute-start.14 = (bf16[2,2,4,16,512]{4,3,2,1,0:T(8,128)(2,1)S(1)}, bf16[2,2,4,16,512]{4,3,2,1,0:T(8,128)(2,1)S(1)}, u32[]{:S(2)}, u32[]{:S(2)}) collective-permute-start(bf16[2,2,4,16,512]{4,3,2,1,0:T(8,128)(2,1)S(1)} %bitcast.28), channel_id=1, source_target_pairs={{0,2},{2,4},{4,6},{6,0},{1,3},{3,5},{5,7},{7,1},{8,10},{10,12},{12... | collective-permute-start | bytes 786440 | tf_op jit(solution)/shard_map/ppermute | solution.py:469
  67.7 20.1 %copy-start.1 = (s32[1,28]{1,0:T(1,128)S(1)}, s32[1,28]{1,0:T(1,128)}, u32[]{:S(2)}) copy-start(s32[1,28]{1,0:T(1,128)} %label_ref.1) | copy-start | bytes 340
  72.9 14.9 %collective-permute-start.17 = (bf16[2,2,4,16,512]{4,3,2,1,0:T(8,128)(2,1)S(1)}, bf16[2,2,4,16,512]{4,3,2,1,0:T(8,128)(2,1)S(1)}, u32[]{:S(2)}, u32[]{:S(2)}) collective-permute-start(bf16[2,2,4,16,512]{4,3,2,1,0:T(8,128)(2,1)S(1)} %bitcast.29), channel_id=1, source_target_pairs={{0,1},{1,0},{2,3},{3,2},{4,5},{5,4},{6,7},{7,6},{8,9},{9,8},{10,11... | collective-permute-start | bytes 786440 | tf_op jit(solution)/shard_map/ppermute | solution.py:463
  73.0 14.8 %collective-permute-start.18 = (bf16[2,2,4,16,512]{4,3,2,1,0:T(8,128)(2,1)S(1)}, bf16[2,2,4,16,512]{4,3,2,1,0:T(8,128)(2,1)S(1)}, u32[]{:S(2)}, u32[]{:S(2)}) collective-permute-start(bf16[2,2,4,16,512]{4,3,2,1,0:T(8,128)(2,1)S(1)} %collective-permute-done.14.refs_1_), channel_id=1, source_target_pairs={{0,1},{1,0},{2,3},{3,2},{4,5},{5,4},{6,7},{7,6},{8,9},{9,8},{10,11... | collective-permute-start | bytes 786440 | tf_op jit(solution)/shard_map/ppermute | solution.py:463
  73.5 14.3 %collective-permute-start.19 = (bf16[2,2,4,16,512]{4,3,2,1,0:T(8,128)(2,1)S(1)}, bf16[2,2,4,16,512]{4,3,2,1,0:T(8,128)(2,1)S(1)}, u32[]{:S(2)}, u32[]{:S(2)}) collective-permute-start(bf16[2,2,4,16,512]{4,3,2,1,0:T(8,128)(2,1)S(1)} %collective-permute-done.15.refs_2_), channel_id=1, source_target_pairs={{0,1},{1,0},{2,3},{3,2},{4,5},{5,4},{6,7},{7,6},{8,9},{9,8},{10,11... | collective-permute-start | bytes 786440 | tf_op jit(solution)/shard_map/ppermute | solution.py:463
  73.6 14.2 %collective-permute-start.20 = (bf16[2,2,4,16,512]{4,3,2,1,0:T(8,128)(2,1)S(1)}, bf16[2,2,4,16,512]{4,3,2,1,0:T(8,128)(2,1)S(1)}, u32[]{:S(2)}, u32[]{:S(2)}) collective-permute-start(bf16[2,2,4,16,512]{4,3,2,1,0:T(8,128)(2,1)S(1)} %collective-permute-done.16.refs_3_), channel_id=1, source_target_pairs={{0,1},{1,0},{2,3},{3,2},{4,5},{5,4},{6,7},{7,6},{8,9},{9,8},{10,11... | collective-permute-start | bytes 786440 | tf_op jit(solution)/shard_map/ppermute | solution.py:463
  87.1 25.0 %collective-permute-start.21 = (bf16[4,128,1024]{2,1,0:T(8,128)(2,1)S(1)}, bf16[4,128,1024]{2,1,0:T(8,128)(2,1)S(1)}, u32[]{:S(2)}, u32[]{:S(2)}) collective-permute-start(bf16[4,128,1024]{2,1,0:T(8,128)(2,1)S(1)} %all-to-all-done.h_ref), channel_id=1, source_target_pairs={{0,64},{64,0},{1,65},{65,1},{2,66},{66,2},{3,67},{67,3},{4,68},{68... | collective-permute-start | bytes 3145736 | tf_op jit(solution)/shard_map/ppermute | solution.py:502
  115.2 2.2 %collective-permute-start.22 = (bf16[16,40,512]{2,1,0:T(8,128)(2,1)S(1)}, bf16[16,40,512]{2,1,0:T(8,128)(2,1)S(1)}, u32[]{:S(2)}, u32[]{:S(2)}) collective-permute-start(bf16[16,40,512]{2,1,0:T(8,128)(2,1)S(1)} %get-tuple-element.44), channel_id=1, source_target_pairs={{0,1},{1,0},{2,3},{3,2},{4,5},{5,4},{6,7},{7,6},{8,9},{9,8},{10,11... | collective-permute-start | bytes 1966088 | tf_op jit(solution)/shard_map/ppermute | solution.py:507

commit v5 on v4

--- a/solution.py
+++ b/solution.py
@@ -479,14 +479,12 @@
     w = gather_core(jnp.concatenate([proj_weight, bilinear], axis=0))
     w = w.reshape(2, -1, w.shape[1])
     w, bil = (v.reshape(-1, v.shape[2]) for v in (w[:, :rows], w[:, rows:]))
-    bil = around(bil, "z")
-    rows = w.shape[0]
-    w = jnp.concatenate([w] + bil, axis=0)
+    w = gather_x(w)
+    bil = jnp.stack(around(bil, "z"))
     h = pack(hidden_states[0, 0])
-    h, w = lax.optimization_barrier((h, w))
-    w = gather_x(w)
-    bil = w[:, :, rows:].reshape(2, 2, len(bil), -1, w.shape[3])
-    w = with_other_core(around(w[:, :, :rows], "y"))
+    h, bil = lax.optimization_barrier((h, bil))
+    w = with_other_core(around(w, "y"))
+    bil = gather_x(bil)
     h = lax.all_to_all(h, "z", 0, 0)
     parts = (project(place, h, w) * SCALE).astype(jnp.float16)
     parts, bil = lax.optimization_barrier((parts, bil))

time: 135 us -> 133 us (0.985)
  waiting for transfers between devices: 34.3 us -> 27.4 us
  starting transfers between devices: 27.7 us -> 31.9 us
    ppermute x9, waiting for transfers between devices: 14.5 us -> 3.15 us  [around(): lax.ppermute(value, axis, [(i, (i + k) % count) for i in range(count)])]
    ppermute x3 -> x6, waiting for transfers between devices: 2.26 us -> 5.75 us  [gather_x(): lax.ppermute(value, ('xh', 'xl'), [(i, i ^ flip) for i in range(4)])]
    ppermute x3 -> x6, starting transfers between devices: 4.17 us -> 6.9 us  [gather_x(): lax.ppermute(value, ('xh', 'xl'), [(i, i ^ flip) for i in range(4)])]
  transfers between devices with their start and end apart: 25 -> 28, of which waited for: 10 -> 9; matrix products, arithmetic and copies ran while one was open for 0% -> 0% of each run, Pallas kernels for 12% -> 12%
where the time goes in v5:
time: 133 us; the launch traced here: 132 us
  blocking collectives  46.7 us (35%)
  starting transfers between devices  31.9 us (24%)
  waiting for transfers between devices  27.4 us (21%)
  Pallas kernels  21.8 us (16%)
  other arithmetic  1.87 us (1%)
  local copies, waits for them, and re-layouts  1.58 us (1%)
    all_to_all x1, blocking collectives, body(): drows = lax.all_to_all(drows, 'z', 0, 0)  17.3 us
    all_to_all x1, blocking collectives, body(): got = lax.all_to_all(sent, ('xh', 'xl', 'y'), 0, 0)  16.1 us
    all_to_all x1, waiting for transfers between devices, body(): parts = lax.all_to_all(parts, CAND, 0, 0)  13.8 us
    all_to_all x1, blocking collectives, body(): means = lax.all_to_all(means, CAND, 0, 0)  13.3 us
    ppermute x9, starting transfers between devices, around(): lax.ppermute(value, axis, [(i, (i + k) % count) for i in range(count)])  12.2 us
    pallas_call x1, Pallas kernels, backward(): pl.pallas_call(backward_kernel, out_shape=(jax.ShapeDtypeStruct((CANDS //...  7.24 us
    ppermute x6, starting transfers between devices, gather_x(): lax.ppermute(value, ('xh', 'xl'), [(i, i ^ flip) for i in range(4)])  6.9 us
    all_to_all x1, starting transfers between devices, body(): parts = lax.all_to_all(parts, CAND, 0, 0)  6.86 us
  transfers between devices with their start and end apart: 28, of which 9 were waited for; matrix products, arithmetic and copies ran while one was open for 0% of the time, Pallas kernels for 12%

profile of v5, /device:TPU:0, one launch (start us, length us, event | category | flops | bytes accessed | tf_op | source)
XLA Modules:
  0.0 132.3 jit_solution(17948228422642875322)
XLA Ops:
  0.6 0.8 constant_dynamic-update-slice_fusion.1
  1.5 0.7 constant_dynamic-update-slice_fusion
  2.2 0.1 collective-permute-start
  2.3 1.2 collective-permute-done
  3.6 4.2 %collective-permute-start.3 = (bf16[16,512]{1,0:T(8,128)(2,1)S(1)}, bf16[16,512]{1,0:T(8,128)(2,1)S(1)}, u32[]{:S(2)}, u32[]{:S(2)}) collective-permute-start(bf16[16,512]{1,0:T(8,128)(2,1)S(1)} %get-tuple-element.50), channel_id=1, source_target_pairs={{0,48},{16,0},{32,16},{48,32},{1,49},{17,1},{33,17},{49,33},{2,50}... | collective-permute-start | bytes 49160 | tf_op jit(solution)/shard_map/ppermute | solution.py:469
  7.7 0.0 collective-permute-start.2
  7.7 1.3 collective-permute-start.1
  9.0 3.4 %shard_map.76 = bf16[4,128,1024]{2,1,0:T(8,128)(2,1)} custom-call(bf16[128,4096]{1,0:T(8,128)(2,1)} %bitcast.34, bf16[128,4096]{1,0:T(8,128)(2,1)} %bitcast.35), custom_call_target="tpu_custom_call" | custom-call | tf_op jit(solution)/shard_map/pallas_call | solution.py:55
  12.4 2.8 %collective-permute-start.6 = (bf16[64,512]{1,0:T(8,128)(2,1)S(1)}, bf16[64,512]{1,0:T(8,128)(2,1)S(1)}, u32[]{:S(2)}, u32[]{:S(2)}) collective-permute-start(bf16[64,512]{1,0:T(8,128)(2,1)S(1)} %bitcast.39), channel_id=1, source_target_pairs={{0,72},{8,64},{64,8},{72,0},{1,73},{9,65},{65,9},{73,1},{2,74},{10... | collective-permute-start | bytes 196616 | tf_op jit(solution)/shard_map/ppermute | solution.py:455
  15.3 0.8 collective-permute-start.5
  16.1 0.0 collective-permute-done.3
  16.1 0.5 collective-permute-start.4
  16.6 0.0 collective-permute-done.2
  16.6 0.0 collective-permute-done.1
  16.6 3.6 %all-to-all-start = ((bf16[4,128,1024]{2,1,0:T(8,128)(2,1)}), bf16[4,128,1024]{2,1,0:T(8,128)(2,1)S(1)}, u32[]{:S(2)}, u32[]{:S(2)}) async-start(bf16[4,128,1024]{2,1,0:T(8,128)(2,1)} %shard_map.76), calls=%async_computation | async-start | bytes 2097152 | tf_op jit(solution)/shard_map/all_to_all | solution.py:488
  20.2 0.0 collective-permute-done.6
  20.2 0.8 collective-permute-done.5
  21.1 0.0 collective-permute-done.4
  21.1 3.1 %collective-permute-start.9 = (bf16[2,2,64,512]{3,2,1,0:T(8,128)(2,1)S(1)}, bf16[2,2,64,512]{3,2,1,0:T(8,128)(2,1)S(1)}, u32[]{:S(2)}, u32[]{:S(2)}) collective-permute-start(bf16[2,2,64,512]{3,2,1,0:T(8,128)(2,1)S(1)} %maximum_select_fusion.refs_0_), channel_id=1, source_target_pairs={{0,6},{2,0},{4,2},{6,4},{1,7},{3,1},{5,3},{7,5},{8,14},{10,8},{12,... | collective-permute-start | bytes 786440 | tf_op jit(solution)/shard_map/ppermute | solution.py:469
  24.2 0.6 collective-permute-start.8
  24.8 1.0 collective-permute-start.7
  25.8 1.9 %collective-permute-start.16 = (bf16[4,16,512]{2,1,0:T(8,128)(2,1)S(1)}, bf16[4,16,512]{2,1,0:T(8,128)(2,1)S(1)}, u32[]{:S(2)}, u32[]{:S(2)}) collective-permute-start(bf16[4,16,512]{2,1,0:T(8,128)(2,1)S(1)} %pad_maximum_fusion.1), channel_id=1, source_target_pairs={{0,72},{8,64},{64,8},{72,0},{1,73},{9,65},{65,9},{73,1},{2,74},{10... | collective-permute-start | bytes 196616 | tf_op jit(solution)/shard_map/ppermute | solution.py:455
  27.7 0.8 collective-permute-start.15
  28.5 0.1 pad_add_fusion.place_ref
  28.6 2.7 %collective-permute-done.16 = bf16[4,16,512]{2,1,0:T(8,128)(2,1)S(1)} collective-permute-done((bf16[4,16,512]{2,1,0:T(8,128)(2,1)S(1)}, bf16[4,16,512]{2,1,0:T(8,128)(2,1)S(1)}, u32[]{:S(2)}, u32[]{:S(2)}) %collective-permute-start.16) | collective-permute-done | bytes 65568 | tf_op jit(solution)/shard_map/ppermute | solution.py:455
  31.3 2.2 %collective-permute-done.15 = bf16[4,16,512]{2,1,0:T(8,128)(2,1)S(1)} collective-permute-done((bf16[4,16,512]{2,1,0:T(8,128)(2,1)S(1)}, bf16[4,16,512]{2,1,0:T(8,128)(2,1)S(1)}, u32[]{:S(2)}, u32[]{:S(2)}) %collective-permute-start.15) | collective-permute-done | bytes 65568 | tf_op jit(solution)/shard_map/ppermute | solution.py:455
  33.5 0.5 collective-permute-start.13
  34.0 0.4 collective-permute-done.8.refs_2_
  34.4 2.7 %collective-permute-done.7.refs_1_ = bf16[2,2,64,512]{3,2,1,0:T(8,128)(2,1)S(1)} collective-permute-done((bf16[2,2,64,512]{3,2,1,0:T(8,128)(2,1)S(1)}, bf16[2,2,64,512]{3,2,1,0:T(8,128)(2,1)S(1)}, u32[]{:S(2)}, u32[]{:S(2)}) %collective-permute-start.7) | collective-permute-done | bytes 262176 | tf_op jit(solution)/shard_map/ppermute | solution.py:469
  37.2 0.0 collective-permute-done.14
  37.3 0.0 collective-permute-done.13.refs_7_
  37.3 0.0 collective-permute-done.12.refs_6_
  37.3 1.4 %collective-permute-done.11.refs_5_ = bf16[2,2,64,512]{3,2,1,0:T(8,128)(2,1)S(1)} collective-permute-done((bf16[2,2,64,512]{3,2,1,0:T(8,128)(2,1)S(1)}, bf16[2,2,64,512]{3,2,1,0:T(8,128)(2,1)S(1)}, u32[]{:S(2)}, u32[]{:S(2)}) %collective-permute-start.11) | collective-permute-done | bytes 262176 | tf_op jit(solution)/shard_map/ppermute | solution.py:463
  38.7 2.3 %shard_map.77 = f32[8,512,128]{2,1,0:T(8,128)S(1)} custom-call(s32[4]{0:T(128)S(1)} %pad_add_fusion.place_ref, bf16[4,128,1024]{2,1,0:T(8,128)(2,1)S(1)} %all-to-all-done.h_ref, bf16[2,2,64,512]{3,2,1,0:T(8,128)(2,1)S(1)} %maximum_select_fusion.refs_0_, bf16[2,2,64,512]{3,2,1,0:T(8,128)(2,1)S(1)} %collective-permute-done.7.refs_1_, ...), custom_call_target="tpu_custom_call" | custom-call | tf_op jit(solution)/shard_map/pallas_call | solution.py:95
  41.0 1.2 multiply_convert_fusion
  42.2 6.9 %all-to-all-start.1 = ((f16[8,512,128]{2,1,0:T(8,128)(2,1)}), f16[8,512,128]{2,1,0:T(8,128)(2,1)S(1)}, u32[]{:S(2)}, u32[]{:S(2)}) async-start(f16[8,512,128]{2,1,0:T(8,128)(2,1)} %multiply_convert_fusion), calls=%async_computation.1 | async-start | bytes 2097152 | tf_op jit(solution)/shard_map/all_to_all | solution.py:492
  49.1 0.7 collective-permute-start.19
  49.8 0.5 collective-permute-start.18
  50.3 0.8 collective-permute-start.17
  51.1 13.8 %all-to-all-done.1 = f16[8,512,128]{2,1,0:T(8,128)(2,1)S(1)} async-done(((f16[8,512,128]{2,1,0:T(8,128)(2,1)}), f16[8,512,128]{2,1,0:T(8,128)(2,1)S(1)}, u32[]{:S(2)}, u32[]{:S(2)}) %all-to-all-start.1) | async-done | bytes 1048608 | tf_op jit(solution)/shard_map/all_to_all | solution.py:492
  64.9 0.1 convert_reduce_fusion
  65.1 0.0 copy-start.1
  65.2 5.1 %shard_map.78 = (bf16[128,1024]{1,0:T(8,128)(2,1)S(1)}, f32[8,64,128]{2,1,0:T(8,128)S(1)}, f32[2,8,1024]{2,1,0:T(8,128)S(1)}, f32[64,256]{1,0:T(8,128)S(1)}) custom-call(s32[8]{0:T(128)S(1)} %bitcast.32, bf16[1024,128]{1,0:T(8,128)(2,1)S(1)} %bitcast.30), custom_call_target="tpu_custom_call" | custom-call | flops 12884901888 | bytes 16777216 | tf_op jit(solution)/shard_map/pallas_call | solution.py:188
  70.3 0.0 collective-permute-done.18.refs_2_
  70.3 0.0 collective-permute-done.17.refs_1_
  70.3 0.1 collective-permute-start.20
  70.4 0.5 collective-permute-start.21
  70.9 0.3 collective-permute-start.22
  71.2 0.2 collective-permute-start.23
  71.4 13.3 %all_to_all.25.mean_ref = f32[8,64,128]{2,1,0:T(8,128)S(1)} all-to-all(f32[8,64,128]{2,1,0:T(8,128)S(1)} %get-tuple-element.30), channel_id=1, replica_groups=mesh['xh'=2,'z'=4,'xl'=2,'y'=4,'core'=2] {'xh','z'}, dimensions={0} | all-to-all | bytes 524288 | tf_op jit(solution)/shard_map/all_to_all | solution.py:498
  84.7 0.6 collective-permute-start.24
  85.4 0.0 collective-permute-done.20.refs_4_
  85.4 0.0 collective-permute-done.21.refs_5_
  85.4 0.0 collective-permute-done.22.refs_6_
  85.4 0.0 collective-permute-done.23.refs_7_
  85.4 7.2 %shard_map.79 = (bf16[4,1024,128]{2,1,0:T(8,128)(2,1)S(1)}, f32[8,8]{1,0:T(8,128)}, f32[256,512]{1,0:T(8,128)S(1)}) custom-call(s32[8]{0:T(128)S(1)} %bitcast.33, s32[4]{0:T(128)S(1)} %pad_add_fusion.place_ref, f32[8,64,128]{2,1,0:T(8,128)S(1)} %all_to_all.25.mean_ref, bf16[1024,128]{1,0:T(8,128)(2,1)S(1)} %bitcast.31, ...), custom_call_target="tpu_custom_call" | custom-call | flops 8589934592 | bytes 8388608 | tf_op jit(solution)/shard_map/pallas_call | solution.py:337
  92.6 17.3 %all_to_all.26.d_ref = bf16[4,1024,128]{2,1,0:T(8,128)(2,1)S(1)} all-to-all(bf16[4,1024,128]{2,1,0:T(8,128)(2,1)S(1)} %get-tuple-element.41), channel_id=1, replica_groups=mesh['xh'=2,'z'=4,'xl'=2,'y'=4,'core'=2] {'z'}, dimensions={0} | all-to-all | bytes 2097152 | tf_op jit(solution)/shard_map/all_to_all | solution.py:502
  110.0 0.0 collective-permute-done.24.far_ref
  110.0 3.1 %shard_map.80 = (f32[16,40,512]{2,1,0:T(8,128)S(1)}, bf16[16,40,512]{2,1,0:T(8,128)(2,1)S(1)}) custom-call(s32[4]{0:T(128)S(1)} %pad_add_fusion.place_ref, bf16[4,128,1024]{2,1,0:T(8,128)(2,1)S(1)} %all-to-all-done.h_ref, bf16[4,128,1024]{2,1,0:T(8,128)(2,1)S(1)} %collective-permute-done.24.far_ref, bf16[4,1024,128]{2,1,0:T(8,128)(2,1)S(1)} %all_to_all.26.d_ref, ...), custom_call_target="tpu_custom_call" | custom-call | tf_op jit(solution)/shard_map/pallas_call | solution.py:388
  113.1 0.1 collective-permute-start.25
  113.2 2.1 %collective-permute-done.25 = bf16[16,40,512]{2,1,0:T(8,128)(2,1)S(1)} collective-permute-done((bf16[16,40,512]{2,1,0:T(8,128)(2,1)S(1)}, bf16[16,40,512]{2,1,0:T(8,128)(2,1)S(1)}, u32[]{:S(2)}, u32[]{:S(2)}) %collective-permute-start.25) | collective-permute-done | bytes 655392 | tf_op jit(solution)/shard_map/ppermute | solution.py:505
  115.2 0.2 add_convert_fusion
  115.5 16.1 %all_to_all.27.got_ref = bf16[16,40,512]{2,1,0:T(8,128)(2,1)S(1)} all-to-all(bf16[16,40,512]{2,1,0:T(8,128)(2,1)S(1)} %add_convert_fusion), channel_id=1, replica_groups=mesh['xh'=2,'z'=4,'xl'=2,'y'=4,'core'=2] {'xh','xl','y'}, dimensions={0} | all-to-all | bytes 1310720 | tf_op jit(solution)/shard_map/all_to_all | solution.py:507
  131.5 0.7 shard_map.81
  (24 shorter events, 0.2 us)
Async XLA Ops:
  2.2 1.3 collective-permute-start
  3.6 12.5 %collective-permute-start.3 = (bf16[16,512]{1,0:T(8,128)(2,1)S(1)}, bf16[16,512]{1,0:T(8,128)(2,1)S(1)}, u32[]{:S(2)}, u32[]{:S(2)}) collective-permute-start(bf16[16,512]{1,0:T(8,128)(2,1)S(1)} %get-tuple-element.50), channel_id=1, source_target_pairs={{0,48},{16,0},{32,16},{48,32},{1,49},{17,1},{33,17},{49,33},{2,50}... | collective-permute-start | bytes 49160 | tf_op jit(solution)/shard_map/ppermute | solution.py:469
  7.7 8.9 %collective-permute-start.2 = (bf16[16,512]{1,0:T(8,128)(2,1)S(1)}, bf16[16,512]{1,0:T(8,128)(2,1)S(1)}, u32[]{:S(2)}, u32[]{:S(2)}) collective-permute-start(bf16[16,512]{1,0:T(8,128)(2,1)S(1)} %get-tuple-element.50), channel_id=1, source_target_pairs={{0,32},{16,48},{32,0},{48,16},{1,33},{17,49},{33,1},{49,17},{2,34}... | collective-permute-start | bytes 49160 | tf_op jit(solution)/shard_map/ppermute | solution.py:469
  7.7 8.9 %collective-permute-start.1 = (bf16[16,512]{1,0:T(8,128)(2,1)S(1)}, bf16[16,512]{1,0:T(8,128)(2,1)S(1)}, u32[]{:S(2)}, u32[]{:S(2)}) collective-permute-start(bf16[16,512]{1,0:T(8,128)(2,1)S(1)} %get-tuple-element.50), channel_id=1, source_target_pairs={{0,16},{16,32},{32,48},{48,0},{1,17},{17,33},{33,49},{49,1},{2,18}... | collective-permute-start | bytes 49160 | tf_op jit(solution)/shard_map/ppermute | solution.py:469
  12.4 7.8 %collective-permute-start.6 = (bf16[64,512]{1,0:T(8,128)(2,1)S(1)}, bf16[64,512]{1,0:T(8,128)(2,1)S(1)}, u32[]{:S(2)}, u32[]{:S(2)}) collective-permute-start(bf16[64,512]{1,0:T(8,128)(2,1)S(1)} %bitcast.39), channel_id=1, source_target_pairs={{0,72},{8,64},{64,8},{72,0},{1,73},{9,65},{65,9},{73,1},{2,74},{10... | collective-permute-start | bytes 196616 | tf_op jit(solution)/shard_map/ppermute | solution.py:455
  15.3 5.8 %collective-permute-start.5 = (bf16[64,512]{1,0:T(8,128)(2,1)S(1)}, bf16[64,512]{1,0:T(8,128)(2,1)S(1)}, u32[]{:S(2)}, u32[]{:S(2)}) collective-permute-start(bf16[64,512]{1,0:T(8,128)(2,1)S(1)} %bitcast.40), channel_id=1, source_target_pairs={{0,64},{8,72},{64,0},{72,8},{1,65},{9,73},{65,1},{73,9},{2,66},{10... | collective-permute-start | bytes 196616 | tf_op jit(solution)/shard_map/ppermute | solution.py:455
  16.1 5.0 %collective-permute-start.4 = (bf16[64,512]{1,0:T(8,128)(2,1)S(1)}, bf16[64,512]{1,0:T(8,128)(2,1)S(1)}, u32[]{:S(2)}, u32[]{:S(2)}) collective-permute-start(bf16[64,512]{1,0:T(8,128)(2,1)S(1)} %bitcast.41), channel_id=1, source_target_pairs={{0,8},{8,0},{64,72},{72,64},{1,9},{9,1},{65,73},{73,65},{2,10},{10... | collective-permute-start | bytes 196616 | tf_op jit(solution)/shard_map/ppermute | solution.py:455
  16.6 22.1 %all-to-all-start = ((bf16[4,128,1024]{2,1,0:T(8,128)(2,1)}), bf16[4,128,1024]{2,1,0:T(8,128)(2,1)S(1)}, u32[]{:S(2)}, u32[]{:S(2)}) async-start(bf16[4,128,1024]{2,1,0:T(8,128)(2,1)} %shard_map.76), calls=%async_computation | async-start | bytes 2097152 | tf_op jit(solution)/shard_map/all_to_all | solution.py:488
  21.1 12.4 %collective-permute-start.9 = (bf16[2,2,64,512]{3,2,1,0:T(8,128)(2,1)S(1)}, bf16[2,2,64,512]{3,2,1,0:T(8,128)(2,1)S(1)}, u32[]{:S(2)}, u32[]{:S(2)}) collective-permute-start(bf16[2,2,64,512]{3,2,1,0:T(8,128)(2,1)S(1)} %maximum_select_fusion.refs_0_), channel_id=1, source_target_pairs={{0,6},{2,0},{4,2},{6,4},{1,7},{3,1},{5,3},{7,5},{8,14},{10,8},{12,... | collective-permute-start | bytes 786440 | tf_op jit(solution)/shard_map/ppermute | solution.py:469
  24.2 10.2 %collective-permute-start.8 = (bf16[2,2,64,512]{3,2,1,0:T(8,128)(2,1)S(1)}, bf16[2,2,64,512]{3,2,1,0:T(8,128)(2,1)S(1)}, u32[]{:S(2)}, u32[]{:S(2)}) collective-permute-start(bf16[2,2,64,512]{3,2,1,0:T(8,128)(2,1)S(1)} %maximum_select_fusion.refs_0_), channel_id=1, source_target_pairs={{0,4},{2,6},{4,0},{6,2},{1,5},{3,7},{5,1},{7,3},{8,12},{10,14},{12... | collective-permute-start | bytes 786440 | tf_op jit(solution)/shard_map/ppermute | solution.py:469
  24.8 12.3 %collective-permute-start.7 = (bf16[2,2,64,512]{3,2,1,0:T(8,128)(2,1)S(1)}, bf16[2,2,64,512]{3,2,1,0:T(8,128)(2,1)S(1)}, u32[]{:S(2)}, u32[]{:S(2)}) collective-permute-start(bf16[2,2,64,512]{3,2,1,0:T(8,128)(2,1)S(1)} %maximum_select_fusion.refs_0_), channel_id=1, source_target_pairs={{0,2},{2,4},{4,6},{6,0},{1,3},{3,5},{5,7},{7,1},{8,10},{10,12},{12... | collective-permute-start | bytes 786440 | tf_op jit(solution)/shard_map/ppermute | solution.py:469
  25.8 5.5 %collective-permute-start.16 = (bf16[4,16,512]{2,1,0:T(8,128)(2,1)S(1)}, bf16[4,16,512]{2,1,0:T(8,128)(2,1)S(1)}, u32[]{:S(2)}, u32[]{:S(2)}) collective-permute-start(bf16[4,16,512]{2,1,0:T(8,128)(2,1)S(1)} %pad_maximum_fusion.1), channel_id=1, source_target_pairs={{0,72},{8,64},{64,8},{72,0},{1,73},{9,65},{65,9},{73,1},{2,74},{10... | collective-permute-start | bytes 196616 | tf_op jit(solution)/shard_map/ppermute | solution.py:455
  27.7 5.8 %collective-permute-start.15 = (bf16[4,16,512]{2,1,0:T(8,128)(2,1)S(1)}, bf16[4,16,512]{2,1,0:T(8,128)(2,1)S(1)}, u32[]{:S(2)}, u32[]{:S(2)}) collective-permute-start(bf16[4,16,512]{2,1,0:T(8,128)(2,1)S(1)} %pad_maximum_fusion.1), channel_id=1, source_target_pairs={{0,64},{8,72},{64,0},{72,8},{1,65},{9,73},{65,1},{73,9},{2,66},{10... | collective-permute-start | bytes 196616 | tf_op jit(solution)/shard_map/ppermute | solution.py:455
  31.3 5.9 %collective-permute-start.14 = (bf16[4,16,512]{2,1,0:T(8,128)(2,1)S(1)}, bf16[4,16,512]{2,1,0:T(8,128)(2,1)S(1)}, u32[]{:S(2)}, u32[]{:S(2)}) collective-permute-start(bf16[4,16,512]{2,1,0:T(8,128)(2,1)S(1)} %pad_maximum_fusion.1), channel_id=1, source_target_pairs={{0,8},{8,0},{64,72},{72,64},{1,9},{9,1},{65,73},{73,65},{2,10},{10... | collective-permute-start | bytes 196616 | tf_op jit(solution)/shard_map/ppermute | solution.py:455
  33.5 3.7 %collective-permute-start.10 = (bf16[2,2,64,512]{3,2,1,0:T(8,128)(2,1)S(1)}, bf16[2,2,64,512]{3,2,1,0:T(8,128)(2,1)S(1)}, u32[]{:S(2)}, u32[]{:S(2)}) collective-permute-start(bf16[2,2,64,512]{3,2,1,0:T(8,128)(2,1)S(1)} %maximum_select_fusion.refs_0_), channel_id=1, source_target_pairs={{0,1},{1,0},{2,3},{3,2},{4,5},{5,4},{6,7},{7,6},{8,9},{9,8},{10,11... | collective-permute-start | bytes 786440 | tf_op jit(solution)/shard_map/ppermute | solution.py:463
  33.5 3.8 %collective-permute-start.13 = (bf16[2,2,64,512]{3,2,1,0:T(8,128)(2,1)S(1)}, bf16[2,2,64,512]{3,2,1,0:T(8,128)(2,1)S(1)}, u32[]{:S(2)}, u32[]{:S(2)}) collective-permute-start(bf16[2,2,64,512]{3,2,1,0:T(8,128)(2,1)S(1)} %collective-permute-done.9.refs_3_), channel_id=1, source_target_pairs={{0,1},{1,0},{2,3},{3,2},{4,5},{5,4},{6,7},{7,6},{8,9},{9,8},{10,11... | collective-permute-start | bytes 786440 | tf_op jit(solution)/shard_map/ppermute | solution.py:463
  34.4 2.8 %collective-permute-start.12 = (bf16[2,2,64,512]{3,2,1,0:T(8,128)(2,1)S(1)}, bf16[2,2,64,512]{3,2,1,0:T(8,128)(2,1)S(1)}, u32[]{:S(2)}, u32[]{:S(2)}) collective-permute-start(bf16[2,2,64,512]{3,2,1,0:T(8,128)(2,1)S(1)} %collective-permute-done.8.refs_2_), channel_id=1, source_target_pairs={{0,1},{1,0},{2,3},{3,2},{4,5},{5,4},{6,7},{7,6},{8,9},{9,8},{10,11... | collective-permute-start | bytes 786440 | tf_op jit(solution)/shard_map/ppermute | solution.py:463
  37.1 1.5 %collective-permute-start.11 = (bf16[2,2,64,512]{3,2,1,0:T(8,128)(2,1)S(1)}, bf16[2,2,64,512]{3,2,1,0:T(8,128)(2,1)S(1)}, u32[]{:S(2)}, u32[]{:S(2)}) collective-permute-start(bf16[2,2,64,512]{3,2,1,0:T(8,128)(2,1)S(1)} %collective-permute-done.7.refs_1_), channel_id=1, source_target_pairs={{0,1},{1,0},{2,3},{3,2},{4,5},{5,4},{6,7},{7,6},{8,9},{9,8},{10,11... | collective-permute-start | bytes 786440 | tf_op jit(solution)/shard_map/ppermute | solution.py:463
  42.2 22.9 %copy-start = (s32[1,8]{1,0:T(1,128)S(1)}, s32[1,8]{1,0:T(1,128)}, u32[]{:S(2)}) copy-start(s32[1,8]{1,0:T(1,128)} %param.8) | copy-start | bytes 100
  42.2 22.7 %all-to-all-start.1 = ((f16[8,512,128]{2,1,0:T(8,128)(2,1)}), f16[8,512,128]{2,1,0:T(8,128)(2,1)S(1)}, u32[]{:S(2)}, u32[]{:S(2)}) async-start(f16[8,512,128]{2,1,0:T(8,128)(2,1)} %multiply_convert_fusion), calls=%async_computation.1 | async-start | bytes 2097152 | tf_op jit(solution)/shard_map/all_to_all | solution.py:492
  49.1 21.2 %collective-permute-start.19 = (bf16[2,2,4,16,512]{4,3,2,1,0:T(8,128)(2,1)S(1)}, bf16[2,2,4,16,512]{4,3,2,1,0:T(8,128)(2,1)S(1)}, u32[]{:S(2)}, u32[]{:S(2)}) collective-permute-start(bf16[2,2,4,16,512]{4,3,2,1,0:T(8,128)(2,1)S(1)} %maximum_select_fusion.1.refs_0_), channel_id=1, source_target_pairs={{0,6},{2,0},{4,2},{6,4},{1,7},{3,1},{5,3},{7,5},{8,14},{10,8},{12,... | collective-permute-start | bytes 786440 | tf_op jit(solution)/shard_map/ppermute | solution.py:469
  49.8 20.5 %collective-permute-start.18 = (bf16[2,2,4,16,512]{4,3,2,1,0:T(8,128)(2,1)S(1)}, bf16[2,2,4,16,512]{4,3,2,1,0:T(8,128)(2,1)S(1)}, u32[]{:S(2)}, u32[]{:S(2)}) collective-permute-start(bf16[2,2,4,16,512]{4,3,2,1,0:T(8,128)(2,1)S(1)} %maximum_select_fusion.1.refs_0_), channel_id=1, source_target_pairs={{0,4},{2,6},{4,0},{6,2},{1,5},{3,7},{5,1},{7,3},{8,12},{10,14},{12... | collective-permute-start | bytes 786440 | tf_op jit(solution)/shard_map/ppermute | solution.py:469
  50.3 20.0 %collective-permute-start.17 = (bf16[2,2,4,16,512]{4,3,2,1,0:T(8,128)(2,1)S(1)}, bf16[2,2,4,16,512]{4,3,2,1,0:T(8,128)(2,1)S(1)}, u32[]{:S(2)}, u32[]{:S(2)}) collective-permute-start(bf16[2,2,4,16,512]{4,3,2,1,0:T(8,128)(2,1)S(1)} %maximum_select_fusion.1.refs_0_), channel_id=1, source_target_pairs={{0,2},{2,4},{4,6},{6,0},{1,3},{3,5},{5,7},{7,1},{8,10},{10,12},{12... | collective-permute-start | bytes 786440 | tf_op jit(solution)/shard_map/ppermute | solution.py:469
  65.1 20.3 %copy-start.1 = (s32[1,28]{1,0:T(1,128)S(1)}, s32[1,28]{1,0:T(1,128)}, u32[]{:S(2)}) copy-start(s32[1,28]{1,0:T(1,128)} %label_ref.1) | copy-start | bytes 340
  70.3 15.0 %collective-permute-start.20 = (bf16[2,2,4,16,512]{4,3,2,1,0:T(8,128)(2,1)S(1)}, bf16[2,2,4,16,512]{4,3,2,1,0:T(8,128)(2,1)S(1)}, u32[]{:S(2)}, u32[]{:S(2)}) collective-permute-start(bf16[2,2,4,16,512]{4,3,2,1,0:T(8,128)(2,1)S(1)} %maximum_select_fusion.1.refs_0_), channel_id=1, source_target_pairs={{0,1},{1,0},{2,3},{3,2},{4,5},{5,4},{6,7},{7,6},{8,9},{9,8},{10,11... | collective-permute-start | bytes 786440 | tf_op jit(solution)/shard_map/ppermute | solution.py:463
  70.4 15.0 %collective-permute-start.21 = (bf16[2,2,4,16,512]{4,3,2,1,0:T(8,128)(2,1)S(1)}, bf16[2,2,4,16,512]{4,3,2,1,0:T(8,128)(2,1)S(1)}, u32[]{:S(2)}, u32[]{:S(2)}) collective-permute-start(bf16[2,2,4,16,512]{4,3,2,1,0:T(8,128)(2,1)S(1)} %collective-permute-done.17.refs_1_), channel_id=1, source_target_pairs={{0,1},{1,0},{2,3},{3,2},{4,5},{5,4},{6,7},{7,6},{8,9},{9,8},{10,11... | collective-permute-start | bytes 786440 | tf_op jit(solution)/shard_map/ppermute | solution.py:463
  70.9 14.5 %collective-permute-start.22 = (bf16[2,2,4,16,512]{4,3,2,1,0:T(8,128)(2,1)S(1)}, bf16[2,2,4,16,512]{4,3,2,1,0:T(8,128)(2,1)S(1)}, u32[]{:S(2)}, u32[]{:S(2)}) collective-permute-start(bf16[2,2,4,16,512]{4,3,2,1,0:T(8,128)(2,1)S(1)} %collective-permute-done.18.refs_2_), channel_id=1, source_target_pairs={{0,1},{1,0},{2,3},{3,2},{4,5},{5,4},{6,7},{7,6},{8,9},{9,8},{10,11... | collective-permute-start | bytes 786440 | tf_op jit(solution)/shard_map/ppermute | solution.py:463
  71.2 14.2 %collective-permute-start.23 = (bf16[2,2,4,16,512]{4,3,2,1,0:T(8,128)(2,1)S(1)}, bf16[2,2,4,16,512]{4,3,2,1,0:T(8,128)(2,1)S(1)}, u32[]{:S(2)}, u32[]{:S(2)}) collective-permute-start(bf16[2,2,4,16,512]{4,3,2,1,0:T(8,128)(2,1)S(1)} %collective-permute-done.19.refs_3_), channel_id=1, source_target_pairs={{0,1},{1,0},{2,3},{3,2},{4,5},{5,4},{6,7},{7,6},{8,9},{9,8},{10,11... | collective-permute-start | bytes 786440 | tf_op jit(solution)/shard_map/ppermute | solution.py:463
  84.7 25.3 %collective-permute-start.24 = (bf16[4,128,1024]{2,1,0:T(8,128)(2,1)S(1)}, bf16[4,128,1024]{2,1,0:T(8,128)(2,1)S(1)}, u32[]{:S(2)}, u32[]{:S(2)}) collective-permute-start(bf16[4,128,1024]{2,1,0:T(8,128)(2,1)S(1)} %all-to-all-done.h_ref), channel_id=1, source_target_pairs={{0,64},{64,0},{1,65},{65,1},{2,66},{66,2},{3,67},{67,3},{4,68},{68... | collective-permute-start | bytes 3145736 | tf_op jit(solution)/shard_map/ppermute | solution.py:500
  113.1 2.2 %collective-permute-start.25 = (bf16[16,40,512]{2,1,0:T(8,128)(2,1)S(1)}, bf16[16,40,512]{2,1,0:T(8,128)(2,1)S(1)}, u32[]{:S(2)}, u32[]{:S(2)}) collective-permute-start(bf16[16,40,512]{2,1,0:T(8,128)(2,1)S(1)} %get-tuple-element.44), channel_id=1, source_target_pairs={{0,1},{1,0},{2,3},{3,2},{4,5},{5,4},{6,7},{7,6},{8,9},{9,8},{10,11... | collective-permute-start | bytes 1966088 | tf_op jit(solution)/shard_map/ppermute | solution.py:505

commit v6 on v5

--- a/solution.py
+++ b/solution.py
@@ -480,8 +480,9 @@
     w = w.reshape(2, -1, w.shape[1])
     w, bil = (v.reshape(-1, v.shape[2]) for v in (w[:, :rows], w[:, rows:]))
     w = gather_x(w)
+    h = pack(hidden_states[0, 0])
+    h, bil = lax.optimization_barrier((h, bil))
     bil = jnp.stack(around(bil, "z"))
-    h = pack(hidden_states[0, 0])
     h, bil = lax.optimization_barrier((h, bil))
     w = with_other_core(around(w, "y"))
     bil = gather_x(bil)

time: 133 us -> 132 us (level)
  transfers between devices with their start and end apart: 28 -> 28, of which waited for: 9 -> 8; matrix products, arithmetic and copies ran while one was open for 0% -> 0% of each run, Pallas kernels for 12% -> 12%
where the time goes in v6:
time: 132 us; the launch traced here: 131 us
  blocking collectives  46.7 us (35%)
  starting transfers between devices  32.1 us (24%)
  waiting for transfers between devices  26.4 us (20%)
  Pallas kernels  21.9 us (17%)
  other arithmetic  1.87 us (1%)
  local copies, waits for them, and re-layouts  1.58 us (1%)
    all_to_all x1, blocking collectives, body(): drows = lax.all_to_all(drows, 'z', 0, 0)  17.3 us
    all_to_all x1, blocking collectives, body(): got = lax.all_to_all(sent, ('xh', 'xl', 'y'), 0, 0)  16.1 us
    all_to_all x1, waiting for transfers between devices, body(): parts = lax.all_to_all(parts, CAND, 0, 0)  13.8 us
    all_to_all x1, blocking collectives, body(): means = lax.all_to_all(means, CAND, 0, 0)  13.3 us
    ppermute x9, starting transfers between devices, around(): lax.ppermute(value, axis, [(i, (i + k) % count) for i in range(count)])  12.2 us
    pallas_call x1, Pallas kernels, backward(): pl.pallas_call(backward_kernel, out_shape=(jax.ShapeDtypeStruct((CANDS //...  7.24 us
    all_to_all x1, starting transfers between devices, body(): parts = lax.all_to_all(parts, CAND, 0, 0)  6.94 us
    ppermute x6, starting transfers between devices, gather_x(): lax.ppermute(value, ('xh', 'xl'), [(i, i ^ flip) for i in range(4)])  6.9 us
  transfers between devices with their start and end apart: 28, of which 8 were waited for; matrix products, arithmetic and copies ran while one was open for 0% of the time, Pallas kernels for 12%

profile of v6, /device:TPU:0, one launch (start us, length us, event | category | flops | bytes accessed | tf_op | source)
XLA Modules:
  0.0 131.4 jit_solution(9693845375906810413)
XLA Ops:
  0.6 0.8 constant_dynamic-update-slice_fusion.1
  1.5 0.7 constant_dynamic-update-slice_fusion
  2.2 0.1 collective-permute-start
  2.3 3.4 %shard_map.76 = bf16[4,128,1024]{2,1,0:T(8,128)(2,1)} custom-call(bf16[128,4096]{1,0:T(8,128)(2,1)} %bitcast.33, bf16[128,4096]{1,0:T(8,128)(2,1)} %bitcast.34), custom_call_target="tpu_custom_call" | custom-call | tf_op jit(solution)/shard_map/pallas_call | solution.py:55
  5.7 0.0 collective-permute-done
  5.8 4.2 %collective-permute-start.3 = (bf16[16,512]{1,0:T(8,128)(2,1)S(1)}, bf16[16,512]{1,0:T(8,128)(2,1)S(1)}, u32[]{:S(2)}, u32[]{:S(2)}) collective-permute-start(bf16[16,512]{1,0:T(8,128)(2,1)S(1)} %slice_bitcast_fusion), channel_id=1, source_target_pairs={{0,48},{16,0},{32,16},{48,32},{1,49},{17,1},{33,17},{49,33},{2,50}... | collective-permute-start | bytes 49160 | tf_op jit(solution)/shard_map/ppermute | solution.py:469
  10.0 0.0 collective-permute-start.2
  10.0 1.3 collective-permute-start.1
  11.2 2.8 %collective-permute-start.6 = (bf16[64,512]{1,0:T(8,128)(2,1)S(1)}, bf16[64,512]{1,0:T(8,128)(2,1)S(1)}, u32[]{:S(2)}, u32[]{:S(2)}) collective-permute-start(bf16[64,512]{1,0:T(8,128)(2,1)S(1)} %bitcast.38), channel_id=1, source_target_pairs={{0,72},{8,64},{64,8},{72,0},{1,73},{9,65},{65,9},{73,1},{2,74},{10... | collective-permute-start | bytes 196616 | tf_op jit(solution)/shard_map/ppermute | solution.py:455
  14.0 0.8 collective-permute-start.5
  14.8 0.0 collective-permute-done.3
  14.8 0.5 collective-permute-start.4
  15.3 0.0 collective-permute-done.2
  15.3 0.0 collective-permute-done.1
  15.3 3.6 %all-to-all-start = ((bf16[4,128,1024]{2,1,0:T(8,128)(2,1)}), bf16[4,128,1024]{2,1,0:T(8,128)(2,1)S(1)}, u32[]{:S(2)}, u32[]{:S(2)}) async-start(bf16[4,128,1024]{2,1,0:T(8,128)(2,1)} %shard_map.76), calls=%async_computation | async-start | bytes 2097152 | tf_op jit(solution)/shard_map/all_to_all | solution.py:489
  19.0 0.0 collective-permute-done.6
  19.0 0.8 collective-permute-done.5
  19.8 0.0 collective-permute-done.4
  19.8 3.1 %collective-permute-start.9 = (bf16[2,2,64,512]{3,2,1,0:T(8,128)(2,1)S(1)}, bf16[2,2,64,512]{3,2,1,0:T(8,128)(2,1)S(1)}, u32[]{:S(2)}, u32[]{:S(2)}) collective-permute-start(bf16[2,2,64,512]{3,2,1,0:T(8,128)(2,1)S(1)} %maximum_select_fusion.refs_0_), channel_id=1, source_target_pairs={{0,6},{2,0},{4,2},{6,4},{1,7},{3,1},{5,3},{7,5},{8,14},{10,8},{12,... | collective-permute-start | bytes 786440 | tf_op jit(solution)/shard_map/ppermute | solution.py:469
  22.9 0.6 collective-permute-start.8
  23.6 1.0 collective-permute-start.7
  24.5 2.0 %collective-permute-start.16 = (bf16[4,16,512]{2,1,0:T(8,128)(2,1)S(1)}, bf16[4,16,512]{2,1,0:T(8,128)(2,1)S(1)}, u32[]{:S(2)}, u32[]{:S(2)}) collective-permute-start(bf16[4,16,512]{2,1,0:T(8,128)(2,1)S(1)} %pad_maximum_fusion.1), channel_id=1, source_target_pairs={{0,72},{8,64},{64,8},{72,0},{1,73},{9,65},{65,9},{73,1},{2,74},{10... | collective-permute-start | bytes 196616 | tf_op jit(solution)/shard_map/ppermute | solution.py:455
  26.5 0.8 collective-permute-start.15
  27.3 0.1 pad_add_fusion.place_ref
  27.4 2.6 %collective-permute-done.16 = bf16[4,16,512]{2,1,0:T(8,128)(2,1)S(1)} collective-permute-done((bf16[4,16,512]{2,1,0:T(8,128)(2,1)S(1)}, bf16[4,16,512]{2,1,0:T(8,128)(2,1)S(1)}, u32[]{:S(2)}, u32[]{:S(2)}) %collective-permute-start.16) | collective-permute-done | bytes 65568 | tf_op jit(solution)/shard_map/ppermute | solution.py:455
  30.0 0.0 collective-permute-start.14
  30.0 2.6 %collective-permute-done.15 = bf16[4,16,512]{2,1,0:T(8,128)(2,1)S(1)} collective-permute-done((bf16[4,16,512]{2,1,0:T(8,128)(2,1)S(1)}, bf16[4,16,512]{2,1,0:T(8,128)(2,1)S(1)}, u32[]{:S(2)}, u32[]{:S(2)}) %collective-permute-start.15) | collective-permute-done | bytes 65568 | tf_op jit(solution)/shard_map/ppermute | solution.py:455
  32.6 0.0 collective-permute-start.10
  32.6 0.0 collective-permute-done.9.refs_3_
  32.6 0.5 collective-permute-start.13
  33.1 0.3 collective-permute-done.8.refs_2_
  33.5 0.0 collective-permute-start.12
  33.5 2.7 %collective-permute-done.7.refs_1_ = bf16[2,2,64,512]{3,2,1,0:T(8,128)(2,1)S(1)} collective-permute-done((bf16[2,2,64,512]{3,2,1,0:T(8,128)(2,1)S(1)}, bf16[2,2,64,512]{3,2,1,0:T(8,128)(2,1)S(1)}, u32[]{:S(2)}, u32[]{:S(2)}) %collective-permute-start.7) | collective-permute-done | bytes 262176 | tf_op jit(solution)/shard_map/ppermute | solution.py:469
  36.2 0.0 collective-permute-done.14
  36.3 0.0 collective-permute-done.12.refs_6_
  36.3 1.4 %collective-permute-done.11.refs_5_ = bf16[2,2,64,512]{3,2,1,0:T(8,128)(2,1)S(1)} collective-permute-done((bf16[2,2,64,512]{3,2,1,0:T(8,128)(2,1)S(1)}, bf16[2,2,64,512]{3,2,1,0:T(8,128)(2,1)S(1)}, u32[]{:S(2)}, u32[]{:S(2)}) %collective-permute-start.11) | collective-permute-done | bytes 262176 | tf_op jit(solution)/shard_map/ppermute | solution.py:463
  37.7 0.0 all-to-all-done.h_ref
  37.7 2.3 %shard_map.77 = f32[8,512,128]{2,1,0:T(8,128)S(1)} custom-call(s32[4]{0:T(128)S(1)} %pad_add_fusion.place_ref, bf16[4,128,1024]{2,1,0:T(8,128)(2,1)S(1)} %all-to-all-done.h_ref, bf16[2,2,64,512]{3,2,1,0:T(8,128)(2,1)S(1)} %maximum_select_fusion.refs_0_, bf16[2,2,64,512]{3,2,1,0:T(8,128)(2,1)S(1)} %collective-permute-done.7.refs_1_, ...), custom_call_target="tpu_custom_call" | custom-call | tf_op jit(solution)/shard_map/pallas_call | solution.py:95
  40.0 1.2 multiply_convert_fusion
  41.2 6.9 %all-to-all-start.1 = ((f16[8,512,128]{2,1,0:T(8,128)(2,1)}), f16[8,512,128]{2,1,0:T(8,128)(2,1)S(1)}, u32[]{:S(2)}, u32[]{:S(2)}) async-start(f16[8,512,128]{2,1,0:T(8,128)(2,1)} %multiply_convert_fusion), calls=%async_computation.1 | async-start | bytes 2097152 | tf_op jit(solution)/shard_map/all_to_all | solution.py:493
  48.2 0.7 collective-permute-start.19
  48.9 0.5 collective-permute-start.18
  49.4 0.8 collective-permute-start.17
  50.2 13.8 %all-to-all-done.1 = f16[8,512,128]{2,1,0:T(8,128)(2,1)S(1)} async-done(((f16[8,512,128]{2,1,0:T(8,128)(2,1)}), f16[8,512,128]{2,1,0:T(8,128)(2,1)S(1)}, u32[]{:S(2)}, u32[]{:S(2)}) %all-to-all-start.1) | async-done | bytes 1048608 | tf_op jit(solution)/shard_map/all_to_all | solution.py:493
  64.1 0.1 convert_reduce_fusion
  64.3 0.0 copy-start.1
  64.3 5.1 %shard_map.78 = (bf16[128,1024]{1,0:T(8,128)(2,1)S(1)}, f32[8,64,128]{2,1,0:T(8,128)S(1)}, f32[2,8,1024]{2,1,0:T(8,128)S(1)}, f32[64,256]{1,0:T(8,128)S(1)}) custom-call(s32[8]{0:T(128)S(1)} %bitcast.31, bf16[1024,128]{1,0:T(8,128)(2,1)S(1)} %bitcast.29), custom_call_target="tpu_custom_call" | custom-call | flops 12884901888 | bytes 16777216 | tf_op jit(solution)/shard_map/pallas_call | solution.py:188
  69.4 0.0 collective-permute-done.19.refs_3_
  69.4 0.0 collective-permute-done.18.refs_2_
  69.5 0.1 collective-permute-start.20
  69.5 0.5 collective-permute-start.21
  70.0 0.3 collective-permute-start.22
  70.3 0.2 collective-permute-start.23
  70.6 13.3 %all_to_all.25.mean_ref = f32[8,64,128]{2,1,0:T(8,128)S(1)} all-to-all(f32[8,64,128]{2,1,0:T(8,128)S(1)} %get-tuple-element.34), channel_id=1, replica_groups=mesh['xh'=2,'z'=4,'xl'=2,'y'=4,'core'=2] {'xh','z'}, dimensions={0} | all-to-all | bytes 524288 | tf_op jit(solution)/shard_map/all_to_all | solution.py:499
  83.9 0.6 collective-permute-start.24
  84.5 0.0 collective-permute-done.23.refs_7_
  84.5 7.2 %shard_map.79 = (bf16[4,1024,128]{2,1,0:T(8,128)(2,1)S(1)}, f32[8,8]{1,0:T(8,128)}, f32[256,512]{1,0:T(8,128)S(1)}) custom-call(s32[8]{0:T(128)S(1)} %bitcast.32, s32[4]{0:T(128)S(1)} %pad_add_fusion.place_ref, f32[8,64,128]{2,1,0:T(8,128)S(1)} %all_to_all.25.mean_ref, bf16[1024,128]{1,0:T(8,128)(2,1)S(1)} %bitcast.30, ...), custom_call_target="tpu_custom_call" | custom-call | flops 8589934592 | bytes 8388608 | tf_op jit(solution)/shard_map/pallas_call | solution.py:337
  91.8 17.3 %all_to_all.26.d_ref = bf16[4,1024,128]{2,1,0:T(8,128)(2,1)S(1)} all-to-all(bf16[4,1024,128]{2,1,0:T(8,128)(2,1)S(1)} %get-tuple-element.45), channel_id=1, replica_groups=mesh['xh'=2,'z'=4,'xl'=2,'y'=4,'core'=2] {'z'}, dimensions={0} | all-to-all | bytes 2097152 | tf_op jit(solution)/shard_map/all_to_all | solution.py:503
  109.1 3.1 %shard_map.80 = (f32[16,40,512]{2,1,0:T(8,128)S(1)}, bf16[16,40,512]{2,1,0:T(8,128)(2,1)S(1)}) custom-call(s32[4]{0:T(128)S(1)} %pad_add_fusion.place_ref, bf16[4,128,1024]{2,1,0:T(8,128)(2,1)S(1)} %all-to-all-done.h_ref, bf16[4,128,1024]{2,1,0:T(8,128)(2,1)S(1)} %collective-permute-done.24.far_ref, bf16[4,1024,128]{2,1,0:T(8,128)(2,1)S(1)} %all_to_all.26.d_ref, ...), custom_call_target="tpu_custom_call" | custom-call | tf_op jit(solution)/shard_map/pallas_call | solution.py:388
  112.2 0.1 collective-permute-start.25
  112.3 2.1 %collective-permute-done.25 = bf16[16,40,512]{2,1,0:T(8,128)(2,1)S(1)} collective-permute-done((bf16[16,40,512]{2,1,0:T(8,128)(2,1)S(1)}, bf16[16,40,512]{2,1,0:T(8,128)(2,1)S(1)}, u32[]{:S(2)}, u32[]{:S(2)}) %collective-permute-start.25) | collective-permute-done | bytes 655392 | tf_op jit(solution)/shard_map/ppermute | solution.py:506
  114.4 0.2 add_convert_fusion
  114.6 16.1 %all_to_all.27.got_ref = bf16[16,40,512]{2,1,0:T(8,128)(2,1)S(1)} all-to-all(bf16[16,40,512]{2,1,0:T(8,128)(2,1)S(1)} %add_convert_fusion), channel_id=1, replica_groups=mesh['xh'=2,'z'=4,'xl'=2,'y'=4,'core'=2] {'xh','xl','y'}, dimensions={0} | all-to-all | bytes 1310720 | tf_op jit(solution)/shard_map/all_to_all | solution.py:508
  130.7 0.7 shard_map.81
  (24 shorter events, 0.2 us)
Async XLA Ops:
  2.2 3.5 %collective-permute-start = (bf16[40,512]{1,0:T(8,128)(2,1)S(1)}, bf16[40,512]{1,0:T(8,128)(2,1)S(1)}, u32[]{:S(2)}, u32[]{:S(2)}) collective-permute-start(bf16[40,512]{1,0:T(8,128)(2,1)S(1)} %broadcast_select_fusion.2), channel_id=1, source_target_pairs={{0,1},{1,0},{2,3},{3,2},{4,5},{5,4},{6,7},{7,6},{8,9},{9,8},{10,11... | collective-permute-start | bytes 122888 | tf_op jit(solution)/shard_map/ppermute | solution.py:446
  5.8 9.0 %collective-permute-start.3 = (bf16[16,512]{1,0:T(8,128)(2,1)S(1)}, bf16[16,512]{1,0:T(8,128)(2,1)S(1)}, u32[]{:S(2)}, u32[]{:S(2)}) collective-permute-start(bf16[16,512]{1,0:T(8,128)(2,1)S(1)} %slice_bitcast_fusion), channel_id=1, source_target_pairs={{0,48},{16,0},{32,16},{48,32},{1,49},{17,1},{33,17},{49,33},{2,50}... | collective-permute-start | bytes 49160 | tf_op jit(solution)/shard_map/ppermute | solution.py:469
  10.0 5.4 %collective-permute-start.2 = (bf16[16,512]{1,0:T(8,128)(2,1)S(1)}, bf16[16,512]{1,0:T(8,128)(2,1)S(1)}, u32[]{:S(2)}, u32[]{:S(2)}) collective-permute-start(bf16[16,512]{1,0:T(8,128)(2,1)S(1)} %slice_bitcast_fusion), channel_id=1, source_target_pairs={{0,32},{16,48},{32,0},{48,16},{1,33},{17,49},{33,1},{49,17},{2,34}... | collective-permute-start | bytes 49160 | tf_op jit(solution)/shard_map/ppermute | solution.py:469
  10.0 5.4 %collective-permute-start.1 = (bf16[16,512]{1,0:T(8,128)(2,1)S(1)}, bf16[16,512]{1,0:T(8,128)(2,1)S(1)}, u32[]{:S(2)}, u32[]{:S(2)}) collective-permute-start(bf16[16,512]{1,0:T(8,128)(2,1)S(1)} %slice_bitcast_fusion), channel_id=1, source_target_pairs={{0,16},{16,32},{32,48},{48,0},{1,17},{17,33},{33,49},{49,1},{2,18}... | collective-permute-start | bytes 49160 | tf_op jit(solution)/shard_map/ppermute | solution.py:469
  11.2 7.8 %collective-permute-start.6 = (bf16[64,512]{1,0:T(8,128)(2,1)S(1)}, bf16[64,512]{1,0:T(8,128)(2,1)S(1)}, u32[]{:S(2)}, u32[]{:S(2)}) collective-permute-start(bf16[64,512]{1,0:T(8,128)(2,1)S(1)} %bitcast.38), channel_id=1, source_target_pairs={{0,72},{8,64},{64,8},{72,0},{1,73},{9,65},{65,9},{73,1},{2,74},{10... | collective-permute-start | bytes 196616 | tf_op jit(solution)/shard_map/ppermute | solution.py:455
  14.0 5.8 %collective-permute-start.5 = (bf16[64,512]{1,0:T(8,128)(2,1)S(1)}, bf16[64,512]{1,0:T(8,128)(2,1)S(1)}, u32[]{:S(2)}, u32[]{:S(2)}) collective-permute-start(bf16[64,512]{1,0:T(8,128)(2,1)S(1)} %bitcast.39), channel_id=1, source_target_pairs={{0,64},{8,72},{64,0},{72,8},{1,65},{9,73},{65,1},{73,9},{2,66},{10... | collective-permute-start | bytes 196616 | tf_op jit(solution)/shard_map/ppermute | solution.py:455
  14.8 5.0 %collective-permute-start.4 = (bf16[64,512]{1,0:T(8,128)(2,1)S(1)}, bf16[64,512]{1,0:T(8,128)(2,1)S(1)}, u32[]{:S(2)}, u32[]{:S(2)}) collective-permute-start(bf16[64,512]{1,0:T(8,128)(2,1)S(1)} %bitcast.40), channel_id=1, source_target_pairs={{0,8},{8,0},{64,72},{72,64},{1,9},{9,1},{65,73},{73,65},{2,10},{10... | collective-permute-start | bytes 196616 | tf_op jit(solution)/shard_map/ppermute | solution.py:455
  15.3 22.4 %all-to-all-start = ((bf16[4,128,1024]{2,1,0:T(8,128)(2,1)}), bf16[4,128,1024]{2,1,0:T(8,128)(2,1)S(1)}, u32[]{:S(2)}, u32[]{:S(2)}) async-start(bf16[4,128,1024]{2,1,0:T(8,128)(2,1)} %shard_map.76), calls=%async_computation | async-start | bytes 2097152 | tf_op jit(solution)/shard_map/all_to_all | solution.py:489
  19.8 12.8 %collective-permute-start.9 = (bf16[2,2,64,512]{3,2,1,0:T(8,128)(2,1)S(1)}, bf16[2,2,64,512]{3,2,1,0:T(8,128)(2,1)S(1)}, u32[]{:S(2)}, u32[]{:S(2)}) collective-permute-start(bf16[2,2,64,512]{3,2,1,0:T(8,128)(2,1)S(1)} %maximum_select_fusion.refs_0_), channel_id=1, source_target_pairs={{0,6},{2,0},{4,2},{6,4},{1,7},{3,1},{5,3},{7,5},{8,14},{10,8},{12,... | collective-permute-start | bytes 786440 | tf_op jit(solution)/shard_map/ppermute | solution.py:469
  22.9 10.5 %collective-permute-start.8 = (bf16[2,2,64,512]{3,2,1,0:T(8,128)(2,1)S(1)}, bf16[2,2,64,512]{3,2,1,0:T(8,128)(2,1)S(1)}, u32[]{:S(2)}, u32[]{:S(2)}) collective-permute-start(bf16[2,2,64,512]{3,2,1,0:T(8,128)(2,1)S(1)} %maximum_select_fusion.refs_0_), channel_id=1, source_target_pairs={{0,4},{2,6},{4,0},{6,2},{1,5},{3,7},{5,1},{7,3},{8,12},{10,14},{12... | collective-permute-start | bytes 786440 | tf_op jit(solution)/shard_map/ppermute | solution.py:469
  23.6 12.6 %collective-permute-start.7 = (bf16[2,2,64,512]{3,2,1,0:T(8,128)(2,1)S(1)}, bf16[2,2,64,512]{3,2,1,0:T(8,128)(2,1)S(1)}, u32[]{:S(2)}, u32[]{:S(2)}) collective-permute-start(bf16[2,2,64,512]{3,2,1,0:T(8,128)(2,1)S(1)} %maximum_select_fusion.refs_0_), channel_id=1, source_target_pairs={{0,2},{2,4},{4,6},{6,0},{1,3},{3,5},{5,7},{7,1},{8,10},{10,12},{12... | collective-permute-start | bytes 786440 | tf_op jit(solution)/shard_map/ppermute | solution.py:469
  24.5 5.5 %collective-permute-start.16 = (bf16[4,16,512]{2,1,0:T(8,128)(2,1)S(1)}, bf16[4,16,512]{2,1,0:T(8,128)(2,1)S(1)}, u32[]{:S(2)}, u32[]{:S(2)}) collective-permute-start(bf16[4,16,512]{2,1,0:T(8,128)(2,1)S(1)} %pad_maximum_fusion.1), channel_id=1, source_target_pairs={{0,72},{8,64},{64,8},{72,0},{1,73},{9,65},{65,9},{73,1},{2,74},{10... | collective-permute-start | bytes 196616 | tf_op jit(solution)/shard_map/ppermute | solution.py:455
  26.5 6.1 %collective-permute-start.15 = (bf16[4,16,512]{2,1,0:T(8,128)(2,1)S(1)}, bf16[4,16,512]{2,1,0:T(8,128)(2,1)S(1)}, u32[]{:S(2)}, u32[]{:S(2)}) collective-permute-start(bf16[4,16,512]{2,1,0:T(8,128)(2,1)S(1)} %pad_maximum_fusion.1), channel_id=1, source_target_pairs={{0,64},{8,72},{64,0},{72,8},{1,65},{9,73},{65,1},{73,9},{2,66},{10... | collective-permute-start | bytes 196616 | tf_op jit(solution)/shard_map/ppermute | solution.py:455
  30.0 6.2 %collective-permute-start.14 = (bf16[4,16,512]{2,1,0:T(8,128)(2,1)S(1)}, bf16[4,16,512]{2,1,0:T(8,128)(2,1)S(1)}, u32[]{:S(2)}, u32[]{:S(2)}) collective-permute-start(bf16[4,16,512]{2,1,0:T(8,128)(2,1)S(1)} %pad_maximum_fusion.1), channel_id=1, source_target_pairs={{0,8},{8,0},{64,72},{72,64},{1,9},{9,1},{65,73},{73,65},{2,10},{10... | collective-permute-start | bytes 196616 | tf_op jit(solution)/shard_map/ppermute | solution.py:455
  32.6 3.7 %collective-permute-start.10 = (bf16[2,2,64,512]{3,2,1,0:T(8,128)(2,1)S(1)}, bf16[2,2,64,512]{3,2,1,0:T(8,128)(2,1)S(1)}, u32[]{:S(2)}, u32[]{:S(2)}) collective-permute-start(bf16[2,2,64,512]{3,2,1,0:T(8,128)(2,1)S(1)} %maximum_select_fusion.refs_0_), channel_id=1, source_target_pairs={{0,1},{1,0},{2,3},{3,2},{4,5},{5,4},{6,7},{7,6},{8,9},{9,8},{10,11... | collective-permute-start | bytes 786440 | tf_op jit(solution)/shard_map/ppermute | solution.py:463
  32.6 3.7 %collective-permute-start.13 = (bf16[2,2,64,512]{3,2,1,0:T(8,128)(2,1)S(1)}, bf16[2,2,64,512]{3,2,1,0:T(8,128)(2,1)S(1)}, u32[]{:S(2)}, u32[]{:S(2)}) collective-permute-start(bf16[2,2,64,512]{3,2,1,0:T(8,128)(2,1)S(1)} %collective-permute-done.9.refs_3_), channel_id=1, source_target_pairs={{0,1},{1,0},{2,3},{3,2},{4,5},{5,4},{6,7},{7,6},{8,9},{9,8},{10,11... | collective-permute-start | bytes 786440 | tf_op jit(solution)/shard_map/ppermute | solution.py:463
  33.5 2.9 %collective-permute-start.12 = (bf16[2,2,64,512]{3,2,1,0:T(8,128)(2,1)S(1)}, bf16[2,2,64,512]{3,2,1,0:T(8,128)(2,1)S(1)}, u32[]{:S(2)}, u32[]{:S(2)}) collective-permute-start(bf16[2,2,64,512]{3,2,1,0:T(8,128)(2,1)S(1)} %collective-permute-done.8.refs_2_), channel_id=1, source_target_pairs={{0,1},{1,0},{2,3},{3,2},{4,5},{5,4},{6,7},{7,6},{8,9},{9,8},{10,11... | collective-permute-start | bytes 786440 | tf_op jit(solution)/shard_map/ppermute | solution.py:463
  36.2 1.5 %collective-permute-start.11 = (bf16[2,2,64,512]{3,2,1,0:T(8,128)(2,1)S(1)}, bf16[2,2,64,512]{3,2,1,0:T(8,128)(2,1)S(1)}, u32[]{:S(2)}, u32[]{:S(2)}) collective-permute-start(bf16[2,2,64,512]{3,2,1,0:T(8,128)(2,1)S(1)} %collective-permute-done.7.refs_1_), channel_id=1, source_target_pairs={{0,1},{1,0},{2,3},{3,2},{4,5},{5,4},{6,7},{7,6},{8,9},{9,8},{10,11... | collective-permute-start | bytes 786440 | tf_op jit(solution)/shard_map/ppermute | solution.py:463
  41.2 23.0 %copy-start = (s32[1,8]{1,0:T(1,128)S(1)}, s32[1,8]{1,0:T(1,128)}, u32[]{:S(2)}) copy-start(s32[1,8]{1,0:T(1,128)} %param.8) | copy-start | bytes 100
  41.2 22.8 %all-to-all-start.1 = ((f16[8,512,128]{2,1,0:T(8,128)(2,1)}), f16[8,512,128]{2,1,0:T(8,128)(2,1)S(1)}, u32[]{:S(2)}, u32[]{:S(2)}) async-start(f16[8,512,128]{2,1,0:T(8,128)(2,1)} %multiply_convert_fusion), calls=%async_computation.1 | async-start | bytes 2097152 | tf_op jit(solution)/shard_map/all_to_all | solution.py:493
  48.2 21.2 %collective-permute-start.19 = (bf16[2,2,4,16,512]{4,3,2,1,0:T(8,128)(2,1)S(1)}, bf16[2,2,4,16,512]{4,3,2,1,0:T(8,128)(2,1)S(1)}, u32[]{:S(2)}, u32[]{:S(2)}) collective-permute-start(bf16[2,2,4,16,512]{4,3,2,1,0:T(8,128)(2,1)S(1)} %maximum_select_fusion.1.refs_0_), channel_id=1, source_target_pairs={{0,6},{2,0},{4,2},{6,4},{1,7},{3,1},{5,3},{7,5},{8,14},{10,8},{12,... | collective-permute-start | bytes 786440 | tf_op jit(solution)/shard_map/ppermute | solution.py:469
  48.9 20.5 %collective-permute-start.18 = (bf16[2,2,4,16,512]{4,3,2,1,0:T(8,128)(2,1)S(1)}, bf16[2,2,4,16,512]{4,3,2,1,0:T(8,128)(2,1)S(1)}, u32[]{:S(2)}, u32[]{:S(2)}) collective-permute-start(bf16[2,2,4,16,512]{4,3,2,1,0:T(8,128)(2,1)S(1)} %maximum_select_fusion.1.refs_0_), channel_id=1, source_target_pairs={{0,4},{2,6},{4,0},{6,2},{1,5},{3,7},{5,1},{7,3},{8,12},{10,14},{12... | collective-permute-start | bytes 786440 | tf_op jit(solution)/shard_map/ppermute | solution.py:469
  49.4 20.0 %collective-permute-start.17 = (bf16[2,2,4,16,512]{4,3,2,1,0:T(8,128)(2,1)S(1)}, bf16[2,2,4,16,512]{4,3,2,1,0:T(8,128)(2,1)S(1)}, u32[]{:S(2)}, u32[]{:S(2)}) collective-permute-start(bf16[2,2,4,16,512]{4,3,2,1,0:T(8,128)(2,1)S(1)} %maximum_select_fusion.1.refs_0_), channel_id=1, source_target_pairs={{0,2},{2,4},{4,6},{6,0},{1,3},{3,5},{5,7},{7,1},{8,10},{10,12},{12... | collective-permute-start | bytes 786440 | tf_op jit(solution)/shard_map/ppermute | solution.py:469
  64.3 20.3 %copy-start.1 = (s32[1,28]{1,0:T(1,128)S(1)}, s32[1,28]{1,0:T(1,128)}, u32[]{:S(2)}) copy-start(s32[1,28]{1,0:T(1,128)} %label_ref.1) | copy-start | bytes 340
  69.5 15.0 %collective-permute-start.20 = (bf16[2,2,4,16,512]{4,3,2,1,0:T(8,128)(2,1)S(1)}, bf16[2,2,4,16,512]{4,3,2,1,0:T(8,128)(2,1)S(1)}, u32[]{:S(2)}, u32[]{:S(2)}) collective-permute-start(bf16[2,2,4,16,512]{4,3,2,1,0:T(8,128)(2,1)S(1)} %maximum_select_fusion.1.refs_0_), channel_id=1, source_target_pairs={{0,1},{1,0},{2,3},{3,2},{4,5},{5,4},{6,7},{7,6},{8,9},{9,8},{10,11... | collective-permute-start | bytes 786440 | tf_op jit(solution)/shard_map/ppermute | solution.py:463
  69.5 15.0 %collective-permute-start.21 = (bf16[2,2,4,16,512]{4,3,2,1,0:T(8,128)(2,1)S(1)}, bf16[2,2,4,16,512]{4,3,2,1,0:T(8,128)(2,1)S(1)}, u32[]{:S(2)}, u32[]{:S(2)}) collective-permute-start(bf16[2,2,4,16,512]{4,3,2,1,0:T(8,128)(2,1)S(1)} %collective-permute-done.17.refs_1_), channel_id=1, source_target_pairs={{0,1},{1,0},{2,3},{3,2},{4,5},{5,4},{6,7},{7,6},{8,9},{9,8},{10,11... | collective-permute-start | bytes 786440 | tf_op jit(solution)/shard_map/ppermute | solution.py:463
  70.0 14.5 %collective-permute-start.22 = (bf16[2,2,4,16,512]{4,3,2,1,0:T(8,128)(2,1)S(1)}, bf16[2,2,4,16,512]{4,3,2,1,0:T(8,128)(2,1)S(1)}, u32[]{:S(2)}, u32[]{:S(2)}) collective-permute-start(bf16[2,2,4,16,512]{4,3,2,1,0:T(8,128)(2,1)S(1)} %collective-permute-done.18.refs_2_), channel_id=1, source_target_pairs={{0,1},{1,0},{2,3},{3,2},{4,5},{5,4},{6,7},{7,6},{8,9},{9,8},{10,11... | collective-permute-start | bytes 786440 | tf_op jit(solution)/shard_map/ppermute | solution.py:463
  70.3 14.2 %collective-permute-start.23 = (bf16[2,2,4,16,512]{4,3,2,1,0:T(8,128)(2,1)S(1)}, bf16[2,2,4,16,512]{4,3,2,1,0:T(8,128)(2,1)S(1)}, u32[]{:S(2)}, u32[]{:S(2)}) collective-permute-start(bf16[2,2,4,16,512]{4,3,2,1,0:T(8,128)(2,1)S(1)} %collective-permute-done.19.refs_3_), channel_id=1, source_target_pairs={{0,1},{1,0},{2,3},{3,2},{4,5},{5,4},{6,7},{7,6},{8,9},{9,8},{10,11... | collective-permute-start | bytes 786440 | tf_op jit(solution)/shard_map/ppermute | solution.py:463
  83.9 25.3 %collective-permute-start.24 = (bf16[4,128,1024]{2,1,0:T(8,128)(2,1)S(1)}, bf16[4,128,1024]{2,1,0:T(8,128)(2,1)S(1)}, u32[]{:S(2)}, u32[]{:S(2)}) collective-permute-start(bf16[4,128,1024]{2,1,0:T(8,128)(2,1)S(1)} %all-to-all-done.h_ref), channel_id=1, source_target_pairs={{0,64},{64,0},{1,65},{65,1},{2,66},{66,2},{3,67},{67,3},{4,68},{68... | collective-permute-start | bytes 3145736 | tf_op jit(solution)/shard_map/ppermute | solution.py:501
  112.2 2.2 %collective-permute-start.25 = (bf16[16,40,512]{2,1,0:T(8,128)(2,1)S(1)}, bf16[16,40,512]{2,1,0:T(8,128)(2,1)S(1)}, u32[]{:S(2)}, u32[]{:S(2)}) collective-permute-start(bf16[16,40,512]{2,1,0:T(8,128)(2,1)S(1)} %get-tuple-element.48), channel_id=1, source_target_pairs={{0,1},{1,0},{2,3},{3,2},{4,5},{5,4},{6,7},{7,6},{8,9},{9,8},{10,11... | collective-permute-start | bytes 1966088 | tf_op jit(solution)/shard_map/ppermute | solution.py:506
